TPU v7x, 32 devices: a whole 2x2x4 slice. The times are simulated.
32 devices in a mesh: fsdp: 16 (over z, y, core), dp: 2 (over x).
Axes of the slice: x: 2, y: 2, z: 4, core: 2. Of those that a mesh axis runs over, the one named last changes fastest.
Arguments:
- tokens: bfloat16 [32, 1024, 1024], P(('fsdp', 'dp')), may hold values from -6 to 6
- segments: int32 [32, 1024], P(('fsdp', 'dp')), may hold values from 0 to 4, never falling along the last dimension, each value on 1 to 512 neighbouring positions
- cotangent: bfloat16 [32, 1024, 1024], P(('fsdp', 'dp')), may hold values from -6 to 6
- w_in: bfloat16 [1024, 3352], P(('fsdp', 'dp')), may hold values from -0.1875 to 0.1875
- w_out: bfloat16 [1536, 1024], P(None, ('fsdp', 'dp')), may hold values from -0.15625 to 0.15625
- w_query: bfloat16 [1024, 1024], P(('fsdp', 'dp')), may hold values from -0.1875 to 0.1875
- w_key: bfloat16 [1024, 256], P(('fsdp', 'dp')), may hold values from -0.1875 to 0.1875
- w_value: bfloat16 [1024, 256], P(('fsdp', 'dp')), may hold values from -0.1875 to 0.1875
- w_attn_out: bfloat16 [1024, 1024], P(None, ('fsdp', 'dp')), may hold values from -3 to 3
- w_gate: bfloat16 [1024, 2048], P(('fsdp', 'dp')), may hold values from -0.1875 to 0.1875
- w_up: bfloat16 [1024, 2048], P(('fsdp', 'dp')), may hold values from -0.1875 to 0.1875
- w_down: bfloat16 [2048, 1024], P(None, ('fsdp', 'dp')), may hold values from -0.125 to 0.125
- norm_in: float32 [1024], replicated, may hold values from 0.5 to 1.5
- conv_weight: float32 [4, 1792], replicated, may hold values from -3 to 3
- conv_bias: float32 [1792], replicated, may hold values from -3 to 3
- dt_bias: float32 [24], replicated, may hold values from -6 to -2
- a_log: float32 [24], replicated, may hold values from -4 to 1.5
- skip_gain: float32 [24], replicated, may hold values from 0.5 to 2
- norm_gated: float32 [1536], replicated, may hold values from 0.5 to 1.5
- norm_mid: float32 [1024], replicated, may hold values from 0.5 to 1.5
Outputs:
- mixed: bfloat16 [32, 1024, 1024], P(('fsdp', 'dp'))
- grad_tokens: float32 [32, 1024, 1024], P(('fsdp', 'dp'))
- grad_w_in: float32 [1024, 3352], P(('fsdp', 'dp'))
- grad_w_out: float32 [1536, 1024], P(None, ('fsdp', 'dp'))
- grad_w_query: float32 [1024, 1024], P(('fsdp', 'dp'))
- grad_w_key: float32 [1024, 256], P(('fsdp', 'dp'))
- grad_w_value: float32 [1024, 256], P(('fsdp', 'dp'))
- grad_w_attn_out: float32 [1024, 1024], P(None, ('fsdp', 'dp'))
- grad_w_gate: float32 [1024, 2048], P(('fsdp', 'dp'))
- grad_w_up: float32 [1024, 2048], P(('fsdp', 'dp'))
- grad_w_down: float32 [2048, 1024], P(None, ('fsdp', 'dp'))
- grad_norm_in: float32 [1024], replicated
- grad_conv_weight: float32 [4, 1792], replicated
- grad_conv_bias: float32 [1792], replicated
- grad_dt_bias: float32 [24], replicated
- grad_a_log: float32 [24], replicated
- grad_skip_gain: float32 [24], replicated
- grad_norm_gated: float32 [1536], replicated
- grad_norm_mid: float32 [1024], replicated
Inputs may be any that keep to these rules, and one draw needn't show every extreme that they name: `segments`: within a sequence the document numbers never fall; a document has at most 512 tokens, and some has exactly that many.
All inputs are finite; a program needn't handle non-finite values.
Results may differ from a plain program's by a relative error of at most 0.012.
Values may be sent and summed in bfloat16 or wider, within the bound.
No kernel may reach another device: no remote copies, remote signals or barrier semaphores. Data moves between devices by JAX's collectives and lax.ppermute only.
A program may use at most 384 MiB of HBM per device.

v0:
```python
from functools import partial

import jax
import jax.numpy as jnp
from jax import lax
from jax.sharding import PartitionSpec as P

HEADS = 8
KV_HEADS = 2
HEAD_DIM = 128
M_HEADS = 24
M_HDIM = 64
STATE = 128
SPAN = 128
D_SSM = 1536
CONV_CH = 1792


highest = lax.Precision.HIGHEST
eps = 1e-06
rope_base = 100000000000.0


def round_plain(values):
    return lax.optimization_barrier(values.astype(jnp.bfloat16)).astype(jnp.float32)


def rms_norm(values, gain):
    return values * lax.rsqrt(jnp.mean(values * values, axis=-1, keepdims=True) + eps) * gain


def rotate(values, positions):
    half_dim = values.shape[-1] // 2
    frequency = rope_base ** (-jnp.arange(half_dim, dtype=jnp.float32) / half_dim)
    angles = positions.astype(jnp.float32)[:, None] * frequency[None, :]
    cosine = jnp.cos(angles)[:, None, :]
    sine = jnp.sin(angles)[:, None, :]
    front_half = values[..., :half_dim]
    back_half = values[..., half_dim:]
    return jnp.concatenate(
        [front_half * cosine - back_half * sine, back_half * cosine + front_half * sine], axis=-1
    )


def conv_reset(conv_in, doc_ids, conv_weight, conv_bias):
    length = conv_in.shape[0]
    summed = conv_bias[None, :] + conv_weight[0][None, :] * conv_in
    for offset in range(1, conv_weight.shape[0]):
        shifted = jnp.pad(conv_in, ((offset, 0), (0, 0)))[:length]
        shifted_doc = jnp.pad(doc_ids, (offset, 0), constant_values=-1)[:length]
        summed = summed + jnp.where(
            (shifted_doc == doc_ids)[:, None], conv_weight[offset][None, :] * shifted, 0.0
        )
    return summed


def build_pieces():

    def value_fwd(values):
        return round_plain(values)

    def value_keep(values):
        return (round_plain(values), None)

    def value_back(kept, incoming):
        return (incoming,)

    round_value = jax.custom_vjp(value_fwd)
    round_value.defvjp(value_keep, value_back)

    def grad_fwd(values):
        return values

    def grad_keep(values):
        return (values, None)

    def grad_back(kept, incoming):
        return (round_plain(incoming),)

    round_grad = jax.custom_vjp(grad_fwd)
    round_grad.defvjp(grad_keep, grad_back)

    def project_fwd(left_op, right_op):
        return jnp.dot(
            left_op.astype(jnp.bfloat16),
            right_op.astype(jnp.bfloat16),
            preferred_element_type=jnp.float32,
        )

    def project_keep(left_op, right_op):
        left_low = left_op.astype(jnp.bfloat16)
        right_low = right_op.astype(jnp.bfloat16)
        return (
            jnp.dot(left_low, right_low, preferred_element_type=jnp.float32),
            (left_low, right_low),
        )

    def project_back(saved, incoming):
        left_low, right_low = saved
        incoming_low = incoming.astype(jnp.bfloat16)
        grad_left = jnp.dot(incoming_low, right_low.T, preferred_element_type=jnp.float32)
        grad_right = jnp.dot(left_low.T, incoming_low, preferred_element_type=jnp.float32)
        return (grad_left, grad_right)

    project = jax.custom_vjp(project_fwd)
    project.defvjp(project_keep, project_back)

    def einsum_fwd(form, left_op, right_op):
        return jnp.einsum(
            form,
            left_op.astype(jnp.bfloat16),
            right_op.astype(jnp.bfloat16),
            preferred_element_type=jnp.float32,
        )

    def einsum_keep(form, left_op, right_op):
        return (einsum_fwd(form, left_op, right_op), (left_op, right_op))

    def einsum_back(form, saved, incoming):
        left_op, right_op = saved
        result_val, backward = jax.vjp(
            lambda left_in, right_in: jnp.einsum(form, left_in, right_in, precision=highest),
            left_op,
            right_op,
        )
        return backward(incoming)

    rounded_einsum = jax.custom_vjp(einsum_fwd, nondiff_argnums=(0,))
    rounded_einsum.defvjp(einsum_keep, einsum_back)

    def scan_block(carried_in, block_in):
        ssm_state, prior_doc = carried_in
        x_block, b_block, c_block, step_block, decay_block, doc_block = block_in
        order = jnp.arange(doc_block.shape[0])
        cum_decay = jnp.cumsum(decay_block, axis=0)
        allowed = (doc_block[:, None] == doc_block[None, :]) & (order[:, None] >= order[None, :])
        log_gap = jnp.where(allowed[:, :, None], cum_decay[:, None, :] - cum_decay[None, :, :], 0.0)
        decays = jnp.where(allowed[:, :, None], jnp.exp(log_gap), 0.0)
        affinity = rounded_einsum("tn,sn->ts", c_block, b_block)
        weights = affinity[:, :, None] * decays * step_block[None, :, :]
        inside = jnp.einsum("tsh,shp->thp", weights, x_block, precision=highest)
        carried = jnp.where((doc_block == prior_doc)[:, None], jnp.exp(cum_decay), 0.0)
        from_state = (
            jnp.einsum("tn,hpn->thp", c_block, ssm_state, precision=highest) * carried[:, :, None]
        )
        last_doc = doc_block[-1]
        tail_decay = (
            jnp.where(
                (doc_block == last_doc)[:, None], jnp.exp(cum_decay[-1][None, :] - cum_decay), 0.0
            )
            * step_block
        )
        keep_factor = jnp.where(last_doc == prior_doc, jnp.exp(cum_decay[-1]), 0.0)
        new_state = ssm_state * keep_factor[:, None, None] + jnp.einsum(
            "shp,sn->hpn", x_block * tail_decay[:, :, None], b_block, precision=highest
        )
        return ((new_state, last_doc), inside + from_state)

    def ssd_scan(x_heads, b_proj, c_proj, step_size, log_decay, doc_ids):
        blocks = x_heads.shape[0] // SPAN

        def shape_blocks(member):
            return member.reshape((blocks, SPAN) + member.shape[1:])

        start = (jnp.zeros((M_HEADS, M_HDIM, STATE), jnp.float32), jnp.array(-1, jnp.int32))
        members = tuple(
            (
                shape_blocks(member)
                for member in (x_heads, b_proj, c_proj, step_size, log_decay, doc_ids)
            )
        )
        final_carry, ssm_out = lax.scan(jax.checkpoint(scan_block), start, members)
        return ssm_out.reshape(x_heads.shape)

    def attention(query, key, value, doc_ids):
        length = query.shape[0]
        block_rows = min(512, length)
        blocks = length // block_rows
        group_size = HEADS // KV_HEADS
        positions = jnp.arange(length)
        query_blocks = query.reshape(blocks, block_rows, KV_HEADS, group_size, HEAD_DIM)

        def attend_block(block_in):
            query_block, query_pos, query_doc = block_in
            scores = rounded_einsum("bgrd,kgd->bgrk", query_block, key) * HEAD_DIM ** (-0.5)
            allowed = (query_pos[:, None] >= positions[None, :]) & (
                query_doc[:, None] == doc_ids[None, :]
            )
            scores = jnp.where(allowed[:, None, None, :], scores, -1e30)
            row_max = jnp.max(scores, axis=-1, keepdims=True)
            exponent = jnp.exp(scores - row_max)
            probability = round_value(exponent / jnp.sum(exponent, axis=-1, keepdims=True))
            return rounded_einsum("bgrk,kgd->bgrd", probability, value)

        result = lax.map(
            jax.checkpoint(attend_block),
            (
                query_blocks,
                positions.reshape(blocks, block_rows),
                doc_ids.reshape(blocks, block_rows),
            ),
        )
        return result.reshape(length, HEADS * HEAD_DIM)

    def mixer_piece(doc_ids, stream, weights, small_params):
        w_in, w_out, w_query, w_key, w_value, w_attn_out = weights
        norm_in, conv_weight, conv_bias, dt_bias, a_log, skip_gain, norm_gated = small_params
        length = stream.shape[0]
        normed = round_value(rms_norm(stream, norm_in))
        mixer_proj = round_grad(project(normed, w_in))
        z_gate = mixer_proj[:, :D_SSM]
        conv_in = mixer_proj[:, D_SSM : D_SSM + CONV_CH]
        dt_raw = mixer_proj[:, D_SSM + CONV_CH :]
        conv_act = jax.nn.silu(conv_reset(conv_in, doc_ids, conv_weight, conv_bias))
        x_heads = round_value(conv_act[:, :D_SSM]).reshape(length, M_HEADS, M_HDIM)
        b_proj = round_value(conv_act[:, D_SSM : D_SSM + STATE])
        c_proj = round_value(conv_act[:, D_SSM + STATE :])
        step_size = jax.nn.softplus(dt_raw + dt_bias)
        log_decay = -step_size * jnp.exp(a_log)
        ssm_out = (
            ssd_scan(x_heads, b_proj, c_proj, step_size, log_decay, doc_ids)
            + skip_gain[None, :, None] * x_heads
        )
        gated = rms_norm(ssm_out.reshape(length, D_SSM) * jax.nn.silu(z_gate), norm_gated)
        mamba_branch = round_grad(project(round_value(gated), w_out))
        positions = jnp.arange(length)
        query = round_value(
            rotate(round_grad(project(normed, w_query)).reshape(length, HEADS, HEAD_DIM), positions)
        )
        key = round_value(
            rotate(
                round_grad(project(normed, w_key)).reshape(length, KV_HEADS, HEAD_DIM), positions
            )
        )
        value = round_value(round_grad(project(normed, w_value))).reshape(
            length, KV_HEADS, HEAD_DIM
        )
        attended = attention(query, key, value, doc_ids)
        attn_branch = round_grad(project(round_value(attended), w_attn_out))
        return stream + attn_branch + mamba_branch

    def ffn_piece(resid, weights, norm_mid):
        w_gate, w_up, w_down = weights
        mid_in = round_value(rms_norm(resid, norm_mid))
        gate = round_grad(project(mid_in, w_gate))
        up_proj = round_grad(project(mid_in, w_up))
        hidden = round_value(jax.nn.silu(gate) * up_proj)
        return resid + round_grad(project(hidden, w_down))

    return (mixer_piece, ffn_piece)


def shards(
    tokens,
    segments,
    cotangent,
    w_in,
    w_out,
    w_query,
    w_key,
    w_value,
    w_attn_out,
    w_gate,
    w_up,
    w_down,
    norm_in,
    conv_weight,
    conv_bias,
    dt_bias,
    a_log,
    skip_gain,
    norm_gated,
    norm_mid,
):
    mixer_piece, ffn_piece = build_pieces()
    small_params = (norm_in, conv_weight, conv_bias, dt_bias, a_log, skip_gain, norm_gated)
    gathered = (
        lax.all_gather(w_in, ("fsdp", "dp"), axis=0, tiled=True),
        lax.all_gather(w_out, ("fsdp", "dp"), axis=1, tiled=True),
        lax.all_gather(w_query, ("fsdp", "dp"), axis=0, tiled=True),
        lax.all_gather(w_key, ("fsdp", "dp"), axis=0, tiled=True),
        lax.all_gather(w_value, ("fsdp", "dp"), axis=0, tiled=True),
        lax.all_gather(w_attn_out, ("fsdp", "dp"), axis=1, tiled=True),
        lax.all_gather(w_gate, ("fsdp", "dp"), axis=0, tiled=True),
        lax.all_gather(w_up, ("fsdp", "dp"), axis=0, tiled=True),
        lax.all_gather(w_down, ("fsdp", "dp"), axis=1, tiled=True),
    )
    mixer_w = gathered[:6]
    mixer_w = tuple((member.astype(jnp.float32) for member in mixer_w))
    index = 0
    resid, backward = jax.vjp(
        partial(mixer_piece, segments[index]),
        tokens[index].astype(jnp.float32),
        mixer_w,
        small_params,
    )
    resids = [resid]
    mixer_backs = [backward]
    ffn_w = gathered[6:]
    ffn_w = tuple((member.astype(jnp.float32) for member in ffn_w))
    index = 0
    block_out, backward = jax.vjp(ffn_piece, resids[index], ffn_w, norm_mid)
    grad_resid, grad_ffn, grad_gain = backward(cotangent[index].astype(jnp.float32))
    outputs = [block_out.astype(jnp.bfloat16)]
    resid_grads = [grad_resid]
    index = 0
    grad_stream, grad_mixer, grad_small = mixer_backs[index](resid_grads[index])
    token_grads = [grad_stream]
    big_shards = (
        lax.psum_scatter(grad_mixer[0], ("fsdp", "dp"), scatter_dimension=0, tiled=True),
        lax.psum_scatter(grad_mixer[1], ("fsdp", "dp"), scatter_dimension=1, tiled=True),
        lax.psum_scatter(grad_mixer[2], ("fsdp", "dp"), scatter_dimension=0, tiled=True),
        lax.psum_scatter(grad_mixer[3], ("fsdp", "dp"), scatter_dimension=0, tiled=True),
        lax.psum_scatter(grad_mixer[4], ("fsdp", "dp"), scatter_dimension=0, tiled=True),
        lax.psum_scatter(grad_mixer[5], ("fsdp", "dp"), scatter_dimension=1, tiled=True),
        lax.psum_scatter(grad_ffn[0], ("fsdp", "dp"), scatter_dimension=0, tiled=True),
        lax.psum_scatter(grad_ffn[1], ("fsdp", "dp"), scatter_dimension=0, tiled=True),
        lax.psum_scatter(grad_ffn[2], ("fsdp", "dp"), scatter_dimension=1, tiled=True),
    )
    small_total = lax.psum(
        (
            grad_small[0],
            grad_small[1],
            grad_small[2],
            grad_small[3],
            grad_small[4],
            grad_small[5],
            grad_small[6],
            grad_gain,
        ),
        ("fsdp", "dp"),
    )
    mixed = jnp.stack(outputs, axis=0)
    grad_tokens = jnp.stack(token_grads, axis=0)
    return (mixed, grad_tokens) + tuple(big_shards) + tuple(small_total)


def solution(mesh):
    in_specs = (
        P(("fsdp", "dp"), None, None),
        P(("fsdp", "dp"), None),
        P(("fsdp", "dp"), None, None),
        P(("fsdp", "dp"), None),
        P(None, ("fsdp", "dp")),
        P(("fsdp", "dp"), None),
        P(("fsdp", "dp"), None),
        P(("fsdp", "dp"), None),
        P(None, ("fsdp", "dp")),
        P(("fsdp", "dp"), None),
        P(("fsdp", "dp"), None),
        P(None, ("fsdp", "dp")),
        P(),
        P(),
        P(),
        P(),
        P(),
        P(),
        P(),
        P(),
    )
    out_specs = (
        P(("fsdp", "dp"), None, None),
        P(("fsdp", "dp"), None, None),
        P(("fsdp", "dp"), None),
        P(None, ("fsdp", "dp")),
        P(("fsdp", "dp"), None),
        P(("fsdp", "dp"), None),
        P(("fsdp", "dp"), None),
        P(None, ("fsdp", "dp")),
        P(("fsdp", "dp"), None),
        P(("fsdp", "dp"), None),
        P(None, ("fsdp", "dp")),
        P(),
        P(),
        P(),
        P(),
        P(),
        P(),
        P(),
        P(),
    )
    return jax.shard_map(shards, mesh=mesh, in_specs=in_specs, out_specs=out_specs, check_vma=False)
```

profile of v0, /device:TPU:1, one launch (start us, length us, event | category | flops | bytes accessed | tf_op | source)
XLA Modules:
  0.0 2393.2 jit_solution(16872555103438316229)
XLA Ops:
  20.9 69.7 %all_gather.28 = bf16[1024,256]{1,0:T(8,128)(2,1)S(1)} all-gather(bf16[32,256]{1,0:T(8,128)(2,1)S(1)} %copy-done.102), channel_id=1, replica_groups=mesh['fsdp'=16,'dp'=2] {'fsdp','dp'}, dimensions={0}, use_global_device_ids=true | all-gather | bytes 540672 | tf_op jit(solution)/shard_map/all_gather | solution.py:281
  97.8 67.9 %all_gather.29 = bf16[1024,256]{1,0:T(8,128)(2,1)S(1)} all-gather(bf16[32,256]{1,0:T(8,128)(2,1)S(1)} %copy-done.103), channel_id=1, replica_groups=mesh['fsdp'=16,'dp'=2] {'fsdp','dp'}, dimensions={0}, use_global_device_ids=true | all-gather | bytes 540672 | tf_op jit(solution)/shard_map/all_gather | solution.py:282
  195.4 45.1 %while.77 = (s32[]{:T(128)}, bf16[2,512,2,4,128]{4,1,3,2,0:T(8,128)(2,1)}, s32[2,512]{1,0:T(2,128)S(1)}, s32[2,512]{1,0:T(2,128)S(1)}, s32[1,1024]{1,0:T(1,128)S...) while((s32[]{:T(128)}, ...), condition=%wide.region_4.5_spmd.clone, body=%wide.region_1.4_spmd.clone.sunk | while | flops 2174223360 | bytes 72401064 | solution.py:195
  312.3 298.5 %while.78 = (s32[]{:T(128)}, f32[24,64,128]{2,1,0:T(8,128)S(1)}, s32[]{:T(128)}, f32[8,128,24,64]{1,0,3,2:T(8,128)}, f32[8,24,64,128]{3,2,1,0:T(8,128)}, /*index...) while((s32[]{:T(128)}, f32[24,64,128]{2,1,0:T(8,128)S(1)}, ...), condition=%wide.region_7.8_spmd.clone, body=%wide.region_5.7_spmd.clone.sunk | while | flops 914154752 | bytes 10073902 | solution.py:172
  438.9 20.8 dynamic_update_slice.111
  688.7 293.7 %while.79 = (s32[]{:T(128)}, f32[1024,2,128]{2,0,1:T(8,128)}, f32[1024,2,128]{0,2,1:T(8,128)}, f32[2,512,2,4,128]{4,1,0,3,2:T(8,128)}, f32[2,512,2,4,128]{4,1,3,...) while((s32[]{:T(128)}, f32[1024,2,128]{2,0,1:T(8,128)}, ...), condition=%wide.region_17.18_spmd.clone, body=%wide.region_11.17_spmd.clone.sunk | while | flops 26999521280 | bytes 500060800 | solution.py:195
  729.7 24.6 %fusion.385 = (f32[512,2,4]{0,2,1:T(4,128)S(1)}, f32[2,512,4,1024]{3,1,2,0:T(8,128)}) fusion(f32[512,2,4]{0,2,1:T(4,128)S(1)} %multiply_divide_fusion.2, f32[512,2,4]{0,2,1:T(4,128)S(1)} %get-tuple-element.1945, f32[2,1024,512,4]{1,2,3,0:T(8,128)} %copy-done, pred[512,1024]{1,0:T(8,128)(4,1)S(1)} %compare_and_fusion.4, ...), kind=kOutput, calls=%fused_computation.89.clone.1 | convolution fusion | flops 6467612672 | bytes 37273600 | tf_op jit(solution)/shard_map/transpose(jvp())/while/body/eval_jaxpr/checkpoint/transpose(jvp(bgrk,kgd->bgrd))/dot_general | solution.py:193
  790.3 31.0 %fusion.389 = f32[1024,2,128]{2,0,1:T(8,128)} fusion(f32[2,1024,512,4]{1,2,3,0:T(8,128)} %fusion.388, f32[512,2,4,128]{3,0,2,1:T(8,128)} %dynamic-slice_bitcast_fusion.19, f32[1024,2,128]{2,0,1:T(8,128)} %get-tuple-element.2143, pred[]{:T(512)S(6)} %compare.35), kind=kOutput, calls=%fused_computation.109.clone.1 | convolution fusion | flops 6442975232 | bytes 20971520 | tf_op jit(solution)/shard_map/transpose(jvp())/while/body/eval_jaxpr/checkpoint/transpose(jvp(bgrd,kgd->bgrk))/dot_general | solution.py:185
  861.0 24.6 %fusion.385 = (f32[512,2,4]{0,2,1:T(4,128)S(1)}, f32[2,512,4,1024]{3,1,2,0:T(8,128)}) fusion(f32[512,2,4]{0,2,1:T(4,128)S(1)} %multiply_divide_fusion.2, f32[512,2,4]{0,2,1:T(4,128)S(1)} %get-tuple-element.1945, f32[2,1024,512,4]{1,2,3,0:T(8,128)} %copy-done, pred[512,1024]{1,0:T(8,128)(4,1)S(1)} %compare_and_fusion.4, ...), kind=kOutput, calls=%fused_computation.89.clone.1 | convolution fusion | flops 6467612672 | bytes 37273600 | tf_op jit(solution)/shard_map/transpose(jvp())/while/body/eval_jaxpr/checkpoint/transpose(jvp(bgrk,kgd->bgrd))/dot_general | solution.py:193
  921.6 31.1 %fusion.389 = f32[1024,2,128]{2,0,1:T(8,128)} fusion(f32[2,1024,512,4]{1,2,3,0:T(8,128)} %fusion.388, f32[512,2,4,128]{3,0,2,1:T(8,128)} %dynamic-slice_bitcast_fusion.19, f32[1024,2,128]{2,0,1:T(8,128)} %get-tuple-element.2143, pred[]{:T(512)S(6)} %compare.35), kind=kOutput, calls=%fused_computation.109.clone.1 | convolution fusion | flops 6442975232 | bytes 20971520 | tf_op jit(solution)/shard_map/transpose(jvp())/while/body/eval_jaxpr/checkpoint/transpose(jvp(bgrd,kgd->bgrk))/dot_general | solution.py:185
  1086.9 559.7 %while.80 = (s32[]{:T(128)}, f32[24,64,128]{2,1,0:T(8,128)}, f32[8,128,24,64]{1,0,3,2:T(8,128)}, f32[8,128,128]{2,1,0:T(8,128)}, f32[8,128,128]{2,1,0:T(8,128)},...) while((s32[]{:T(128)}, f32[24,64,128]{2,1,0:T(8,128)}, ...), condition=%wide.region_30.31_spmd.clone, body=%wide.region_19.30_spmd.clone.sunk | while | flops 2180012288 | bytes 25603896 | solution.py:172
  1126.6 20.8 dynamic_update_slice.117
  1196.7 20.8 dynamic_update_slice.117
  1266.7 20.9 dynamic_update_slice.117
  1336.9 20.8 dynamic_update_slice.117
  1406.9 20.8 dynamic_update_slice.117
  1477.0 20.8 dynamic_update_slice.117
  1547.0 20.8 dynamic_update_slice.117
  1617.1 20.8 dynamic_update_slice.117
  1755.2 41.7 %all-reduce.25 = (f32[1024]{0:T(1024)}, f32[4,1792]{1,0:T(4,128)}, f32[1792]{0:T(1024)}, f32[24]{0:T(128)}, f32[24]{0:T(128)}, /*index=5*/f32[24]{0:T(128)}, f32[1536]{0:T(1024)}, f32[1024]{0:T(1024)}) all-reduce(f32[1024]{0:T(1024)S(1)} %get-tuple-element.1423, ...), channel_id=1, replica_groups=mesh['fsdp'=16,'dp'=2] {'fsdp','dp'}, use_global_device_ids=true, to_apply=%region_42.43 | all-reduce | flops 12616 | bytes 100928 | tf_op jit(solution)/shard_map/psum | solution.py:320
  1796.9 45.7 %reduce-scatter.22.cloned.1.call-done = f32[32,2048]{1,0:T(8,128)} async-done(((f32[1024,2048]{1,0:T(8,128)}), f32[32,2048]{1,0:T(8,128)}) %reduce-scatter.22.cloned.1.call-update) | async-done | bytes 262160 | tf_op jit(solution)/shard_map/reduce_scatter | solution.py:316
  1842.6 186.9 %reduce-scatter.24.cloned.1.call-done = f32[32,2048]{1,0:T(8,128)} async-done(((f32[1024,2048]{1,0:T(8,128)}), f32[32,2048]{1,0:T(8,128)}) %reduce-scatter.24.cloned.1.call-update) | async-done | bytes 262160 | tf_op jit(solution)/shard_map/reduce_scatter | solution.py:317
  2029.5 186.9 %reduce-scatter.26.cloned.1.call-done = f32[2048,32]{0,1:T(8,128)} async-done(((f32[2048,1024]{0,1:T(8,128)}), f32[2048,32]{0,1:T(8,128)}) %reduce-scatter.26.cloned.1.call-update) | async-done | bytes 262160 | tf_op jit(solution)/shard_map/reduce_scatter | solution.py:318
  2216.4 170.1 %reduce-scatter.10.cloned.1.call-done = f32[32,3352]{1,0:T(8,128)} async-done(((f32[1024,3352]{1,0:T(8,128)}), f32[32,3352]{1,0:T(8,128)}) %reduce-scatter.10.cloned.1.call-update) | async-done | bytes 429072 | tf_op jit(solution)/shard_map/reduce_scatter | solution.py:310
  (1081 shorter events, 1255.3 us)
Async XLA Ops:
  7.2 163.3 %all-gather.8.cloned.1.call-start = ((), (), s32[]{:S(2)}) async-start(), calls=%async_computation.9 | async-start | bytes 2162688 | tf_op jit(solution)/shard_map/all_gather | solution.py:280
  7.9 241.6 %all-gather.10.cloned.1.call-start = ((), (), s32[]{:S(2)}) async-start(), calls=%async_computation.10 | async-start | bytes 2162688 | tf_op jit(solution)/shard_map/all_gather | solution.py:283
  8.7 247.4 %all-gather.20.cloned.1.call-start = ((), (), s32[]{:S(2)}) async-start(), calls=%async_computation.15 | async-start | bytes 4325376 | tf_op jit(solution)/shard_map/all_gather | solution.py:286
  9.4 259.7 %all-gather.12.cloned.1.call-start = ((), (), s32[]{:S(2)}) async-start(), calls=%async_computation.11 | async-start | bytes 7299072 | tf_op jit(solution)/shard_map/all_gather | solution.py:278
  10.0 613.5 %all-gather.14.cloned.1.call-start = ((), (), s32[]{:S(2)}) async-start(), calls=%async_computation.12 | async-start | bytes 3244032 | tf_op jit(solution)/shard_map/all_gather | solution.py:279
  10.6 622.9 %all-gather.18.cloned.1.call-start = ((), (), s32[]{:S(2)}) async-start(), calls=%async_computation.14 | async-start | bytes 4325376 | tf_op jit(solution)/shard_map/all_gather | solution.py:285
  11.2 632.0 %all-gather.16.cloned.1.call-start = ((), (), s32[]{:S(2)}) async-start(), calls=%async_computation.13 | async-start | bytes 4325376 | tf_op jit(solution)/shard_map/all_gather | solution.py:284
  11.9 1785.0 %reduce-scatter.16.cloned.1.call-start = ((), (), s32[]{:S(2)}) async-start(), calls=%async_computation.19 | async-start | bytes 1081344 | tf_op jit(solution)/shard_map/reduce_scatter | solution.py:313
  95.7 185.8 %copy-start.68 = (f32[1792]{0:T(1024)}, f32[1792]{0:T(1024)S(1)}, u32[]{:S(2)}) copy-start(f32[1792]{0:T(1024)S(1)} %get-tuple-element.1425) | copy-start | bytes 21508
  95.7 185.8 %copy-start.70 = (f32[1792]{0:T(1024)}, f32[1792]{0:T(1024)S(1)}, u32[]{:S(2)}) copy-start(f32[1792]{0:T(1024)S(1)} %get-tuple-element.1426) | copy-start | bytes 21508
  95.7 185.8 %copy-start.72 = (f32[1792]{0:T(1024)}, f32[1792]{0:T(1024)S(1)}, u32[]{:S(2)}) copy-start(f32[1792]{0:T(1024)S(1)} %get-tuple-element.1427) | copy-start | bytes 21508
  95.7 185.8 %copy-start.74 = (f32[1792]{0:T(1024)}, f32[1792]{0:T(1024)S(1)}, u32[]{:S(2)}) copy-start(f32[1792]{0:T(1024)S(1)} %get-tuple-element.1428) | copy-start | bytes 21508
  95.8 185.7 %copy-start.98 = (pred[1024]{0:T(1024)(128)(4,1)}, pred[1024]{0:T(1024)(128)(4,1)S(1)}, u32[]{:S(2)}) copy-start(pred[1024]{0:T(1024)(128)(4,1)S(1)} %get-tuple-element.1598) | copy-start | bytes 3076
  95.8 185.7 %copy-start.100 = (pred[1024]{0:T(1024)(128)(4,1)}, pred[1024]{0:T(1024)(128)(4,1)S(1)}, u32[]{:S(2)}) copy-start(pred[1024]{0:T(1024)(128)(4,1)S(1)} %get-tuple-element.1599) | copy-start | bytes 3076
  96.6 200.5 %copy-start.108 = (f32[24]{0:T(128)}, f32[24]{0:T(128)S(1)}, u32[]{:S(2)}) copy-start(f32[24]{0:T(128)S(1)} %exp.154) | copy-start | bytes 292
  312.3 298.5 %copy-start.65 = (f32[1536]{0:T(1024)S(1)}, f32[1536]{0:T(1024)}, u32[]{:S(2)}) copy-start(f32[1536]{0:T(1024)} %mul.1095) | copy-start | bytes 18436
  987.9 808.9 %reduce-scatter.18.cloned.1.call-start = ((), (), s32[]{:S(2)}) async-start(), calls=%async_computation.20 | async-start | bytes 1081344 | tf_op jit(solution)/shard_map/reduce_scatter | solution.py:314
  990.6 806.2 %reduce-scatter.12.cloned.1.call-start = ((), (), s32[]{:S(2)}) async-start(), calls=%async_computation.17 | async-start | bytes 6488064 | tf_op jit(solution)/shard_map/reduce_scatter | solution.py:311
  999.4 797.5 %reduce-scatter.14.cloned.1.call-start = ((), (), s32[]{:S(2)}) async-start(), calls=%async_computation.18 | async-start | bytes 4325376 | tf_op jit(solution)/shard_map/reduce_scatter | solution.py:312
  1017.7 779.2 %reduce-scatter.20.cloned.1.call-start = ((), (), s32[]{:S(2)}) async-start(), calls=%async_computation.21 | async-start | bytes 4325376 | tf_op jit(solution)/shard_map/reduce_scatter | solution.py:315
  1025.2 817.4 %reduce-scatter.22.cloned.1.call-start = ((), (), s32[]{:S(2)}) async-start(), calls=%async_computation.22 | async-start | bytes 8650752 | tf_op jit(solution)/shard_map/reduce_scatter | solution.py:316
  1036.1 993.4 %reduce-scatter.24.cloned.1.call-start = ((), (), s32[]{:S(2)}) async-start(), calls=%async_computation.23 | async-start | bytes 8650752 | tf_op jit(solution)/shard_map/reduce_scatter | solution.py:317
  1045.1 1171.3 %reduce-scatter.26.cloned.1.call-start = ((), (), s32[]{:S(2)}) async-start(), calls=%async_computation.24 | async-start | bytes 8650752 | tf_op jit(solution)/shard_map/reduce_scatter | solution.py:318
  1080.2 1306.3 %reduce-scatter.10.cloned.1.call-start = ((), (), s32[]{:S(2)}) async-start(), calls=%async_computation.16 | async-start | bytes 14598144 | tf_op jit(solution)/shard_map/reduce_scatter | solution.py:310
  (184 other events, 2216.9 us)
Sparse Core Ops, SparseCore 0:
  11.0 60.0 all-gather.7
  74.1 56.2 all-gather.9
  133.3 61.9 all-gather.19
  198.1 70.9 all-gather.11
  271.9 57.6 all-gather.13
  332.4 60.9 all-gather.17
  396.3 60.6 all-gather.15
  988.1 131.0 reduce-scatter.15
  1122.1 131.1 reduce-scatter.17
  1259.3 111.7 reduce-scatter.11
  1374.0 140.5 reduce-scatter.13
  1517.3 139.0 reduce-scatter.19
  1659.4 183.1 reduce-scatter.21
  1845.4 184.0 reduce-scatter.23
  2032.3 184.0 reduce-scatter.25
  2223.9 162.5 reduce-scatter.9
where the time goes:
time: 2420 us; the launch traced here: 2390 us
  local copies, waits for them, and re-layouts  652 us (27%)
  waiting for transfers between devices  598 us (25%)
  matrix products  591 us (24%)
  other arithmetic  302 us (12%)
  blocking collectives  179 us (7%)
  loops' own time  54.8 us (2%)
    dynamic_update_slice x24, local copies, waits for them, and re-layouts, ssd_scan(): final_carry, ssm_out = lax.scan(jax.checkpoint(scan_block), start, members)  342 us
    reduce_scatter x1, waiting for transfers between devices, shards(): lax.psum_scatter(grad_ffn[1], ('fsdp', 'dp'), scatter_dimension=0, tiled=...  187 us
    reduce_scatter x1, waiting for transfers between devices, shards(): lax.psum_scatter(grad_ffn[2], ('fsdp', 'dp'), scatter_dimension=1, tiled=...  187 us
    reduce_scatter x1, waiting for transfers between devices, shards(): lax.psum_scatter(grad_mixer[0], ('fsdp', 'dp'), scatter_dimension=0, tile...  170 us
    dot_general x24, matrix products, scan_block(): inside = jnp.einsum('tsh,shp->thp', weights, x_block, precision=highest)  108 us
    dot_general x6, matrix products, attend_block(): rounded_einsum('bgrd,kgd->bgrk', query_block, key) * HEAD_DIM ** (-0.5)  101 us
    all_gather x1, blocking collectives, shards(): lax.all_gather(w_key, ('fsdp', 'dp'), axis=0, tiled=True)  69.7 us
    dot_general x9, matrix products, project_keep(): jnp.dot(left_low, right_low, preferred_element_type=jnp.float32)  68 us
  transfers between devices with their start and end apart: 16, of which 5 were waited for; matrix products, arithmetic and copies ran while one was open for 50% of the time, Pallas kernels for 0%

commit v1 on v0

v1 whole, which is shorter than its diff:
```python
from functools import partial

import jax
import jax.numpy as jnp
from jax import lax
from jax.experimental import pallas as pl
from jax.experimental.pallas import tpu as pltpu
from jax.sharding import PartitionSpec as P

HEADS = 8
KV_HEADS = 2
HEAD_DIM = 128
M_HEADS = 24
M_HDIM = 64
STATE = 128
SPAN = 128
D_SSM = 1536
CONV_CH = 1792
QKV = (HEADS + 2 * KV_HEADS) * HEAD_DIM
PAIRS = M_HEADS // 2
QROWS = 256
REACH = 512

AXES = ("fsdp", "dp")
bf16 = jnp.bfloat16
f32 = jnp.float32
eps = 1e-06
rope_base = 100000000000.0
NEG = -1e30

NT = (((1,), (1,)), ((), ()))
TN = (((0,), (0,)), ((), ()))


def mm(left, right):
    return jnp.dot(left, right, preferred_element_type=f32)


def mm_nt(left, right):
    return lax.dot_general(left, right, NT, preferred_element_type=f32)


def mm_tn(left, right):
    return lax.dot_general(left, right, TN, preferred_element_type=f32)


def exact_mm(left, right):
    return jnp.dot(left, right, precision=lax.Precision.HIGHEST, preferred_element_type=f32)


def split_mm(value, selector):
    high = value.astype(bf16)
    low = (value - high.astype(f32)).astype(bf16)
    return mm(high, selector) + mm(low, selector)


def iota2(shape, axis):
    return lax.broadcasted_iota(jnp.int32, shape, axis)


def head_spread():
    rows = iota2((SPAN, D_SSM), 0)
    cols = iota2((SPAN, D_SSM), 1)
    return jnp.where(cols // M_HDIM == rows, 1.0, 0.0).astype(bf16)


def head_gather():
    rows = iota2((D_SSM, SPAN), 0)
    cols = iota2((D_SSM, SPAN), 1)
    return jnp.where(rows // M_HDIM == cols, 1.0, 0.0).astype(bf16)


def split_pair(block):
    lanes = iota2(block.shape, 1)
    zero = jnp.zeros_like(block)
    return jnp.concatenate(
        [jnp.where(lanes < M_HDIM, block, zero), jnp.where(lanes < M_HDIM, zero, block)], axis=0
    )


def block_terms(ld_ref, st_ref, spread):
    ld = ld_ref[...]
    st = st_ref[...]
    rows = iota2((SPAN, SPAN), 0)
    cols = iota2((SPAN, SPAN), 1)
    cum = exact_mm(jnp.where(rows >= cols, 1.0, 0.0), ld)
    cum_t = cum.T
    st_t = st.T
    doc = st[:, 127:128]
    prior = st[:, 126:127]
    last = st[:, 125:126]
    doc_row = st_t[127:128, :]
    carried = jnp.where(doc == prior, jnp.exp(cum), 0.0)
    gap = jnp.where(doc == last, jnp.exp(cum[SPAN - 1 : SPAN, :] - cum), 0.0)
    keep = jnp.where(last == prior, jnp.exp(cum[SPAN - 1 : SPAN, :]), 0.0)
    keep = keep[0:8, :]
    return (st, cum, cum_t, st_t, doc, doc_row, carried, gap, keep)


def scan_fwd_kernel(x_ref, b_ref, c_ref, ld_ref, st_ref, y_ref, states_ref, state):
    spread = head_spread()

    @pl.when(pl.program_id(0) == 0)
    def _():
        state[...] = jnp.zeros_like(state)

    st, cum, cum_t, st_t, doc, doc_row, carried, gap, keep = block_terms(ld_ref, st_ref, spread)
    rows = iota2((SPAN, SPAN), 0)
    cols = iota2((SPAN, SPAN), 1)
    bias = jnp.where((doc == doc_row) & (rows >= cols), 0.0, NEG)
    b_blk = b_ref[...]
    c_blk = c_ref[...]
    affinity = mm_nt(c_blk, b_blk)
    old = state[...]
    old_low = old.astype(bf16)
    states_ref[0] = old_low
    from_state = mm(c_blk, old_low) * split_mm(carried, spread)
    for pair in range(PAIRS):
        lo, hi = pair * SPAN, (pair + 1) * SPAN
        mats = []
        for h in (2 * pair, 2 * pair + 1):
            decay = jnp.exp(cum[:, h : h + 1] - cum_t[h : h + 1, :] + bias)
            mats.append((affinity * decay * st_t[h : h + 1, :]).astype(bf16))
        inside = mm(jnp.concatenate(mats, axis=1), split_pair(x_ref[:, lo:hi]))
        y_ref[:, lo:hi] = inside + from_state[:, lo:hi]
    tail = split_mm(gap * st, spread)
    pushed = (x_ref[...].astype(f32) * tail).astype(bf16)
    state[...] = old * split_mm(keep, spread)[0:1, :] + mm_tn(b_blk, pushed)


def scan_bwd_kernel(
    x_ref, b_ref, c_ref, ld_ref, st_ref, states_ref, dy_ref,
    dx_ref, db_ref, dc_ref, dst_ref, dld_ref, dstate, grow, gcol,
):
    spread = head_spread()
    gather = head_gather()

    @pl.when(pl.program_id(0) == 0)
    def _():
        dstate[...] = jnp.zeros_like(dstate)
        grow[...] = jnp.zeros_like(grow)
        gcol[...] = jnp.zeros_like(gcol)

    st, cum, cum_t, st_t, doc, doc_row, carried, gap, keep = block_terms(ld_ref, st_ref, spread)
    rows = iota2((SPAN, SPAN), 0)
    cols = iota2((SPAN, SPAN), 1)
    bias = jnp.where((doc == doc_row) & (cols >= rows), 0.0, NEG)
    b_blk = b_ref[...]
    c_blk = c_ref[...]
    x_blk = x_ref[...]
    dy = dy_ref[...]
    dy_low = dy.astype(bf16)
    affinity = mm_nt(b_blk, c_blk)
    old_low = states_ref[0]
    d_new = dstate[...]
    d_new_low = d_new.astype(bf16)
    carried_wide = split_mm(carried, spread)
    tail_wide = split_mm(gap * st, spread)
    keep_wide = split_mm(keep, spread)[0:1, :]
    from_tail = mm(b_blk, d_new_low)
    d_aff = jnp.zeros((SPAN, SPAN), f32)
    for pair in range(PAIRS):
        lo, hi = pair * SPAN, (pair + 1) * SPAN
        d_mats = mm_nt(split_pair(x_blk[:, lo:hi]), dy_low[:, lo:hi])
        mats = []
        for which, h in enumerate((2 * pair, 2 * pair + 1)):
            step = st[:, h : h + 1]
            decay = jnp.exp(cum_t[h : h + 1, :] - cum[:, h : h + 1] + bias)
            scaled = affinity * decay
            mats.append((scaled * step).astype(bf16))
            d_mat = d_mats[which * SPAN : (which + 1) * SPAN, :]
            d_aff = d_aff + d_mat * decay * step
            products = d_mat * scaled
            gcol[:, h : h + 1] = jnp.sum(products, axis=1, keepdims=True)
            grow[h : h + 1, :] = jnp.sum(products * step, axis=0, keepdims=True)
        inside = mm(jnp.concatenate(mats, axis=1), split_pair(dy_low[:, lo:hi]))
        dx_ref[:, lo:hi] = inside + from_tail[:, lo:hi] * tail_wide[:, lo:hi]
    flowing = dy * carried_wide
    flowing_low = flowing.astype(bf16)
    d_cum = split_mm(flowing * mm(c_blk, old_low), gather)
    d_tail = split_mm(x_blk.astype(f32) * from_tail, gather)
    moved = d_tail * gap * st
    d_keep = jnp.sum(d_new * old_low.astype(f32), axis=0, keepdims=True)
    d_keep = split_mm(jnp.broadcast_to(d_keep, (8, D_SSM)), gather) * keep
    at_end = jnp.sum(moved, axis=0, keepdims=True) + d_keep[0:1, :]
    d_cum = d_cum - moved + grow[...].T - gcol[...] * st
    d_cum = d_cum + jnp.where(rows == SPAN - 1, at_end, 0.0)
    dst_ref[...] = gcol[...] + d_tail * gap
    dld_ref[...] = exact_mm(jnp.where(cols >= rows, 1.0, 0.0), d_cum)
    d_aff_low = d_aff.astype(bf16)
    pushed = (x_blk.astype(f32) * tail_wide).astype(bf16)
    dc_ref[...] = mm_tn(d_aff_low, b_blk) + mm_nt(flowing_low, old_low)
    db_ref[...] = mm(d_aff_low, c_blk) + mm_nt(pushed, d_new_low)
    dstate[...] = d_new * keep_wide + mm_tn(c_blk, flowing_low)


def scan_fwd(act_low, ld, st):
    length = act_low.shape[0]
    blocks = length // SPAN
    return pl.pallas_call(
        scan_fwd_kernel,
        grid=(blocks,),
        in_specs=[
            pl.BlockSpec((SPAN, D_SSM), lambda i: (i, 0)),
            pl.BlockSpec((SPAN, STATE), lambda i: (i, D_SSM // STATE)),
            pl.BlockSpec((SPAN, STATE), lambda i: (i, D_SSM // STATE + 1)),
            pl.BlockSpec((SPAN, 128), lambda i: (i, 0)),
            pl.BlockSpec((SPAN, 128), lambda i: (i, 0)),
        ],
        out_specs=[
            pl.BlockSpec((SPAN, D_SSM), lambda i: (i, 0)),
            pl.BlockSpec((1, STATE, D_SSM), lambda i: (i, 0, 0)),
        ],
        out_shape=[
            jax.ShapeDtypeStruct((length, D_SSM), f32),
            jax.ShapeDtypeStruct((blocks, STATE, D_SSM), bf16),
        ],
        scratch_shapes=[pltpu.VMEM((STATE, D_SSM), f32)],
        compiler_params=pltpu.CompilerParams(vmem_limit_bytes=40 * 2**20),
    )(act_low, act_low, act_low, ld, st)


def scan_bwd(act_low, ld, st, states, dy):
    length = act_low.shape[0]
    blocks = length // SPAN
    end = blocks - 1
    return pl.pallas_call(
        scan_bwd_kernel,
        grid=(blocks,),
        in_specs=[
            pl.BlockSpec((SPAN, D_SSM), lambda i: (end - i, 0)),
            pl.BlockSpec((SPAN, STATE), lambda i: (end - i, D_SSM // STATE)),
            pl.BlockSpec((SPAN, STATE), lambda i: (end - i, D_SSM // STATE + 1)),
            pl.BlockSpec((SPAN, 128), lambda i: (end - i, 0)),
            pl.BlockSpec((SPAN, 128), lambda i: (end - i, 0)),
            pl.BlockSpec((1, STATE, D_SSM), lambda i: (end - i, 0, 0)),
            pl.BlockSpec((SPAN, D_SSM), lambda i: (end - i, 0)),
        ],
        out_specs=[
            pl.BlockSpec((SPAN, D_SSM), lambda i: (end - i, 0)),
            pl.BlockSpec((SPAN, STATE), lambda i: (end - i, 0)),
            pl.BlockSpec((SPAN, STATE), lambda i: (end - i, 0)),
            pl.BlockSpec((SPAN, 128), lambda i: (end - i, 0)),
            pl.BlockSpec((SPAN, 128), lambda i: (end - i, 0)),
        ],
        out_shape=[
            jax.ShapeDtypeStruct((length, D_SSM), f32),
            jax.ShapeDtypeStruct((length, STATE), f32),
            jax.ShapeDtypeStruct((length, STATE), f32),
            jax.ShapeDtypeStruct((length, 128), f32),
            jax.ShapeDtypeStruct((length, 128), f32),
        ],
        scratch_shapes=[
            pltpu.VMEM((STATE, D_SSM), f32),
            pltpu.VMEM((SPAN, SPAN), f32),
            pltpu.VMEM((SPAN, SPAN), f32),
        ],
        compiler_params=pltpu.CompilerParams(vmem_limit_bytes=40 * 2**20),
    )(act_low, act_low, act_low, ld, st, states, dy)


def key_span(block):
    return max(0, block * QROWS - REACH), (block + 1) * QROWS


def fill_bias(doc_col_ref, doc_row_ref, bias, blocks):
    for block in range(blocks):
        k0, k1 = key_span(block)
        q0, q1 = block * QROWS, (block + 1) * QROWS
        shape = (k1 - k0, QROWS)
        allowed = (doc_col_ref[k0:k1, :] == doc_row_ref[:, q0:q1]) & (
            iota2(shape, 0) + k0 <= iota2(shape, 1) + q0
        )
        bias[block, 0 : k1 - k0, :] = jnp.where(allowed, 0.0, NEG)


def attend_fwd_kernel(q_ref, k_ref, v_ref, doc_col_ref, doc_row_ref, out_ref, lse_ref, bias):
    blocks = q_ref.shape[0] // QROWS

    @pl.when(pl.program_id(0) == 0)
    def _():
        fill_bias(doc_col_ref, doc_row_ref, bias, blocks)

    for block in range(blocks):
        k0, k1 = key_span(block)
        q0, q1 = block * QROWS, (block + 1) * QROWS
        scores = mm_nt(k_ref[k0:k1, :], q_ref[q0:q1, :]) * HEAD_DIM ** (-0.5)
        scores = scores + bias[block, 0 : k1 - k0, :]
        top = jnp.max(scores, axis=0, keepdims=True)
        exponent = jnp.exp(scores - top)
        total = jnp.sum(exponent, axis=0, keepdims=True)
        probability = (exponent * (1.0 / total)).astype(bf16)
        out_ref[q0:q1, :] = mm_tn(v_ref[k0:k1, :], probability).T.astype(bf16)
        lse_ref[0, :, q0:q1] = top + jnp.log(total)


def attend_bwd_kernel(
    q_ref, k_ref, v_ref, do_ref, lse_ref, doc_col_ref, doc_row_ref, dq_ref, dk_ref, dv_ref, bias
):
    blocks = q_ref.shape[0] // QROWS

    @pl.when((pl.program_id(0) == 0) & (pl.program_id(1) == 0))
    def _():
        fill_bias(doc_col_ref, doc_row_ref, bias, blocks)

    @pl.when(pl.program_id(1) == 0)
    def _():
        dk_ref[...] = jnp.zeros_like(dk_ref)
        dv_ref[...] = jnp.zeros_like(dv_ref)

    for block in range(blocks):
        k0, k1 = key_span(block)
        q0, q1 = block * QROWS, (block + 1) * QROWS
        query = q_ref[q0:q1, :]
        key = k_ref[k0:k1, :]
        d_out = do_ref[q0:q1, :].astype(bf16)
        scores = mm_nt(key, query) * HEAD_DIM ** (-0.5) + bias[block, 0 : k1 - k0, :]
        probability = jnp.exp(scores - lse_ref[0, :, q0:q1])
        dv_ref[k0:k1, :] += mm(probability.astype(bf16), d_out)
        d_prob = mm_nt(v_ref[k0:k1, :], d_out)
        delta = jnp.sum(probability * d_prob, axis=0, keepdims=True)
        d_scores = (probability * (d_prob - delta) * HEAD_DIM ** (-0.5)).astype(bf16)
        dk_ref[k0:k1, :] += mm(d_scores, query)
        dq_ref[q0:q1, :] = mm_tn(key, d_scores).T


def attend_fwd(query, key, value, doc_col, doc_row):
    length = query.shape[0]
    group = HEADS // KV_HEADS
    blocks = length // QROWS
    return pl.pallas_call(
        attend_fwd_kernel,
        grid=(HEADS,),
        in_specs=[
            pl.BlockSpec((length, HEAD_DIM), lambda h: (0, h)),
            pl.BlockSpec((length, HEAD_DIM), lambda h: (0, h // group)),
            pl.BlockSpec((length, HEAD_DIM), lambda h: (0, h // group)),
            pl.BlockSpec((length, 1), lambda h: (0, 0)),
            pl.BlockSpec((1, length), lambda h: (0, 0)),
        ],
        out_specs=[
            pl.BlockSpec((length, HEAD_DIM), lambda h: (0, h)),
            pl.BlockSpec((1, 1, length), lambda h: (h, 0, 0)),
        ],
        out_shape=[
            jax.ShapeDtypeStruct((length, HEADS * HEAD_DIM), bf16),
            jax.ShapeDtypeStruct((HEADS, 1, length), f32),
        ],
        scratch_shapes=[pltpu.VMEM((blocks, QROWS + REACH, QROWS), f32)],
        compiler_params=pltpu.CompilerParams(vmem_limit_bytes=40 * 2**20),
    )(query, key, value, doc_col, doc_row)


def attend_bwd(query, key, value, d_out, lse, doc_col, doc_row):
    length = query.shape[0]
    group = HEADS // KV_HEADS
    blocks = length // QROWS
    per_query = pl.BlockSpec((length, HEAD_DIM), lambda g, r: (0, g * group + r))
    per_key = pl.BlockSpec((length, HEAD_DIM), lambda g, r: (0, g))
    return pl.pallas_call(
        attend_bwd_kernel,
        grid=(KV_HEADS, group),
        in_specs=[
            per_query,
            per_key,
            per_key,
            per_query,
            pl.BlockSpec((1, 1, length), lambda g, r: (g * group + r, 0, 0)),
            pl.BlockSpec((length, 1), lambda g, r: (0, 0)),
            pl.BlockSpec((1, length), lambda g, r: (0, 0)),
        ],
        out_specs=[per_query, per_key, per_key],
        out_shape=[
            jax.ShapeDtypeStruct((length, HEADS * HEAD_DIM), f32),
            jax.ShapeDtypeStruct((length, KV_HEADS * HEAD_DIM), f32),
            jax.ShapeDtypeStruct((length, KV_HEADS * HEAD_DIM), f32),
        ],
        scratch_shapes=[pltpu.VMEM((blocks, QROWS + REACH, QROWS), f32)],
        compiler_params=pltpu.CompilerParams(vmem_limit_bytes=40 * 2**20),
    )(query, key, value, d_out, lse, doc_col, doc_row)


def inv_norm(values):
    return lax.rsqrt(jnp.mean(values * values, axis=-1, keepdims=True) + eps)


def norm_back(normed_grad, gain, values, inv):
    unit = values * inv
    scaled = normed_grad * gain
    back = inv * (scaled - unit * jnp.mean(scaled * unit, axis=-1, keepdims=True))
    return back, jnp.sum(normed_grad * unit, axis=0)


def angles(length):
    half_dim = HEAD_DIM // 2
    frequency = rope_base ** (-jnp.arange(half_dim, dtype=f32) / half_dim)
    table = jnp.arange(length).astype(f32)[:, None] * frequency[None, :]
    return jnp.cos(table), jnp.sin(table)


def turn(values, cosine, sine):
    length, width = values.shape
    heads = values.reshape(length, width // HEAD_DIM, HEAD_DIM)
    front, back = jnp.split(heads, 2, axis=-1)
    cosine, sine = cosine[:, None, :], sine[:, None, :]
    turned = jnp.concatenate([front * cosine - back * sine, back * cosine + front * sine], axis=-1)
    return turned.reshape(length, width)


def silu_slope(values):
    gate = jax.nn.sigmoid(values)
    return gate * (1.0 + values * (1.0 - gate))


def same_doc(doc_ids, offset):
    earlier = jnp.pad(doc_ids, (offset, 0), constant_values=-1)[: doc_ids.shape[0]]
    return (earlier == doc_ids)[:, None]


def scatter(grads):
    return lax.psum_scatter(grads.astype(bf16), AXES, scatter_dimension=0, tiled=True).astype(f32)


def gather(parts):
    return lax.all_gather(jnp.concatenate(parts, axis=1), AXES, axis=0, tiled=True)


def shards(
    tokens, segments, cotangent, w_in, w_out, w_query, w_key, w_value, w_attn_out, w_gate, w_up,
    w_down, norm_in, conv_weight, conv_bias, dt_bias, a_log, skip_gain, norm_gated, norm_mid,
):
    length = tokens.shape[1]
    blocks = length // SPAN
    conv_end = D_SSM + CONV_CH
    rows_held = w_in.shape[0]
    dt_pad = jnp.zeros((rows_held, 128 - M_HEADS), bf16)
    w_first = gather(
        (w_in[:, :D_SSM], w_query, w_key, w_value, w_in[:, D_SSM:conv_end], w_in[:, conv_end:], dt_pad)
    )
    w_second = gather((w_attn_out.T, w_out.T))
    w_third = gather((w_gate, w_up))
    w_fourth = gather((w_down.T,))

    stream = tokens[0].astype(f32)
    doc_ids = segments[0]
    cot = cotangent[0]

    inv_in = inv_norm(stream)
    normed = (stream * inv_in * norm_in).astype(bf16)
    proj = mm(normed, w_first)
    z_gate = proj[:, :D_SSM]
    q_at, k_at, v_at = D_SSM, D_SSM + HEADS * HEAD_DIM, D_SSM + (HEADS + KV_HEADS) * HEAD_DIM
    conv_at = D_SSM + QKV
    dt_at = conv_at + CONV_CH
    conv_in = proj[:, conv_at:dt_at]
    cosine, sine = angles(length)
    query = turn(proj[:, q_at:k_at], cosine, sine).astype(bf16)
    key = turn(proj[:, k_at:v_at], cosine, sine).astype(bf16)
    value = proj[:, v_at:conv_at].astype(bf16)
    doc_float = doc_ids.astype(f32)
    doc_col, doc_row = doc_float[:, None], doc_float[None, :]
    attended, lse = attend_fwd(query, key, value, doc_col, doc_row)

    taps = conv_weight.shape[0]
    convolved = conv_bias[None, :] + conv_weight[0][None, :] * conv_in
    for offset in range(1, taps):
        shifted = jnp.pad(conv_in, ((offset, 0), (0, 0)))[:length]
        convolved = convolved + jnp.where(
            same_doc(doc_ids, offset), conv_weight[offset][None, :] * shifted, 0.0
        )
    act_low = jax.nn.silu(convolved).astype(bf16)
    x_heads = act_low[:, :D_SSM]
    raw = proj[:, dt_at : dt_at + M_HEADS] + dt_bias
    step_size = jax.nn.softplus(raw)
    log_decay = -step_size * jnp.exp(a_log)
    doc_blocks = doc_float.reshape(blocks, SPAN)
    last = doc_blocks[:, -1]
    prior = jnp.concatenate([jnp.full((1,), -1.0, f32), last[:-1]])
    wide_last = jnp.repeat(last, SPAN)[:, None]
    wide_prior = jnp.repeat(prior, SPAN)[:, None]
    ld = jnp.pad(log_decay, ((0, 0), (0, 128 - M_HEADS)))
    st = jnp.concatenate(
        [step_size, jnp.zeros((length, 125 - M_HEADS), f32), wide_last, wide_prior, doc_col], axis=1
    )
    scanned, states = scan_fwd(act_low, ld, st)
    skip_wide = jnp.repeat(skip_gain, M_HDIM)[None, :]
    ssm_out = scanned + skip_wide * x_heads.astype(f32)
    mixed_in = ssm_out * jax.nn.silu(z_gate)
    inv_gated = inv_norm(mixed_in)
    gated = (mixed_in * inv_gated * norm_gated).astype(bf16)
    branches = jnp.concatenate([attended, gated], axis=1)
    resid = stream + mm_nt(branches, w_second)
    inv_mid = inv_norm(resid)
    mid_in = (resid * inv_mid * norm_mid).astype(bf16)
    both = mm(mid_in, w_third)
    hidden_units = both.shape[1] // 2
    gate, up = both[:, :hidden_units], both[:, hidden_units:]
    hidden = (jax.nn.silu(gate) * up).astype(bf16)
    mixed = (resid + mm_nt(hidden, w_fourth)).astype(bf16)

    d_hidden = mm(cot, w_fourth)
    sum_fourth = scatter(mm_tn(cot, hidden))
    d_both = jnp.concatenate(
        [(d_hidden * up * silu_slope(gate)).astype(bf16), (d_hidden * jax.nn.silu(gate)).astype(bf16)],
        axis=1,
    )
    sum_third = scatter(mm_tn(mid_in, d_both))
    d_mid = mm_nt(d_both, w_third)
    back, g_norm_mid = norm_back(d_mid, norm_mid, resid, inv_mid)
    d_resid = cot.astype(f32) + back
    d_resid_low = d_resid.astype(bf16)
    sum_second = scatter(mm_tn(d_resid_low, branches))
    d_branches = mm(d_resid_low, w_second)
    attn_width = HEADS * HEAD_DIM
    d_query, d_key, d_value = attend_bwd(
        query, key, value, d_branches[:, :attn_width], lse, doc_col, doc_row
    )
    d_mixed_in, g_norm_gated = norm_back(d_branches[:, attn_width:], norm_gated, mixed_in, inv_gated)
    d_ssm = d_mixed_in * jax.nn.silu(z_gate)
    d_first = jnp.concatenate(
        [
            (d_mixed_in * ssm_out * silu_slope(z_gate)).astype(bf16),
            turn(d_query, cosine, -sine).astype(bf16),
            turn(d_key, cosine, -sine).astype(bf16),
            d_value.astype(bf16),
        ],
        axis=1,
    )
    sum_first = scatter(mm_tn(normed, d_first))
    g_skip = jnp.sum(jnp.sum(d_ssm * x_heads.astype(f32), axis=0).reshape(M_HEADS, M_HDIM), axis=1)
    d_x, d_b, d_c, d_st, d_ld = scan_bwd(act_low, ld, st, states, d_ssm)
    d_act = jnp.concatenate([d_x + skip_wide * d_ssm, d_b, d_c], axis=1)
    d_conv = d_act * silu_slope(convolved)
    g_conv_bias = jnp.sum(d_conv, axis=0)
    d_conv_in = conv_weight[0][None, :] * d_conv
    g_taps = [jnp.sum(d_conv * conv_in, axis=0)]
    for offset in range(1, taps):
        masked = jnp.where(same_doc(doc_ids, offset), d_conv, 0.0)
        shifted = jnp.pad(conv_in, ((offset, 0), (0, 0)))[:length]
        g_taps.append(jnp.sum(masked * shifted, axis=0))
        later = jnp.pad(masked, ((0, offset), (0, 0)))[offset:]
        d_conv_in = d_conv_in + conv_weight[offset][None, :] * later
    g_conv_weight = jnp.stack(g_taps)
    d_ld = d_ld[:, :M_HEADS]
    d_step = d_st[:, :M_HEADS] - d_ld * jnp.exp(a_log)
    g_a_log = jnp.sum(d_ld * log_decay, axis=0)
    d_raw = d_step * jax.nn.sigmoid(raw)
    g_dt_bias = jnp.sum(d_raw, axis=0)
    d_last = jnp.concatenate(
        [d_conv_in.astype(bf16), jnp.pad(d_raw, ((0, 0), (0, 128 - M_HEADS))).astype(bf16)], axis=1
    )
    sum_last = scatter(mm_tn(normed, d_last))
    d_normed = mm_nt(d_first, w_first[:, :conv_at]) + mm_nt(d_last, w_first[:, conv_at:])
    back, g_norm_in = norm_back(d_normed, norm_in, stream, inv_in)
    grad_tokens = d_resid + back

    small = (
        g_norm_in, g_conv_weight, g_conv_bias, g_dt_bias, g_a_log, g_skip, g_norm_gated, g_norm_mid
    )
    flat = jnp.concatenate([member.reshape(-1) for member in small])
    flat = lax.psum(jnp.pad(flat, (0, -flat.shape[0] % 1024)).reshape(-1, 128), AXES).reshape(-1)
    totals, at = [], 0
    for member in small:
        totals.append(flat[at : at + member.size].reshape(member.shape))
        at += member.size

    g_w_in = jnp.concatenate([sum_first[:, :D_SSM], sum_last[:, : CONV_CH + M_HEADS]], axis=1)
    return (
        mixed[None],
        grad_tokens[None],
        g_w_in,
        sum_second[:, attn_width:].T,
        sum_first[:, q_at:k_at],
        sum_first[:, k_at:v_at],
        sum_first[:, v_at:],
        sum_second[:, :attn_width].T,
        sum_third[:, :hidden_units],
        sum_third[:, hidden_units:],
        sum_fourth.T,
    ) + tuple(totals)


def solution(mesh):
    rows = P(AXES, None)
    cols = P(None, AXES)
    whole = P(AXES, None, None)
    weights = (rows, cols, rows, rows, rows, cols, rows, rows, cols)
    in_specs = (whole, rows, whole) + weights + (P(),) * 8
    out_specs = (whole, whole) + weights + (P(),) * 8
    return jax.shard_map(shards, mesh=mesh, in_specs=in_specs, out_specs=out_specs, check_vma=False)
```

time: 2420 us -> 1170 us (0.48)
  local copies, waits for them, and re-layouts: 652 us -> 80.1 us
  matrix products: 591 us -> 172 us
  other arithmetic: 302 us -> 124 us
  blocking collectives: 179 us -> 40 us
  Pallas kernels: 0 us -> 90.3 us
  loops' own time: 54.8 us -> 0 us
  waiting for transfers between devices: 598 us -> 637 us
    dot_general x151 -> x14, matrix products: 569 us -> 172 us  [the longest x4 61 us: mm(): return jnp.dot(left, right, preferred_element_type=f32)]
    dynamic_update_slice x24 -> x0, local copies, waits for them, and re-layouts: 342 us -> none  [ssd_scan(): final_carry, ssm_out = lax.scan(jax.checkpoint(scan_block), start, members)]
    reduce_scatter x9 -> x4, waiting for transfers between devices: 590 us -> 439 us  [scatter(): lax.psum_scatter(grads.astype(bf16), AXES, scatter_dimension=0, tiled=True)]
    all_gather x2 -> x0, blocking collectives: 138 us -> none  [the longest x1 69.7 us: shards(): lax.all_gather(w_key, ('fsdp', 'dp'), axis=0, tiled=True)]
    all_gather x7 -> x4, waiting for transfers between devices: 3.86 us -> 139 us  [gather(): lax.all_gather(jnp.concatenate(parts, axis=1), AXES, axis=0, tiled=True)]
    pallas_call x0 -> x4, Pallas kernels: none -> 90.3 us  [the longest x1 32.1 us: scan_bwd(): pl.pallas_call(scan_bwd_kernel, grid=(blocks,), in_specs=[pl.BlockSpec((S...]
    squeeze x82 -> x0, local copies, waits for them, and re-layouts: 59.8 us -> none  [the longest x72 53.3 us: ssd_scan(): final_carry, ssm_out = lax.scan(jax.checkpoint(scan_block), start, members)]
    another operation x4 -> x0, loops' own time: 54.8 us -> none  [the longest x2 32.1 us: attention(): lax.map(jax.checkpoint(attend_block), (query_blocks, positions.reshape(bl...]
  transfers between devices with their start and end apart: 16 -> 9, of which waited for: 5 -> 7; matrix products, arithmetic and copies ran while one was open for 50% -> 21% of each run, Pallas kernels for 0% -> 5%
where the time goes in v1:
time: 1170 us; the launch traced here: 1160 us
  waiting for transfers between devices  637 us (54%)
  matrix products  172 us (15%)
  other arithmetic  124 us (11%)
  Pallas kernels  90.3 us (8%)
  local copies, waits for them, and re-layouts  80.1 us (7%)
  blocking collectives  40 us (3%)
  between operations  15.1 us (1%)
    reduce_scatter x4, waiting for transfers between devices, scatter(): lax.psum_scatter(grads.astype(bf16), AXES, scatter_dimension=0, tiled=True)  439 us
    all_gather x4, waiting for transfers between devices, gather(): lax.all_gather(jnp.concatenate(parts, axis=1), AXES, axis=0, tiled=True)  139 us
    dot_general x4, matrix products, mm(): return jnp.dot(left, right, preferred_element_type=f32)  61 us
    dot_general x5, matrix products, mm_nt(): return lax.dot_general(left, right, NT, preferred_element_type=f32)  60.4 us
    unnamed x10, waiting for transfers between devices  58.9 us
    dot_general x5, matrix products, mm_tn(): return lax.dot_general(left, right, TN, preferred_element_type=f32)  50.3 us
    unnamed x172, local copies, waits for them, and re-layouts  46.1 us
    psum x1, blocking collectives, shards(): lax.psum(jnp.pad(flat, (0, -flat.shape[0] % 1024)).reshape(-1, 128), AXES)  40 us
  transfers between devices with their start and end apart: 9, of which 7 were waited for; matrix products, arithmetic and copies ran while one was open for 21% of the time, Pallas kernels for 5%

profile of v1, /device:TPU:1, one launch (start us, length us, event | category | flops | bytes accessed | tf_op | source)
XLA Modules:
  0.0 1158.2 jit_solution(13807810068044672669)
XLA Ops:
  29.3 70.4 %all-gather.5.cloned.1.call-done = bf16[1024,4992]{1,0:T(8,128)(2,1)} async-done(((bf16[32,4992]{1,0:T(8,128)(2,1)}), bf16[1024,4992]{1,0:T(8,128)(2,1)}) %all-gather.5.cloned.1.call-update) | async-done | bytes 10223632 | tf_op jit(solution)/shard_map/all_gather | solution.py:425
  99.6 18.0 %fusion.64 = f32[1024,4992]{1,0:T(8,128)} fusion(bf16[1024,4992]{1,0:T(8,128)(2,1)} %all-gather.5.cloned.1.call-done, bf16[1,1024,1024]{1,2,0:T(8,128)(2,1)S(1)} %copy.102, f32[1024]{0:T(1024)S(1)} %copy-done.61, f32[1024]{0:T(1024)S(1)} %add_rsqrt_fusion.2), kind=kOutput, calls=%fused_computation.161 | convolution fusion | flops 10473177088 | bytes 32776192 | tf_op jit(solution)/shard_map/dot_general | solution.py:36
  149.8 18.9 %multiply_convert_fusion.3 = (bf16[1024,1792]{1,0:T(8,128)(2,1)S(1)}, f32[1024,1792]{1,0:T(8,128)}) fusion(f32[1024,1792]{1,0:T(8,128)} %slice.230, f32[1792]{0:T(1024)S(1)} %get-tuple-element.151, pred[1024]{0:T(1024)(128)(4,1)S(1)} %get-tuple-element.194, f32[1792]{0:T(1024)S(1)} %get-tuple-element.152, pred[1024]{0:T(1024)(128)(4,1)S(1)} %get-tuple-element.193, ...), kind=kLoop, calls=%fused_computation.29 | loop fusion | flops 29360128 | bytes 18388992 | tf_op jit(solution)/shard_map/convert_element_type | solution.py:471
  168.8 13.2 %shard_map.340 = (f32[1024,1536]{1,0:T(8,128)S(1)}, bf16[8,128,1536]{2,1,0:T(8,128)(2,1)S(1)}) custom-call(bf16[1024,1792]{1,0:T(8,128)(2,1)S(1)} %get-tuple-element.165.x_ref.b_ref.c_ref, bf16[1024,1792]{1,0:T(8,128)(2,1)S(1)} %get-tuple-element.165.x_ref.b_ref.c_ref, bf16[1024,1792]{1,0:T(8,128)(2,1)S(1)} %get-tuple-element.165.x_ref.b_ref.c_ref, ...), custom_call_target="tpu_custom_call" | custom-call | tf_op jit(solution)/shard_map/pallas_call | solution.py:200
  183.6 20.3 %shard_map.339 = (bf16[1024,1024]{1,0:T(8,128)(2,1)S(1)}, f32[8,1,1024]{2,1,0:T(1,128)S(1)}) custom-call(bf16[1024,1024]{1,0:T(8,128)(2,1)S(1)} %bitcast.84, bf16[1024,256]{1,0:T(8,128)(2,1)S(1)} %bitcast.86, bf16[1024,256]{1,0:T(8,128)(2,1)S(1)} %copy-done.5, f32[1024,1]{1,0:T(8,128)S(1)} %copy.103.doc_col_ref, f32[1,1024]{1,0:T(1,128)S(1)} %get-tuple-element.191.doc_row_ref), custom_call_target="tpu_custom_call" | custom-call | tf_op jit(solution)/shard_map/pallas_call | solution.py:331
  214.3 10.8 multiply_reduce_fusion.9
  225.1 21.8 %all-gather.9.cloned.1.call-done = bf16[1024,4096]{1,0:T(8,128)(2,1)} async-done(((bf16[32,4096]{1,0:T(8,128)(2,1)}), bf16[1024,4096]{1,0:T(8,128)(2,1)}) %all-gather.9.cloned.1.call-update) | async-done | bytes 8388624 | tf_op jit(solution)/shard_map/all_gather | solution.py:425
  246.9 16.4 %fusion.61 = f32[1024,4096]{1,0:T(8,128)} fusion(bf16[1024,4096]{1,0:T(8,128)(2,1)} %all-gather.9.cloned.1.call-done, f32[1024,1024]{0,1:T(8,128)} %get-tuple-element.196, f32[1024]{0:T(1024)S(1)} %copy-done.60, f32[1024]{0:T(1024)S(1)} %add_rsqrt_fusion), kind=kOutput, calls=%fused_computation.160 | convolution fusion | flops 8593080320 | bytes 29368320 | tf_op jit(solution)/shard_map/dot_general | solution.py:36
  263.3 47.1 %all-gather.11.cloned.1.call-done = bf16[1024,2048]{1,0:T(8,128)(2,1)} async-done(((bf16[32,2048]{1,0:T(8,128)(2,1)}), bf16[1024,2048]{1,0:T(8,128)(2,1)}) %all-gather.11.cloned.1.call-update) | async-done | bytes 4194320 | tf_op jit(solution)/shard_map/all_gather | solution.py:425
  310.4 14.2 %multiply_convert_fusion.1 = (bf16[1024,2048]{1,0:T(8,128)(2,1)S(1)}, bf16[1024,2048]{1,0:T(8,128)(2,1)}, bf16[1024,2048]{1,0:T(8,128)(2,1)}) fusion(f32[1024,4096]{1,0:T(8,128)} %fusion.61, bf16[1024,2048]{1,0:T(8,128)(2,1)} %all-gather.11.cloned.1.call-done, bf16[1,1024,1024]{2,1,0:T(8,128)(2,1)S(1)} %copy-done.40), kind=kOutput, calls=%fused_computation.2 | convolution fusion | flops 4326424576 | bytes 35651584 | tf_op jit(solution)/shard_map/dot_general | solution.py:36
  324.7 17.3 %multiply_reduce_fusion.7 = (f32[1024]{0:T(1024)}, f32[1024]{0:T(1024)S(1)}, f32[1024,1024]{0,1:T(8,128)}) fusion(f32[1024,1024]{0,1:T(8,128)S(1)} %copy-done.37, f32[1024]{0:T(1024)S(1)} %add_rsqrt_fusion, f32[1024]{0:T(1024)S(1)} %copy-done.60, bf16[1024,4096]{1,0:T(8,128)(2,1)} %all-gather.9.cloned.1.call-done, ...), kind=kOutput, calls=%fused_computation.67 | convolution fusion | flops 8613001216 | bytes 25182208 | tf_op jit(solution)/shard_map/dot_general | solution.py:40
  346.7 12.3 %fusion.43 = f32[1024,2560]{1,0:T(8,128)} fusion(bf16[1024,2560]{1,0:T(8,128)(2,1)} %all-gather.7.cloned.1.call-done, f32[1024,1024]{0,1:T(8,128)S(1)} %multiply_add_fusion.1), kind=kOutput, calls=%fused_computation.103 | convolution fusion | flops 5369757696 | bytes 19922944 | tf_op jit(solution)/shard_map/dot_general | solution.py:36
  363.5 12.4 %fusion.10 = (f32[1536]{0:T(1024)S(1)}, f32[1024,1536]{1,0:T(8,128)}, bf16[1024,1536]{1,0:T(8,128)(2,1)}) fusion(bf16[1024,1792]{1,0:T(8,128)(2,1)S(1)} %copy-done.1, f32[1024,4992]{1,0:T(8,128)} %fusion.64, f32[1024]{0:T(1024)S(1)} %broadcast_multiply_fusion, f32[1024,1536]{1,0:T(8,128)S(1)} %bitcast.92, f32[1536]{0:T(1024)S(1)} %copy-done.52, ...), kind=kLoop, calls=%fused_computation.33 | loop fusion | flops 34601472 | bytes 37775360 | tf_op jit(solution)/shard_map/reduce_sum | solution.py:530
  376.0 32.1 %shard_map.342 = (f32[1024,1536]{1,0:T(8,128)}, f32[1024,128]{1,0:T(8,128)S(1)}, f32[1024,128]{1,0:T(8,128)S(1)}, f32[1024,128]{1,0:T(8,128)S(1)}, f32[1024,128]{1,0:T(8,128)S(1)}) custom-call(bf16[1024,1792]{1,0:T(8,128)(2,1)S(1)} %copy-done.1, bf16[1024,1792]{1,0:T(8,128)(2,1)S(1)} %copy-done.1, bf16[1024,1792]{1,0:T(8,128)(2,1)S(1)} %copy-done.1, ...), custom_call_target="tpu_custom_call" | custom-call | tf_op jit(solution)/shard_map/pallas_call | solution.py:227
  415.2 11.6 %fusion.66 = (f32[1792]{0:T(1024)S(1)}, f32[1792]{0:T(1024)S(1)}, f32[1024,1792]{1,0:T(8,128)}) fusion(f32[1024,4992]{1,0:T(8,128)} %fusion.64, f32[1024,1792]{1,0:T(8,128)} %get-tuple-element.166, f32[1024,128]{1,0:T(8,128)S(1)} %get-tuple-element.40, f32[1024,128]{1,0:T(8,128)S(1)} %get-tuple-element.39, f32[1024,1536]{1,0:T(8,128)} %multiply_add_fusion), kind=kLoop, calls=%fused_computation.162 | loop fusion | flops 23851520 | bytes 29374464 | tf_op jit(solution)/shard_map/reduce_sum | solution.py:534
  427.0 12.6 %multiply_reduce_fusion.2 = (f32[1792]{0:T(1024)S(1)}, f32[1792]{0:T(1024)S(1)}, f32[1792]{0:T(1024)S(1)}, f32[1024,1792]{1,0:T(8,128)}, f32[1024,1792]{1,0:T(8,128)}, /*index=5*/f32[1024,1792]{1,0:T(8,128)}) fusion(f32[1024,1792]{1,0:T(8,128)S(1)} %bitcast.94, f32[1024,1792]{1,0:T(8,128)} %get-tuple-element.157, pred[1024]{0:T(1024)(128)(4,1)S(1)} %get-tuple-element.194, ...), kind=kLoop, calls=%fused_computation.27 | loop fusion | flops 16509696 | bytes 36724736 | tf_op jit(solution)/shard_map/reduce_sum | solution.py:540
  476.9 24.7 %shard_map.341 = (f32[1024,1024]{1,0:T(8,128)S(1)}, f32[1024,256]{1,0:T(8,128)S(1)}, f32[1024,256]{1,0:T(8,128)S(1)}) custom-call(bf16[1024,1024]{1,0:T(8,128)(2,1)S(1)} %bitcast.85, bf16[1024,256]{1,0:T(8,128)(2,1)S(1)} %bitcast.87, bf16[1024,256]{1,0:T(8,128)(2,1)S(1)} %copy-done.6, f32[1024,1024]{1,0:T(8,128)S(1)} %slice.237.do_ref, ...), custom_call_target="tpu_custom_call" | custom-call | tf_op jit(solution)/shard_map/pallas_call | solution.py:360
  535.9 15.9 %convolution_convert_fusion = bf16[1024,4096]{1,0:T(8,128)(2,1)} fusion(bf16[1024,2048]{1,0:T(8,128)(2,1)} %get-tuple-element.169, bf16[1024,2048]{1,0:T(8,128)(2,1)} %copy-done.69, f32[1024,1024]{0,1:T(8,128)} %get-tuple-element.196, f32[1024]{0:T(1024)S(1)} %copy-done.60, f32[1024]{0:T(1024)S(1)} %add_rsqrt_fusion), kind=kOutput, calls=%fused_computation.10 | convolution fusion | flops 8614051840 | bytes 20979712 | tf_op jit(solution)/shard_map/dot_general | solution.py:44
  562.0 13.1 %fusion.25 = (f32[1024]{0:T(1024)S(1)}, f32[1024]{0:T(1024)S(1)}, f32[1024,1024]{0,1:T(8,128)}) fusion(bf16[1,1024,1024]{1,2,0:T(8,128)(2,1)S(1)} %copy-done.29, f32[1024]{0:T(1024)S(1)} %copy-done.57, f32[1024]{0:T(1024)S(1)} %copy-done.62, f32[1024,1024]{0,1:T(8,128)} %fusion.29, bf16[1024,4992]{1,0:T(8,128)(2,1)} %all-gather.5.cloned.1.call-done, ...), kind=kOutput, calls=%fused_computation.64 | convolution fusion | flops 6476003328 | bytes 23085056 | tf_op jit(solution)/shard_map/dot_general | solution.py:40
  575.3 40.0 %psum.7 = f32[104,128]{1,0:T(8,128)S(1)} all-reduce(f32[104,128]{1,0:T(8,128)S(1)} %pad_bitcast_fusion), channel_id=1, replica_groups=mesh['fsdp'=16,'dp'=2] {'fsdp','dp'}, use_global_device_ids=true, to_apply=%region_23.24 | all-reduce | flops 13312 | bytes 106496 | tf_op jit(solution)/shard_map/psum | solution.py:561
  643.6 58.2 %reduce-scatter.16.cloned.1.call-done = bf16[32,2048]{1,0:T(8,128)(2,1)} async-done(((bf16[1024,2048]{1,0:T(8,128)(2,1)}), bf16[32,2048]{1,0:T(8,128)(2,1)}) %reduce-scatter.16.cloned.1.call-update) | async-done | bytes 131088
  704.1 115.2 %reduce-scatter.8.cloned.1.call-done = bf16[32,3072]{1,0:T(8,128)(2,1)} async-done(((bf16[1024,3072]{1,0:T(8,128)(2,1)}), bf16[32,3072]{1,0:T(8,128)(2,1)}) %reduce-scatter.8.cloned.1.call-update) | async-done | bytes 196624 | tf_op jit(solution)/shard_map/reduce_scatter | solution.py:421
  823.9 140.8 %reduce-scatter.12.cloned.1.call-done = bf16[32,2560]{1,0:T(8,128)(2,1)} async-done(((bf16[1024,2560]{1,0:T(8,128)(2,1)}), bf16[32,2560]{1,0:T(8,128)(2,1)}) %reduce-scatter.12.cloned.1.call-update) | async-done | bytes 163856 | tf_op jit(solution)/shard_map/reduce_scatter | solution.py:421
  967.0 182.7 %reduce-scatter.14.cloned.1.call-done = bf16[32,4096]{1,0:T(8,128)(2,1)} async-done(((bf16[1024,4096]{1,0:T(8,128)(2,1)}), bf16[32,4096]{1,0:T(8,128)(2,1)}) %reduce-scatter.14.cloned.1.call-update) | async-done | bytes 262160 | tf_op jit(solution)/shard_map/reduce_scatter | solution.py:421
  (287 shorter events, 202.9 us)
Async XLA Ops:
  7.2 92.4 %all-gather.5.cloned.1.call-start = ((), (), s32[]{:S(2)}) async-start(), calls=%async_computation.5 | async-start | bytes 10543104 | tf_op jit(solution)/shard_map/all_gather | solution.py:425
  10.8 203.4 %all-gather.7.cloned.1.call-start = ((), (), s32[]{:S(2)}) async-start(), calls=%async_computation.6 | async-start | bytes 5406720 | tf_op jit(solution)/shard_map/all_gather | solution.py:425
  12.5 234.4 %all-gather.9.cloned.1.call-start = ((), (), s32[]{:S(2)}) async-start(), calls=%async_computation.7 | async-start | bytes 8650752 | tf_op jit(solution)/shard_map/all_gather | solution.py:425
  14.2 296.2 %all-gather.11.cloned.1.call-start = ((), (), s32[]{:S(2)}) async-start(), calls=%async_computation.8 | async-start | bytes 4325376 | tf_op jit(solution)/shard_map/all_gather | solution.py:425
  14.8 627.9 %reduce-scatter.10.cloned.1.call-start = ((), (), s32[]{:S(2)}) async-start(), calls=%async_computation.10 | async-start | bytes 4055040 | tf_op jit(solution)/shard_map/reduce_scatter | solution.py:421
  18.6 99.1 %copy-start.26 = (bf16[1,1024,1024]{1,2,0:T(8,128)(2,1)}, bf16[1,1024,1024]{1,2,0:T(8,128)(2,1)S(1)}, u32[]{:S(2)}) copy-start(bf16[1,1024,1024]{1,2,0:T(8,128)(2,1)S(1)} %copy.102) | copy-start | bytes 6291460
  18.6 81.0 %copy-start.61 = (f32[1024]{0:T(1024)S(1)}, f32[1024]{0:T(1024)}, u32[]{:S(2)}) copy-start(f32[1024]{0:T(1024)} %param.32) | copy-start | bytes 12292
  19.1 98.5 %copy-start.56 = (f32[1024]{0:T(1024)}, f32[1024]{0:T(1024)S(1)}, u32[]{:S(2)}) copy-start(f32[1024]{0:T(1024)S(1)} %add_rsqrt_fusion.2) | copy-start | bytes 12292
  19.2 130.5 %copy-start.44 = (f32[1792]{0:T(1024)}, f32[1792]{0:T(1024)S(1)}, u32[]{:S(2)}) copy-start(f32[1792]{0:T(1024)S(1)} %get-tuple-element.149) | copy-start | bytes 21508
  19.2 130.5 %copy-start.46 = (f32[1792]{0:T(1024)}, f32[1792]{0:T(1024)S(1)}, u32[]{:S(2)}) copy-start(f32[1792]{0:T(1024)S(1)} %get-tuple-element.150) | copy-start | bytes 21508
  19.2 130.5 %copy-start.48 = (f32[1792]{0:T(1024)}, f32[1792]{0:T(1024)S(1)}, u32[]{:S(2)}) copy-start(f32[1792]{0:T(1024)S(1)} %get-tuple-element.151) | copy-start | bytes 21508
  19.2 130.5 %copy-start.50 = (f32[1792]{0:T(1024)}, f32[1792]{0:T(1024)S(1)}, u32[]{:S(2)}) copy-start(f32[1792]{0:T(1024)S(1)} %get-tuple-element.152) | copy-start | bytes 21508
  19.3 125.7 %copy-start.65 = (f32[24]{0:T(128)}, f32[24]{0:T(128)S(1)}, u32[]{:S(2)}) copy-start(f32[24]{0:T(128)S(1)} %exp.30) | copy-start | bytes 292
  29.3 110.2 %copy-start.30 = (f32[1024,64]{1,0:T(8,128)}, f32[1024,64]{1,0:T(8,128)S(1)}, u32[]{:S(2)}) copy-start(f32[1024,64]{1,0:T(8,128)S(1)} %get-tuple-element.189) | copy-start | bytes 786436
  168.7 35.3 %copy-start = (bf16[1024,1792]{1,0:T(8,128)(2,1)}, bf16[1024,1792]{1,0:T(8,128)(2,1)S(1)}, u32[]{:S(2)}) copy-start(bf16[1024,1792]{1,0:T(8,128)(2,1)S(1)} %get-tuple-element.165.x_ref.b_ref.c_ref) | copy-start | bytes 11010052
  183.6 25.5 %copy-start.2 = (f32[1024,1536]{1,0:T(8,128)}, f32[1024,1536]{1,0:T(8,128)S(1)}, u32[]{:S(2)}) copy-start(f32[1024,1536]{1,0:T(8,128)S(1)} %get-tuple-element.32) | copy-start | bytes 18874372
  214.3 32.6 %copy-start.60 = (f32[1024]{0:T(1024)S(1)}, f32[1024]{0:T(1024)}, u32[]{:S(2)}) copy-start(f32[1024]{0:T(1024)} %param.39) | copy-start | bytes 12292
  246.9 63.6 %copy-start.40 = (bf16[1,1024,1024]{2,1,0:T(8,128)(2,1)S(1)}, bf16[1,1024,1024]{2,1,0:T(8,128)(2,1)}, u32[]{:S(2)}) copy-start(bf16[1,1024,1024]{2,1,0:T(8,128)(2,1)} %param.22) | copy-start | bytes 6291460
  342.0 21.5 %slice-start = ((s8[6291456]{0:T(1024)(128)(4,1)}), s8[2097152]{0:T(1024)(128)(4,1)S(1)}, s32[]{:S(2)}) async-start(s8[6291456]{0:T(1024)(128)(4,1)} %bitcast.82), calls=%async_computation.14 | async-start | bytes 4194304
  376.0 32.1 %copy-start.24 = (f32[1024,1536]{1,0:T(8,128)S(1)}, f32[1024,1536]{1,0:T(8,128)}, u32[]{:S(2)}) copy-start(f32[1024,1536]{1,0:T(8,128)} %get-tuple-element.154.dy_ref) | copy-start | bytes 18874372
  458.6 243.3 %reduce-scatter.16.cloned.1.call-start = ((), (), s32[]{:S(2)}) async-start(), calls=%async_computation.13 | async-start | bytes 4325376
  473.6 345.7 %reduce-scatter.8.cloned.1.call-start = ((), (), s32[]{:S(2)}) async-start(), calls=%async_computation.9 | async-start | bytes 6488064 | tf_op jit(solution)/shard_map/reduce_scatter | solution.py:421
  524.4 440.2 %reduce-scatter.12.cloned.1.call-start = ((), (), s32[]{:S(2)}) async-start(), calls=%async_computation.11 | async-start | bytes 5406720 | tf_op jit(solution)/shard_map/reduce_scatter | solution.py:421
  535.8 613.8 %reduce-scatter.14.cloned.1.call-start = ((), (), s32[]{:S(2)}) async-start(), calls=%async_computation.12 | async-start | bytes 8650752 | tf_op jit(solution)/shard_map/reduce_scatter | solution.py:421
  (64 other events, 623.1 us)
Sparse Core Ops, SparseCore 0:
  11.5 88.0 all-gather.4
  103.0 63.8 all-gather.6
  170.5 76.3 all-gather.8
  249.7 60.6 all-gather.10
  458.7 100.6 reduce-scatter.9
  561.5 140.3 reduce-scatter.15
  707.5 111.7 reduce-scatter.7
  821.7 142.9 reduce-scatter.11
  967.1 182.5 reduce-scatter.13

commit v2 on v1

--- a/solution.py
+++ b/solution.py
@@ -417,8 +417,74 @@
     return (earlier == doc_ids)[:, None]
 
 
+def flip(values, bit):
+    places = lax.axis_size(AXES)
+    return lax.ppermute(values, AXES, [(i, i ^ bit) for i in range(places)])
+
+
+def add(left, right):
+    return (left.astype(f32) + right.astype(f32)).astype(bf16)
+
+
+def at(values, index, axis):
+    return lax.dynamic_index_in_dim(values, index, axis, keepdims=False)
+
+
 def scatter(grads):
-    return lax.psum_scatter(grads.astype(bf16), AXES, scatter_dimension=0, tiled=True).astype(f32)
+    dp = lax.axis_size("dp")
+    chips = lax.axis_size("fsdp") // 2
+    if dp != 2 or chips < 4:
+        return lax.psum_scatter(grads, AXES, scatter_dimension=0, tiled=True).astype(f32)
+    rows, width = grads.shape
+    held = rows // (4 * chips)
+    place = lax.axis_index("fsdp")
+    core, y, z, x = place % 2, (place // 2) % 2, place // 4, lax.axis_index("dp")
+    blocks = grads.reshape(chips, 2, 2 * held, width)
+    shape = (chips // 2, 2, 2, held, width)
+    own = at(blocks, core, 1).reshape(shape)
+    other = flip(at(blocks, 1 - core, 1), 2).reshape(shape)
+
+    def pick(row, col):
+        zero = jnp.zeros((), place.dtype)
+        start, size = (zero, row, col, zero, zero), (chips // 2, 1, 1, held, width)
+        return add(lax.dynamic_slice(own, start, size), lax.dynamic_slice(other, start, size))[:, 0, 0]
+
+    def along(first):
+        return jnp.stack(
+            [
+                pick(jnp.where(core == 0, second, first), jnp.where(core == 0, first, second))
+                for second in jnp.arange(2, dtype=place.dtype)
+            ]
+        )
+
+    near = jnp.where(core == 0, x, y)
+    far = jnp.where(core == 0, y, x)
+    places = 4 * chips
+    crossing = [(i, i ^ (4 if i & 2 else 1)) for i in range(places)]
+    back = [(i, i ^ (1 if i & 2 else 4)) for i in range(places)]
+    sent, own = along(1 - near), along(near)
+    other = lax.ppermute(sent, AXES, crossing)
+    sent = add(at(own, 1 - far, 0), at(other, 1 - far, 0))
+    own = add(at(own, far, 0), at(other, far, 0))
+    other = lax.ppermute(sent, AXES, back)
+    level = 1
+    while level < chips // 2:
+        shape = (-1, 2, held, width)
+        mine = (z // level) % 2
+        own, other = own.reshape(shape), other.reshape(shape)
+        sent = add(at(own, 1 - mine, 1), at(other, 1 - mine, 1))
+        own = add(at(own, mine, 1), at(other, mine, 1))
+        other = flip(sent, 8 * level)
+        level *= 2
+    return (own.astype(f32) + other.astype(f32)).reshape(held, width)
+
+
+def sum_everywhere(values):
+    bit = 1
+    while bit < lax.axis_size(AXES):
+        values = values + flip(values, bit)
+        bit *= 2
+    return values
 
 
 def gather(parts):
@@ -499,17 +565,17 @@
     mixed = (resid + mm_nt(hidden, w_fourth)).astype(bf16)
 
     d_hidden = mm(cot, w_fourth)
-    sum_fourth = scatter(mm_tn(cot, hidden))
+    sum_fourth = scatter(mm_tn(cot, hidden).astype(bf16))
     d_both = jnp.concatenate(
         [(d_hidden * up * silu_slope(gate)).astype(bf16), (d_hidden * jax.nn.silu(gate)).astype(bf16)],
         axis=1,
     )
-    sum_third = scatter(mm_tn(mid_in, d_both))
+    sum_third = scatter(mm_tn(mid_in, d_both).astype(bf16))
     d_mid = mm_nt(d_both, w_third)
     back, g_norm_mid = norm_back(d_mid, norm_mid, resid, inv_mid)
     d_resid = cot.astype(f32) + back
     d_resid_low = d_resid.astype(bf16)
-    sum_second = scatter(mm_tn(d_resid_low, branches))
+    sum_second = scatter(mm_tn(d_resid_low, branches).astype(bf16))
     d_branches = mm(d_resid_low, w_second)
     attn_width = HEADS * HEAD_DIM
     d_query, d_key, d_value = attend_bwd(
@@ -526,7 +592,7 @@
         ],
         axis=1,
     )
-    sum_first = scatter(mm_tn(normed, d_first))
+    sum_first = scatter(mm_tn(normed, d_first).astype(bf16))
     g_skip = jnp.sum(jnp.sum(d_ssm * x_heads.astype(f32), axis=0).reshape(M_HEADS, M_HDIM), axis=1)
     d_x, d_b, d_c, d_st, d_ld = scan_bwd(act_low, ld, st, states, d_ssm)
     d_act = jnp.concatenate([d_x + skip_wide * d_ssm, d_b, d_c], axis=1)
@@ -549,7 +615,7 @@
     d_last = jnp.concatenate(
         [d_conv_in.astype(bf16), jnp.pad(d_raw, ((0, 0), (0, 128 - M_HEADS))).astype(bf16)], axis=1
     )
-    sum_last = scatter(mm_tn(normed, d_last))
+    sum_last = scatter(mm_tn(normed, d_last).astype(bf16))
     d_normed = mm_nt(d_first, w_first[:, :conv_at]) + mm_nt(d_last, w_first[:, conv_at:])
     back, g_norm_in = norm_back(d_normed, norm_in, stream, inv_in)
     grad_tokens = d_resid + back
@@ -558,7 +624,7 @@
         g_norm_in, g_conv_weight, g_conv_bias, g_dt_bias, g_a_log, g_skip, g_norm_gated, g_norm_mid
     )
     flat = jnp.concatenate([member.reshape(-1) for member in small])
-    flat = lax.psum(jnp.pad(flat, (0, -flat.shape[0] % 1024)).reshape(-1, 128), AXES).reshape(-1)
+    flat = sum_everywhere(jnp.pad(flat, (0, -flat.shape[0] % 1024)).reshape(-1, 128)).reshape(-1)
     totals, at = [], 0
     for member in small:
         totals.append(flat[at : at + member.size].reshape(member.shape))

time: 1170 us -> 782 us (0.67)
  waiting for transfers between devices: 637 us -> 236 us
  blocking collectives: 40 us -> 0 us
  starting transfers between devices: 0.37 us -> 28.7 us
  other arithmetic: 124 us -> 140 us
    reduce_scatter x4 -> x0, waiting for transfers between devices: 439 us -> none  [scatter(): lax.psum_scatter(grads.astype(bf16), AXES, scatter_dimension=0, tiled=True)]
    ppermute x0 -> x30, waiting for transfers between devices: none -> 102 us  [the longest x20 50.5 us: flip(): return lax.ppermute(values, AXES, [(i, i ^ bit) for i in range(places)])]
    unnamed x10 -> x4, waiting for transfers between devices: 58.9 us -> 0.56 us
    psum x1 -> x0, blocking collectives: 40 us -> none  [shards(): lax.psum(jnp.pad(flat, (0, -flat.shape[0] % 1024)).reshape(-1, 128), AXES)]
    ppermute x0 -> x30, starting transfers between devices: none -> 28.5 us  [the longest x20 21 us: flip(): return lax.ppermute(values, AXES, [(i, i ^ bit) for i in range(places)])]
    another operation x4 -> x19, other arithmetic: 10.3 us -> 29.2 us  [the longest x15 19 us: along(): jnp.stack([pick(jnp.where(core == 0, second, first), jnp.where(core == 0,...]
    dynamic_slice x0 -> x5, local copies, waits for them, and re-layouts: none -> 16.7 us  [at(): return lax.dynamic_index_in_dim(values, index, axis, keepdims=False)]
    unnamed x172 -> x205, local copies, waits for them, and re-layouts: 46.1 us -> 44.1 us
  transfers between devices with their start and end apart: 9 -> 34, of which waited for: 7 -> 19; matrix products, arithmetic and copies ran while one was open for 21% -> 25% of each run, Pallas kernels for 5% -> 4%
where the time goes in v2:
time: 782 us; the launch traced here: 771 us
  waiting for transfers between devices  236 us (30%)
  matrix products  164 us (21%)
  other arithmetic  140 us (18%)
  local copies, waits for them, and re-layouts  91.3 us (12%)
  Pallas kernels  90.4 us (12%)
  starting transfers between devices  28.7 us (4%)
  between operations  20.7 us (3%)
    all_gather x4, waiting for transfers between devices, gather(): lax.all_gather(jnp.concatenate(parts, axis=1), AXES, axis=0, tiled=True)  133 us
    dot_general x4, matrix products, mm(): return jnp.dot(left, right, preferred_element_type=f32)  60.2 us
    dot_general x5, matrix products, mm_nt(): return lax.dot_general(left, right, NT, preferred_element_type=f32)  54.6 us
    ppermute x20, waiting for transfers between devices, flip(): return lax.ppermute(values, AXES, [(i, i ^ bit) for i in range(places)])  50.5 us
    dot_general x5, matrix products, mm_tn(): return lax.dot_general(left, right, TN, preferred_element_type=f32)  49.3 us
    unnamed x205, local copies, waits for them, and re-layouts  44.1 us
    ppermute x5, waiting for transfers between devices, scatter(): other = lax.ppermute(sent, AXES, crossing)  36.2 us
    pallas_call x1, Pallas kernels, scan_bwd(): pl.pallas_call(scan_bwd_kernel, grid=(blocks,), in_specs=[pl.BlockSpec((S...  31.8 us
  transfers between devices with their start and end apart: 34, of which 19 were waited for; matrix products, arithmetic and copies ran while one was open for 25% of the time, Pallas kernels for 4%

profile of v2, /device:TPU:1, one launch (start us, length us, event | category | flops | bytes accessed | tf_op | source)
XLA Modules:
  0.0 770.6 jit_solution(2984720633463451583)
XLA Ops:
  35.1 64.5 %all-gather.5.cloned.1.call-done = bf16[1024,4992]{1,0:T(8,128)(2,1)} async-done(((bf16[32,4992]{1,0:T(8,128)(2,1)}), bf16[1024,4992]{1,0:T(8,128)(2,1)}) %all-gather.5.cloned.1.call-update) | async-done | bytes 10223632 | tf_op jit(solution)/shard_map/all_gather | solution.py:491
  99.6 18.1 %fusion.115 = f32[1024,4992]{1,0:T(8,128)} fusion(bf16[1024,4992]{1,0:T(8,128)(2,1)} %all-gather.5.cloned.1.call-done, bf16[1,1024,1024]{1,2,0:T(8,128)(2,1)S(1)} %copy.152, f32[1024]{0:T(1024)S(1)} %copy-done.76, f32[1024]{0:T(1024)S(1)} %add_rsqrt_fusion.2), kind=kOutput, calls=%fused_computation.300 | convolution fusion | flops 10473177088 | bytes 32776192 | tf_op jit(solution)/shard_map/dot_general | solution.py:36
  149.7 19.0 %multiply_convert_fusion.3 = (bf16[1024,1792]{1,0:T(8,128)(2,1)S(1)}, f32[1024,1792]{1,0:T(8,128)}) fusion(f32[1024,1792]{1,0:T(8,128)} %slice.226, f32[1792]{0:T(1024)S(1)} %get-tuple-element.132, pred[1024]{0:T(1024)(128)(4,1)S(1)} %get-tuple-element.220, f32[1792]{0:T(1024)S(1)} %get-tuple-element.133, pred[1024]{0:T(1024)(128)(4,1)S(1)} %get-tuple-element.219, ...), kind=kLoop, calls=%fused_computation.29 | loop fusion | flops 29360128 | bytes 18388992 | tf_op jit(solution)/shard_map/convert_element_type | solution.py:537
  168.7 13.2 %shard_map.340 = (f32[1024,1536]{1,0:T(8,128)S(1)}, bf16[8,128,1536]{2,1,0:T(8,128)(2,1)S(1)}) custom-call(bf16[1024,1792]{1,0:T(8,128)(2,1)S(1)} %get-tuple-element.146.x_ref.b_ref.c_ref, bf16[1024,1792]{1,0:T(8,128)(2,1)S(1)} %get-tuple-element.146.x_ref.b_ref.c_ref, bf16[1024,1792]{1,0:T(8,128)(2,1)S(1)} %get-tuple-element.146.x_ref.b_ref.c_ref, ...), custom_call_target="tpu_custom_call" | custom-call | tf_op jit(solution)/shard_map/pallas_call | solution.py:200
  183.6 20.6 %shard_map.339 = (bf16[1024,1024]{1,0:T(8,128)(2,1)S(1)}, f32[8,1,1024]{2,1,0:T(1,128)S(1)}) custom-call(bf16[1024,1024]{1,0:T(8,128)(2,1)S(1)} %bitcast.295, bf16[1024,256]{1,0:T(8,128)(2,1)S(1)} %bitcast.297, bf16[1024,256]{1,0:T(8,128)(2,1)S(1)} %copy-done.6, f32[1024,1]{1,0:T(8,128)S(1)} %copy.153.doc_col_ref, f32[1,1024]{1,0:T(1,128)S(1)} %get-tuple-element.217.doc_row_ref), custom_call_target="tpu_custom_call" | custom-call | tf_op jit(solution)/shard_map/pallas_call | solution.py:331
  214.4 10.8 %multiply_reduce_fusion.9 = (f32[1024]{0:T(1024)S(1)}, f32[1024,1024]{0,1:T(8,128)}) fusion(bf16[1024,2560]{1,0:T(8,128)(2,1)} %all-gather.7.cloned.1.call-done, bf16[1024,1536]{1,0:T(8,128)(2,1)} %multiply_convert_fusion.5, bf16[1024,1024]{1,0:T(8,128)(2,1)S(1)} %copy-done.25, bf16[1,1024,1024]{1,2,0:T(8,128)(2,1)} %copy-done.32), kind=kOutput, calls=%fused_computation.75 | convolution fusion | flops 5383388160 | bytes 16781312 | tf_op jit(solution)/shard_map/dot_general | solution.py:40
  225.2 21.7 %all-gather.9.cloned.1.call-done = bf16[1024,4096]{1,0:T(8,128)(2,1)} async-done(((bf16[32,4096]{1,0:T(8,128)(2,1)}), bf16[1024,4096]{1,0:T(8,128)(2,1)}) %all-gather.9.cloned.1.call-update) | async-done | bytes 8388624 | tf_op jit(solution)/shard_map/all_gather | solution.py:491
  246.9 16.3 %fusion.112 = f32[1024,4096]{1,0:T(8,128)} fusion(bf16[1024,4096]{1,0:T(8,128)(2,1)} %all-gather.9.cloned.1.call-done, f32[1024,1024]{0,1:T(8,128)} %get-tuple-element.224, f32[1024]{0:T(1024)S(1)} %copy-done.75, f32[1024]{0:T(1024)S(1)} %add_rsqrt_fusion), kind=kOutput, calls=%fused_computation.299 | convolution fusion | flops 8593080320 | bytes 29368320 | tf_op jit(solution)/shard_map/dot_general | solution.py:36
  263.2 47.2 %all-gather.11.cloned.1.call-done = bf16[1024,2048]{1,0:T(8,128)(2,1)} async-done(((bf16[32,2048]{1,0:T(8,128)(2,1)}), bf16[1024,2048]{1,0:T(8,128)(2,1)}) %all-gather.11.cloned.1.call-update) | async-done | bytes 4194320 | tf_op jit(solution)/shard_map/all_gather | solution.py:491
  310.4 16.3 %multiply_convert_fusion.1 = (bf16[1024,2048]{1,0:T(8,128)(2,1)}, bf16[1024,2048]{1,0:T(8,128)(2,1)}, bf16[1024,2048]{1,0:T(8,128)(2,1)}) fusion(f32[1024,4096]{1,0:T(8,128)} %fusion.112, bf16[1024,2048]{1,0:T(8,128)(2,1)} %all-gather.11.cloned.1.call-done, bf16[1,1024,1024]{2,1,0:T(8,128)(2,1)} %param.22), kind=kOutput, calls=%fused_computation.2 | convolution fusion | flops 4326424576 | bytes 35651584 | tf_op jit(solution)/shard_map/dot_general | solution.py:36
  326.8 16.3 %multiply_reduce_fusion.7 = (f32[1024]{0:T(1024)}, f32[1024]{0:T(1024)S(1)}, f32[1024,1024]{0,1:T(8,128)}) fusion(f32[1024,1024]{0,1:T(8,128)S(1)} %copy-done.44, f32[1024]{0:T(1024)S(1)} %add_rsqrt_fusion, f32[1024]{0:T(1024)S(1)} %copy-done.75, bf16[1024,4096]{1,0:T(8,128)(2,1)} %all-gather.9.cloned.1.call-done, ...), kind=kOutput, calls=%fused_computation.67 | convolution fusion | flops 8613001216 | bytes 25182208 | tf_op jit(solution)/shard_map/dot_general | solution.py:40
  362.4 15.8 %convolution_convert_fusion = bf16[1024,4096]{1,0:T(8,128)(2,1)} fusion(bf16[1024,2048]{1,0:T(8,128)(2,1)} %get-tuple-element.150, bf16[1024,2048]{1,0:T(8,128)(2,1)} %get-tuple-element.149, f32[1024,1024]{0,1:T(8,128)} %get-tuple-element.224, f32[1024]{0:T(1024)S(1)} %copy-done.75, f32[1024]{0:T(1024)S(1)} %add_rsqrt_fusion), kind=kOutput, calls=%fused_computation.10 | convolution fusion | flops 8614051840 | bytes 20979712 | tf_op jit(solution)/shard_map/dot_general | solution.py:44
  378.2 10.0 %convolution_convert_fusion.1 = bf16[1024,2560]{1,0:T(8,128)(2,1)} fusion(bf16[1024,1536]{1,0:T(8,128)(2,1)S(1)} %copy-done.48, bf16[1024,1024]{1,0:T(8,128)(2,1)S(1)} %copy-done.25, f32[1024,1024]{0,1:T(8,128)} %copy-done.30), kind=kOutput, calls=%fused_computation.54 | convolution fusion | flops 5382864896 | bytes 14680064 | tf_op jit(solution)/shard_map/dot_general | solution.py:44
  388.2 13.6 %fusion.10 = (f32[1536]{0:T(1024)S(1)}, f32[1024,1536]{1,0:T(8,128)}, bf16[1024,1536]{1,0:T(8,128)(2,1)}) fusion(bf16[1024,1792]{1,0:T(8,128)(2,1)S(1)} %copy-done.1, f32[1024,4992]{1,0:T(8,128)} %fusion.115, f32[1024]{0:T(1024)S(1)} %broadcast_multiply_fusion, f32[1024,1536]{1,0:T(8,128)} %copy-done.26, f32[1536]{0:T(1024)S(1)} %copy-done.62, ...), kind=kLoop, calls=%fused_computation.33 | loop fusion | flops 34601472 | bytes 37775360 | tf_op jit(solution)/shard_map/reduce_sum | solution.py:596
  401.8 31.8 %shard_map.342 = (f32[1024,1536]{1,0:T(8,128)}, f32[1024,128]{1,0:T(8,128)S(1)}, f32[1024,128]{1,0:T(8,128)S(1)}, f32[1024,128]{1,0:T(8,128)S(1)}, f32[1024,128]{1,0:T(8,128)S(1)}) custom-call(bf16[1024,1792]{1,0:T(8,128)(2,1)S(1)} %copy-done.1, bf16[1024,1792]{1,0:T(8,128)(2,1)S(1)} %copy-done.1, bf16[1024,1792]{1,0:T(8,128)(2,1)S(1)} %copy-done.1, ...), custom_call_target="tpu_custom_call" | custom-call | tf_op jit(solution)/shard_map/pallas_call | solution.py:227
  465.8 24.8 %shard_map.341 = (f32[1024,1024]{1,0:T(8,128)S(1)}, f32[1024,256]{1,0:T(8,128)S(1)}, f32[1024,256]{1,0:T(8,128)S(1)}) custom-call(bf16[1024,1024]{1,0:T(8,128)(2,1)S(1)} %bitcast.296, bf16[1024,256]{1,0:T(8,128)(2,1)S(1)} %bitcast.298, bf16[1024,256]{1,0:T(8,128)(2,1)S(1)} %copy-done.7, f32[1024,1024]{1,0:T(8,128)S(1)} %copy-done.5, ...), custom_call_target="tpu_custom_call" | custom-call | tf_op jit(solution)/shard_map/pallas_call | solution.py:360
  506.1 11.2 %fusion.6 = bf16[1024,1792]{1,0:T(8,128)(2,1)S(1)} fusion(f32[1024,1792]{1,0:T(8,128)} %get-tuple-element.141, f32[1024,1792]{1,0:T(8,128)} %get-tuple-element.140, f32[1024,1792]{1,0:T(8,128)} %get-tuple-element.139, f32[1024,1792]{1,0:T(8,128)} %copy-done.28, f32[1792]{0:T(1024)S(1)} %copy-done.59, f32[1792]{0:T(1024)S(1)} %copy-done.61, ...), kind=kLoop, calls=%fused_computation.21 | loop fusion | flops 14680064 | bytes 33058816 | tf_op jit(solution)/shard_map/convert_element_type | solution.py:616
  523.5 9.8 %convolution_convert_fusion.2 = bf16[1024,3072]{1,0:T(8,128)(2,1)} fusion(bf16[1024,256]{1,0:T(8,128)(2,1)S(1)} %convert_element_type.865, bf16[1024,256]{1,0:T(8,128)(2,1)S(1)} %bitcast.342, bf16[1024,1024]{1,0:T(8,128)(2,1)S(1)} %bitcast.335, bf16[1024,1536]{1,0:T(8,128)(2,1)S(1)} %copy-done.49, bf16[1,1024,1024]{1,2,0:T(8,128)(2,1)S(1)} %copy-done.33, ...), kind=kOutput, calls=%fused_computation.55 | convolution fusion | flops 6474956800 | bytes 14688256 | tf_op jit(solution)/shard_map/dot_general | solution.py:44
  541.5 13.5 %fusion.25 = (f32[1024]{0:T(1024)S(1)}, f32[1024]{0:T(1024)S(1)}, f32[1024,1024]{0,1:T(8,128)}) fusion(bf16[1,1024,1024]{1,2,0:T(8,128)(2,1)S(1)} %copy-done.33, f32[1024]{0:T(1024)S(1)} %copy-done.66, f32[1024]{0:T(1024)S(1)} %copy-done.77, f32[1024,1024]{0,1:T(8,128)} %fusion.29, bf16[1024,4992]{1,0:T(8,128)(2,1)} %all-gather.5.cloned.1.call-done, ...), kind=kOutput, calls=%fused_computation.64 | convolution fusion | flops 6476003328 | bytes 23085056 | tf_op jit(solution)/shard_map/dot_general | solution.py:40
  631.4 15.5 %collective-permute-done.21 = bf16[2,4,32,2048]{3,2,1,0:T(8,128)(2,1)S(1)} collective-permute-done((bf16[2,4,32,2048]{3,2,1,0:T(8,128)(2,1)S(1)}, bf16[2,4,32,2048]{3,2,1,0:T(8,128)(2,1)S(1)}, u32[]{:S(2)}, u32[]{:S(2)}) %collective-permute-start.21) | collective-permute-done | bytes 1048608 | tf_op jit(solution)/shard_map/ppermute | solution.py:466
  677.7 10.7 %collective-permute-done.12 = bf16[4,32,2560]{2,1,0:T(8,128)(2,1)S(1)} collective-permute-done((bf16[4,32,2560]{2,1,0:T(8,128)(2,1)S(1)}, bf16[4,32,2560]{2,1,0:T(8,128)(2,1)S(1)}, u32[]{:S(2)}, u32[]{:S(2)}) %collective-permute-start.12) | collective-permute-done | bytes 655392 | tf_op jit(solution)/shard_map/ppermute | solution.py:469
  703.7 16.4 %collective-permute-done.16 = bf16[2,4,32,4096]{3,2,1,0:T(8,128)(2,1)S(1)} collective-permute-done((bf16[2,4,32,4096]{3,2,1,0:T(8,128)(2,1)S(1)}, bf16[2,4,32,4096]{3,2,1,0:T(8,128)(2,1)S(1)}, u32[]{:S(2)}, u32[]{:S(2)}) %collective-permute-start.16) | collective-permute-done | bytes 2097184 | tf_op jit(solution)/shard_map/ppermute | solution.py:466
  738.6 10.6 %collective-permute-done.18 = bf16[2,32,4096]{2,1,0:T(8,128)(2,1)S(1)} collective-permute-done((bf16[2,32,4096]{2,1,0:T(8,128)(2,1)S(1)}, bf16[2,32,4096]{2,1,0:T(8,128)(2,1)S(1)}, u32[]{:S(2)}, u32[]{:S(2)}) %collective-permute-start.18) | collective-permute-done | bytes 524320 | tf_op jit(solution)/shard_map/ppermute | solution.py:422
  752.4 10.6 %collective-permute-done.19 = bf16[1,32,4096]{2,1,0:T(8,128)(2,1)S(1)} collective-permute-done((bf16[1,32,4096]{2,1,0:T(8,128)(2,1)S(1)}, bf16[1,32,4096]{2,1,0:T(8,128)(2,1)S(1)}, u32[]{:S(2)}, u32[]{:S(2)}) %collective-permute-start.19) | collective-permute-done | bytes 262176 | tf_op jit(solution)/shard_map/ppermute | solution.py:422
  (409 shorter events, 291.9 us)
Async XLA Ops:
  7.2 92.4 %all-gather.5.cloned.1.call-start = ((), (), s32[]{:S(2)}) async-start(), calls=%async_computation | async-start | bytes 10543104 | tf_op jit(solution)/shard_map/all_gather | solution.py:491
  10.8 203.6 %all-gather.7.cloned.1.call-start = ((), (), s32[]{:S(2)}) async-start(), calls=%async_computation.1 | async-start | bytes 5406720 | tf_op jit(solution)/shard_map/all_gather | solution.py:491
  12.4 234.5 %all-gather.9.cloned.1.call-start = ((), (), s32[]{:S(2)}) async-start(), calls=%async_computation.2 | async-start | bytes 8650752 | tf_op jit(solution)/shard_map/all_gather | solution.py:491
  14.2 296.3 %all-gather.11.cloned.1.call-start = ((), (), s32[]{:S(2)}) async-start(), calls=%async_computation.3 | async-start | bytes 4325376 | tf_op jit(solution)/shard_map/all_gather | solution.py:491
  555.1 24.1 %collective-permute-start.25 = (f32[104,128]{1,0:T(8,128)S(1)}, f32[104,128]{1,0:T(8,128)S(1)}, u32[]{:S(2)}, u32[]{:S(2)}) collective-permute-start(f32[104,128]{1,0:T(8,128)S(1)} %pad_bitcast_fusion), channel_id=1, source_target_pairs={{0,1},{1,0},{2,3},{3,2},{4,5},{5,4},{6,7},{7,6},{8,9},{9,8},{10,11... | collective-permute-start | bytes 159752 | tf_op jit(solution)/shard_map/ppermute | solution.py:422
  566.2 51.4 %collective-permute-start.20 = (bf16[8,64,2048]{2,1,0:T(8,128)(2,1)}, bf16[8,64,2048]{2,1,0:T(8,128)(2,1)}, u32[]{:S(2)}, u32[]{:S(2)}) collective-permute-start(bf16[8,64,2048]{2,1,0:T(8,128)(2,1)} %get-tuple-element.175), channel_id=1, source_target_pairs={{0,2},{1,3},{2,0},{3,1},{4,6},{5,7},{6,4},{7,5},{8,10},{9,11},{10,... | collective-permute-start | bytes 6291464 | tf_op jit(solution)/shard_map/ppermute | solution.py:422
  570.5 102.4 %collective-permute-start.15 = (bf16[8,64,4096]{2,1,0:T(8,128)(2,1)}, bf16[8,64,4096]{2,1,0:T(8,128)(2,1)}, u32[]{:S(2)}, u32[]{:S(2)}) collective-permute-start(bf16[8,64,4096]{2,1,0:T(8,128)(2,1)} %get-tuple-element.156), channel_id=1, source_target_pairs={{0,2},{1,3},{2,0},{3,1},{4,6},{5,7},{6,4},{7,5},{8,10},{9,11},{10,... | collective-permute-start | bytes 12582920 | tf_op jit(solution)/shard_map/ppermute | solution.py:422
  576.4 45.6 %collective-permute-start.10 = (bf16[8,64,2560]{2,1,0:T(8,128)(2,1)}, bf16[8,64,2560]{2,1,0:T(8,128)(2,1)}, u32[]{:S(2)}, u32[]{:S(2)}) collective-permute-start(bf16[8,64,2560]{2,1,0:T(8,128)(2,1)} %get-tuple-element.166), channel_id=1, source_target_pairs={{0,2},{1,3},{2,0},{3,1},{4,6},{5,7},{6,4},{7,5},{8,10},{9,11},{10,... | collective-permute-start | bytes 7864328 | tf_op jit(solution)/shard_map/ppermute | solution.py:422
  579.2 34.1 %collective-permute-start.5 = (bf16[8,64,1920]{2,1,0:T(8,128)(2,1)}, bf16[8,64,1920]{2,1,0:T(8,128)(2,1)}, u32[]{:S(2)}, u32[]{:S(2)}) collective-permute-start(bf16[8,64,1920]{2,1,0:T(8,128)(2,1)} %get-tuple-element.182), channel_id=1, source_target_pairs={{0,2},{1,3},{2,0},{3,1},{4,6},{5,7},{6,4},{7,5},{8,10},{9,11},{10,... | collective-permute-start | bytes 5898248 | tf_op jit(solution)/shard_map/ppermute | solution.py:422
  594.6 12.9 %collective-permute-start.29 = (f32[104,128]{1,0:T(8,128)S(1)}, f32[104,128]{1,0:T(8,128)S(1)}, u32[]{:S(2)}, u32[]{:S(2)}) collective-permute-start(f32[104,128]{1,0:T(8,128)S(1)} %add.722), channel_id=1, source_target_pairs={{0,16},{1,17},{2,18},{3,19},{4,20},{5,21},{6,22},{7,23},{8,24},{9,... | collective-permute-start | bytes 159752 | tf_op jit(solution)/shard_map/ppermute | solution.py:422
  607.6 40.5 %collective-permute-start = (bf16[8,64,3072]{2,1,0:T(8,128)(2,1)}, bf16[8,64,3072]{2,1,0:T(8,128)(2,1)}, u32[]{:S(2)}, u32[]{:S(2)}) collective-permute-start(bf16[8,64,3072]{2,1,0:T(8,128)(2,1)} %get-tuple-element.161), channel_id=1, source_target_pairs={{0,2},{1,3},{2,0},{3,1},{4,6},{5,7},{6,4},{7,5},{8,10},{9,11},{10,... | collective-permute-start | bytes 9437192 | tf_op jit(solution)/shard_map/ppermute | solution.py:422
  617.0 13.3 %collective-permute-start.6 = (bf16[2,4,32,1920]{3,2,1,0:T(8,128)(2,1)S(1)}, bf16[2,4,32,1920]{3,2,1,0:T(8,128)(2,1)S(1)}, u32[]{:S(2)}, u32[]{:S(2)}) collective-permute-start(bf16[2,4,32,1920]{3,2,1,0:T(8,128)(2,1)S(1)} %pad_maximum_fusion.17), channel_id=1, source_target_pairs={{0,1},{1,0},{2,6},{3,7},{4,5},{5,4},{6,2},{7,3},{8,9},{9,8},{10,14... | collective-permute-start | bytes 2949128 | tf_op jit(solution)/shard_map/ppermute | solution.py:466
  621.0 25.9 %collective-permute-start.21 = (bf16[2,4,32,2048]{3,2,1,0:T(8,128)(2,1)S(1)}, bf16[2,4,32,2048]{3,2,1,0:T(8,128)(2,1)S(1)}, u32[]{:S(2)}, u32[]{:S(2)}) collective-permute-start(bf16[2,4,32,2048]{3,2,1,0:T(8,128)(2,1)S(1)} %pad_maximum_fusion.16), channel_id=1, source_target_pairs={{0,1},{1,0},{2,6},{3,7},{4,5},{5,4},{6,2},{7,3},{8,9},{9,8},{10,14... | collective-permute-start | bytes 3145736 | tf_op jit(solution)/shard_map/ppermute | solution.py:466
  625.4 45.5 %collective-permute-start.11 = (bf16[2,4,32,2560]{3,2,1,0:T(8,128)(2,1)S(1)}, bf16[2,4,32,2560]{3,2,1,0:T(8,128)(2,1)S(1)}, u32[]{:S(2)}, u32[]{:S(2)}) collective-permute-start(bf16[2,4,32,2560]{3,2,1,0:T(8,128)(2,1)S(1)} %pad_maximum_fusion.13), channel_id=1, source_target_pairs={{0,1},{1,0},{2,6},{3,7},{4,5},{5,4},{6,2},{7,3},{8,9},{9,8},{10,14... | collective-permute-start | bytes 3932168 | tf_op jit(solution)/shard_map/ppermute | solution.py:466
  630.8 21.0 %collective-permute-start.7 = (bf16[4,32,1920]{2,1,0:T(8,128)(2,1)S(1)}, bf16[4,32,1920]{2,1,0:T(8,128)(2,1)S(1)}, u32[]{:S(2)}, u32[]{:S(2)}) collective-permute-start(bf16[4,32,1920]{2,1,0:T(8,128)(2,1)S(1)} %get-tuple-element.196), channel_id=1, source_target_pairs={{0,4},{1,5},{2,3},{3,2},{4,0},{5,1},{6,7},{7,6},{8,12},{9,13},{10,... | collective-permute-start | bytes 1474568 | tf_op jit(solution)/shard_map/ppermute | solution.py:469
  647.5 14.1 %collective-permute-start.22 = (bf16[4,32,2048]{2,1,0:T(8,128)(2,1)S(1)}, bf16[4,32,2048]{2,1,0:T(8,128)(2,1)S(1)}, u32[]{:S(2)}, u32[]{:S(2)}) collective-permute-start(bf16[4,32,2048]{2,1,0:T(8,128)(2,1)S(1)} %get-tuple-element.188), channel_id=1, source_target_pairs={{0,4},{1,5},{2,3},{3,2},{4,0},{5,1},{6,7},{7,6},{8,12},{9,13},{10,... | collective-permute-start | bytes 1572872 | tf_op jit(solution)/shard_map/ppermute | solution.py:469
  653.0 44.3 %collective-permute-start.1 = (bf16[2,4,32,3072]{3,2,1,0:T(8,128)(2,1)S(1)}, bf16[2,4,32,3072]{3,2,1,0:T(8,128)(2,1)S(1)}, u32[]{:S(2)}, u32[]{:S(2)}) collective-permute-start(bf16[2,4,32,3072]{3,2,1,0:T(8,128)(2,1)S(1)} %pad_maximum_fusion.12), channel_id=1, source_target_pairs={{0,1},{1,0},{2,6},{3,7},{4,5},{5,4},{6,2},{7,3},{8,9},{9,8},{10,14... | collective-permute-start | bytes 4718600 | tf_op jit(solution)/shard_map/ppermute | solution.py:466
  670.5 20.2 %collective-permute-start.24 = (bf16[1,32,2048]{2,1,0:T(8,128)(2,1)S(1)}, bf16[1,32,2048]{2,1,0:T(8,128)(2,1)S(1)}, u32[]{:S(2)}, u32[]{:S(2)}) collective-permute-start(bf16[1,32,2048]{2,1,0:T(8,128)(2,1)S(1)} %fusion.90), channel_id=1, source_target_pairs={{0,16},{1,17},{2,18},{3,19},{4,20},{5,21},{6,22},{7,23},{8,24},{9,... | collective-permute-start | bytes 393224 | tf_op jit(solution)/shard_map/ppermute | solution.py:422
  671.5 16.9 %collective-permute-start.12 = (bf16[4,32,2560]{2,1,0:T(8,128)(2,1)S(1)}, bf16[4,32,2560]{2,1,0:T(8,128)(2,1)S(1)}, u32[]{:S(2)}, u32[]{:S(2)}) collective-permute-start(bf16[4,32,2560]{2,1,0:T(8,128)(2,1)S(1)} %get-tuple-element.186), channel_id=1, source_target_pairs={{0,4},{1,5},{2,3},{3,2},{4,0},{5,1},{6,7},{7,6},{8,12},{9,13},{10,... | collective-permute-start | bytes 1966088 | tf_op jit(solution)/shard_map/ppermute | solution.py:469
  677.7 42.5 %collective-permute-start.16 = (bf16[2,4,32,4096]{3,2,1,0:T(8,128)(2,1)S(1)}, bf16[2,4,32,4096]{3,2,1,0:T(8,128)(2,1)S(1)}, u32[]{:S(2)}, u32[]{:S(2)}) collective-permute-start(bf16[2,4,32,4096]{3,2,1,0:T(8,128)(2,1)S(1)} %pad_maximum_fusion.9), channel_id=1, source_target_pairs={{0,1},{1,0},{2,6},{3,7},{4,5},{5,4},{6,2},{7,3},{8,9},{9,8},{10,14... | collective-permute-start | bytes 6291464 | tf_op jit(solution)/shard_map/ppermute | solution.py:466
  698.4 23.2 %collective-permute-start.2 = (bf16[4,32,3072]{2,1,0:T(8,128)(2,1)S(1)}, bf16[4,32,3072]{2,1,0:T(8,128)(2,1)S(1)}, u32[]{:S(2)}, u32[]{:S(2)}) collective-permute-start(bf16[4,32,3072]{2,1,0:T(8,128)(2,1)S(1)} %get-tuple-element.184), channel_id=1, source_target_pairs={{0,4},{1,5},{2,3},{3,2},{4,0},{5,1},{6,7},{7,6},{8,12},{9,13},{10,... | collective-permute-start | bytes 2359304 | tf_op jit(solution)/shard_map/ppermute | solution.py:469
  721.5 14.0 %collective-permute-start.17 = (bf16[4,32,4096]{2,1,0:T(8,128)(2,1)S(1)}, bf16[4,32,4096]{2,1,0:T(8,128)(2,1)S(1)}, u32[]{:S(2)}, u32[]{:S(2)}) collective-permute-start(bf16[4,32,4096]{2,1,0:T(8,128)(2,1)S(1)} %get-tuple-element.177), channel_id=1, source_target_pairs={{0,4},{1,5},{2,3},{3,2},{4,0},{5,1},{6,7},{7,6},{8,12},{9,13},{10,... | collective-permute-start | bytes 3145736 | tf_op jit(solution)/shard_map/ppermute | solution.py:469
  735.8 13.4 %collective-permute-start.18 = (bf16[2,32,4096]{2,1,0:T(8,128)(2,1)S(1)}, bf16[2,32,4096]{2,1,0:T(8,128)(2,1)S(1)}, u32[]{:S(2)}, u32[]{:S(2)}) collective-permute-start(bf16[2,32,4096]{2,1,0:T(8,128)(2,1)S(1)} %get-tuple-element.190), channel_id=1, source_target_pairs={{0,8},{1,9},{2,10},{3,11},{4,12},{5,13},{6,14},{7,15},{8,0},{9,1},... | collective-permute-start | bytes 1572872 | tf_op jit(solution)/shard_map/ppermute | solution.py:422
  749.2 13.8 %collective-permute-start.19 = (bf16[1,32,4096]{2,1,0:T(8,128)(2,1)S(1)}, bf16[1,32,4096]{2,1,0:T(8,128)(2,1)S(1)}, u32[]{:S(2)}, u32[]{:S(2)}) collective-permute-start(bf16[1,32,4096]{2,1,0:T(8,128)(2,1)S(1)} %fusion.74), channel_id=1, source_target_pairs={{0,16},{1,17},{2,18},{3,19},{4,20},{5,21},{6,22},{7,23},{8,24},{9,... | collective-permute-start | bytes 786440 | tf_op jit(solution)/shard_map/ppermute | solution.py:422
  (107 other events, 2232.5 us)
Sparse Core Ops, SparseCore 0:
  11.5 88.0 all-gather.4
  103.0 63.8 all-gather.6
  170.5 76.3 all-gather.8
  249.7 60.6 all-gather.10

commit v3 on v2

--- a/solution.py
+++ b/solution.py
@@ -430,7 +430,7 @@
     return lax.dynamic_index_in_dim(values, index, axis, keepdims=False)
 
 
-def scatter(grads):
+def scatter_steps(grads):
     dp = lax.axis_size("dp")
     chips = lax.axis_size("fsdp") // 2
     if dp != 2 or chips < 4:
@@ -442,7 +442,7 @@
     blocks = grads.reshape(chips, 2, 2 * held, width)
     shape = (chips // 2, 2, 2, held, width)
     own = at(blocks, core, 1).reshape(shape)
-    other = flip(at(blocks, 1 - core, 1), 2).reshape(shape)
+    other = (yield flip(at(blocks, 1 - core, 1), 2)).reshape(shape)
 
     def pick(row, col):
         zero = jnp.zeros((), place.dtype)
@@ -463,10 +463,10 @@
     crossing = [(i, i ^ (4 if i & 2 else 1)) for i in range(places)]
     back = [(i, i ^ (1 if i & 2 else 4)) for i in range(places)]
     sent, own = along(1 - near), along(near)
-    other = lax.ppermute(sent, AXES, crossing)
+    other = yield lax.ppermute(sent, AXES, crossing)
     sent = add(at(own, 1 - far, 0), at(other, 1 - far, 0))
     own = add(at(own, far, 0), at(other, far, 0))
-    other = lax.ppermute(sent, AXES, back)
+    other = yield lax.ppermute(sent, AXES, back)
     level = 1
     while level < chips // 2:
         shape = (-1, 2, held, width)
@@ -474,9 +474,33 @@
         own, other = own.reshape(shape), other.reshape(shape)
         sent = add(at(own, 1 - mine, 1), at(other, 1 - mine, 1))
         own = add(at(own, mine, 1), at(other, mine, 1))
-        other = flip(sent, 8 * level)
+        other = yield flip(sent, 8 * level)
         level *= 2
     return (own.astype(f32) + other.astype(f32)).reshape(held, width)
+
+
+class Sums:
+    def __init__(self):
+        self.flying, self.sums = {}, {}
+
+    def move(self, name, steps, value):
+        try:
+            self.flying[name] = (steps, steps.send(value))
+        except StopIteration as stop:
+            self.sums[name] = stop.value
+            self.flying.pop(name, None)
+
+    def start(self, name, grads):
+        self.move(name, scatter_steps(grads.astype(bf16)), None)
+
+    def step(self, anchor, *names):
+        names = [name for name in (names or tuple(self.flying)) if name in self.flying]
+        anchor, arrived = lax.optimization_barrier(
+            (anchor, tuple(self.flying[name][1] for name in names))
+        )
+        for name, value in zip(names, arrived):
+            self.move(name, self.flying[name][0], value)
+        return anchor
 
 
 def sum_everywhere(values):
@@ -503,9 +527,12 @@
     w_first = gather(
         (w_in[:, :D_SSM], w_query, w_key, w_value, w_in[:, D_SSM:conv_end], w_in[:, conv_end:], dt_pad)
     )
-    w_second = gather((w_attn_out.T, w_out.T))
-    w_third = gather((w_gate, w_up))
-    w_fourth = gather((w_down.T,))
+    w_later = gather((w_attn_out.T, w_out.T, w_gate, w_up, w_down.T))
+    second_end = w_attn_out.shape[0] + w_out.shape[0]
+    third_end = second_end + 2 * w_gate.shape[1]
+    w_second = w_later[:, :second_end]
+    w_third = w_later[:, second_end:third_end]
+    w_fourth = w_later[:, third_end:]
 
     stream = tokens[0].astype(f32)
     doc_ids = segments[0]
@@ -564,23 +591,26 @@
     hidden = (jax.nn.silu(gate) * up).astype(bf16)
     mixed = (resid + mm_nt(hidden, w_fourth)).astype(bf16)
 
+    sums = Sums()
     d_hidden = mm(cot, w_fourth)
-    sum_fourth = scatter(mm_tn(cot, hidden).astype(bf16))
+    sums.start("fourth", mm_tn(cot, hidden))
     d_both = jnp.concatenate(
         [(d_hidden * up * silu_slope(gate)).astype(bf16), (d_hidden * jax.nn.silu(gate)).astype(bf16)],
         axis=1,
     )
-    sum_third = scatter(mm_tn(mid_in, d_both).astype(bf16))
-    d_mid = mm_nt(d_both, w_third)
+    d_both = sums.step(d_both)
+    sums.start("third", mm_tn(mid_in, d_both))
+    d_mid = sums.step(mm_nt(d_both, w_third), "fourth")
     back, g_norm_mid = norm_back(d_mid, norm_mid, resid, inv_mid)
-    d_resid = cot.astype(f32) + back
+    d_resid = sums.step(cot.astype(f32) + back)
     d_resid_low = d_resid.astype(bf16)
-    sum_second = scatter(mm_tn(d_resid_low, branches).astype(bf16))
-    d_branches = mm(d_resid_low, w_second)
+    sums.start("second", mm_tn(d_resid_low, branches))
+    d_branches = sums.step(mm(d_resid_low, w_second))
     attn_width = HEADS * HEAD_DIM
     d_query, d_key, d_value = attend_bwd(
         query, key, value, d_branches[:, :attn_width], lse, doc_col, doc_row
     )
+    d_query, d_branches = sums.step((d_query, d_branches))
     d_mixed_in, g_norm_gated = norm_back(d_branches[:, attn_width:], norm_gated, mixed_in, inv_gated)
     d_ssm = d_mixed_in * jax.nn.silu(z_gate)
     d_first = jnp.concatenate(
@@ -592,9 +622,11 @@
         ],
         axis=1,
     )
-    sum_first = scatter(mm_tn(normed, d_first).astype(bf16))
+    d_ssm, d_first = sums.step((d_ssm, d_first))
+    sums.start("first", mm_tn(normed, d_first))
     g_skip = jnp.sum(jnp.sum(d_ssm * x_heads.astype(f32), axis=0).reshape(M_HEADS, M_HDIM), axis=1)
     d_x, d_b, d_c, d_st, d_ld = scan_bwd(act_low, ld, st, states, d_ssm)
+    d_x = sums.step(d_x)
     d_act = jnp.concatenate([d_x + skip_wide * d_ssm, d_b, d_c], axis=1)
     d_conv = d_act * silu_slope(convolved)
     g_conv_bias = jnp.sum(d_conv, axis=0)
@@ -606,6 +638,7 @@
         g_taps.append(jnp.sum(masked * shifted, axis=0))
         later = jnp.pad(masked, ((0, offset), (0, 0)))[offset:]
         d_conv_in = d_conv_in + conv_weight[offset][None, :] * later
+    d_conv_in = sums.step(d_conv_in)
     g_conv_weight = jnp.stack(g_taps)
     d_ld = d_ld[:, :M_HEADS]
     d_step = d_st[:, :M_HEADS] - d_ld * jnp.exp(a_log)
@@ -615,10 +648,15 @@
     d_last = jnp.concatenate(
         [d_conv_in.astype(bf16), jnp.pad(d_raw, ((0, 0), (0, 128 - M_HEADS))).astype(bf16)], axis=1
     )
-    sum_last = scatter(mm_tn(normed, d_last).astype(bf16))
-    d_normed = mm_nt(d_first, w_first[:, :conv_at]) + mm_nt(d_last, w_first[:, conv_at:])
+    sums.start("last", mm_tn(normed, d_last))
+    d_normed = sums.step(mm_nt(d_first, w_first[:, :conv_at]))
+    d_normed = sums.step(d_normed + mm_nt(d_last, w_first[:, conv_at:]))
     back, g_norm_in = norm_back(d_normed, norm_in, stream, inv_in)
-    grad_tokens = d_resid + back
+    grad_tokens = sums.step(d_resid + back)
+    while sums.flying:
+        sums.step(())
+    sum_first, sum_last = sums.sums["first"], sums.sums["last"]
+    sum_second, sum_third, sum_fourth = sums.sums["second"], sums.sums["third"], sums.sums["fourth"]
 
     small = (
         g_norm_in, g_conv_weight, g_conv_bias, g_dt_bias, g_a_log, g_skip, g_norm_gated, g_norm_mid

time: 782 us -> 705 us (0.902)
  waiting for transfers between devices: 236 us -> 127 us
  other arithmetic: 140 us -> 175 us
  matrix products: 164 us -> 148 us
    all_gather x4 -> x2, waiting for transfers between devices: 133 us -> 82.9 us  [gather(): lax.all_gather(jnp.concatenate(parts, axis=1), AXES, axis=0, tiled=True)]
    ppermute x20, waiting for transfers between devices: 50.5 us -> 17.6 us  [flip(): return lax.ppermute(values, AXES, [(i, i ^ bit) for i in range(places)])]
    ppermute x10, waiting for transfers between devices: 51.5 us -> 26.9 us  [the longest x5 21 us: scatter_steps(): other = (yield lax.ppermute(sent, AXES, crossing))]
    convert_element_type x15, other arithmetic: 5.28 us -> 16.7 us  [add(): return (left.astype(f32) + right.astype(f32)).astype(bf16)]
    optimization_barrier x0 -> x2, local copies, waits for them, and re-layouts: none -> 11 us  [step(): lax.optimization_barrier((anchor, tuple((self.flying[name][1] for name in...]
    add x2 -> x4, other arithmetic: 12.6 us -> 23.2 us  [the longest x1 11.2 us: shards(): d_conv_in = d_conv_in + conv_weight[offset][None, :] * later]
    reduce_sum x1 -> x3, other arithmetic: 2.23 us -> 12.8 us  [norm_back(): return (back, jnp.sum(normed_grad * unit, axis=0))]
    reduce_sum x1, other arithmetic: 13.6 us -> 5.47 us  [shards(): jnp.sum(d_ssm * x_heads.astype(f32), axis=0).reshape(M_HEADS, M_HDIM)]
  transfers between devices with their start and end apart: 34 -> 32, of which waited for: 19 -> 14; matrix products, arithmetic and copies ran while one was open for 25% -> 37% of each run, Pallas kernels for 4% -> 13%
where the time goes in v3:
time: 705 us; the launch traced here: 693 us
  other arithmetic  175 us (25%)
  matrix products  148 us (21%)
  waiting for transfers between devices  127 us (18%)
  local copies, waits for them, and re-layouts  98.6 us (14%)
  Pallas kernels  90.2 us (13%)
  starting transfers between devices  33 us (5%)
  between operations  21.3 us (3%)
    all_gather x2, waiting for transfers between devices, gather(): lax.all_gather(jnp.concatenate(parts, axis=1), AXES, axis=0, tiled=True)  82.9 us
    dot_general x4, matrix products, mm(): return jnp.dot(left, right, preferred_element_type=f32)  55.3 us
    dot_general x5, matrix products, mm_nt(): return lax.dot_general(left, right, NT, preferred_element_type=f32)  51.2 us
    unnamed x241, local copies, waits for them, and re-layouts  43.7 us
    dot_general x5, matrix products, mm_tn(): return lax.dot_general(left, right, TN, preferred_element_type=f32)  41.5 us
    pallas_call x1, Pallas kernels, scan_bwd(): pl.pallas_call(scan_bwd_kernel, grid=(blocks,), in_specs=[pl.BlockSpec((S...  31.9 us
    ppermute x20, starting transfers between devices, flip(): return lax.ppermute(values, AXES, [(i, i ^ bit) for i in range(places)])  26.9 us
    pallas_call x1, Pallas kernels, attend_bwd(): pl.pallas_call(attend_bwd_kernel, grid=(KV_HEADS, group), in_specs=[per_q...  24.7 us
  transfers between devices with their start and end apart: 32, of which 14 were waited for; matrix products, arithmetic and copies ran while one was open for 37% of the time, Pallas kernels for 13%

profile of v3, /device:TPU:1, one launch (start us, length us, event | category | flops | bytes accessed | tf_op | source)
XLA Modules:
  0.0 693.4 jit_solution(5177630241211131718)
XLA Ops:
  26.9 72.7 %all-gather.3.cloned.1.call-done = bf16[1024,4992]{1,0:T(8,128)(2,1)} async-done(((bf16[32,4992]{1,0:T(8,128)(2,1)}), bf16[1024,4992]{1,0:T(8,128)(2,1)}) %all-gather.3.cloned.1.call-update) | async-done | bytes 10223632 | tf_op jit(solution)/shard_map/all_gather | solution.py:515
  99.6 18.0 %fusion.120 = f32[1024,4992]{1,0:T(8,128)} fusion(bf16[1024,4992]{1,0:T(8,128)(2,1)} %all-gather.3.cloned.1.call-done, bf16[1,1024,1024]{1,2,0:T(8,128)(2,1)S(1)} %copy.155, f32[1024]{0:T(1024)S(1)} %copy-done.88, f32[1024]{0:T(1024)S(1)} %add_rsqrt_fusion.2), kind=kOutput, calls=%fused_computation.305 | convolution fusion | flops 10473177088 | bytes 32776192 | tf_op jit(solution)/shard_map/dot_general | solution.py:36
  146.6 19.2 %multiply_convert_fusion.1 = (bf16[1024,1792]{1,0:T(8,128)(2,1)S(1)}, f32[1024,1792]{1,0:T(8,128)}) fusion(f32[1024,1792]{1,0:T(8,128)} %slice.238, f32[1792]{0:T(1024)S(1)} %get-tuple-element.204, pred[1024]{0:T(1024)(128)(4,1)S(1)} %get-tuple-element.293, f32[1792]{0:T(1024)S(1)} %get-tuple-element.205, pred[1024]{0:T(1024)(128)(4,1)S(1)} %get-tuple-element.292, ...), kind=kLoop, calls=%fused_computation.35 | loop fusion | flops 29360128 | bytes 18388992 | tf_op jit(solution)/shard_map/convert_element_type | solution.py:564
  165.9 13.2 %shard_map.340 = (f32[1024,1536]{1,0:T(8,128)S(1)}, bf16[8,128,1536]{2,1,0:T(8,128)(2,1)S(1)}) custom-call(bf16[1024,1792]{1,0:T(8,128)(2,1)S(1)} %get-tuple-element.216.x_ref.b_ref.c_ref, bf16[1024,1792]{1,0:T(8,128)(2,1)S(1)} %get-tuple-element.216.x_ref.b_ref.c_ref, bf16[1024,1792]{1,0:T(8,128)(2,1)S(1)} %get-tuple-element.216.x_ref.b_ref.c_ref, ...), custom_call_target="tpu_custom_call" | custom-call | tf_op jit(solution)/shard_map/pallas_call | solution.py:200
  180.8 20.4 %shard_map.339 = (bf16[1024,1024]{1,0:T(8,128)(2,1)S(1)}, f32[8,1,1024]{2,1,0:T(1,128)S(1)}) custom-call(bf16[1024,1024]{1,0:T(8,128)(2,1)S(1)} %bitcast.304, bf16[1024,256]{1,0:T(8,128)(2,1)S(1)} %bitcast.306, bf16[1024,256]{1,0:T(8,128)(2,1)S(1)} %copy-done.5, f32[1024,1]{1,0:T(8,128)S(1)} %copy.156.doc_col_ref, f32[1,1024]{1,0:T(1,128)S(1)} %get-tuple-element.290.doc_row_ref), custom_call_target="tpu_custom_call" | custom-call | tf_op jit(solution)/shard_map/pallas_call | solution.py:331
  211.3 10.2 %all-gather.5.cloned.1.call-done = bf16[1024,8704]{1,0:T(8,128)(2,1)} async-done(((bf16[32,8704]{1,0:T(8,128)(2,1)}), bf16[1024,8704]{1,0:T(8,128)(2,1)}) %all-gather.5.cloned.1.call-update) | async-done | bytes 17825808 | tf_op jit(solution)/shard_map/all_gather | solution.py:515
  221.4 9.2 %multiply_reduce_fusion.9 = (f32[1024]{0:T(1024)S(1)}, f32[1024,1024]{0,1:T(8,128)S(1)}) fusion(bf16[1024,8704]{1,0:T(8,128)(2,1)} %all-gather.5.cloned.1.call-done, bf16[1024,1536]{1,0:T(8,128)(2,1)} %multiply_convert_fusion.3, bf16[1024,1024]{1,0:T(8,128)(2,1)S(1)} %copy-done.18, bf16[1,1024,1024]{1,2,0:T(8,128)(2,1)} %copy-done.25), kind=kOutput, calls=%fused_computation.82 | convolution fusion | flops 5383388160 | bytes 16781312 | tf_op jit(solution)/shard_map/dot_general | solution.py:40
  232.7 15.1 %fusion.7 = f32[1024,4096]{1,0:T(8,128)} fusion(bf16[1024,8704]{1,0:T(8,128)(2,1)} %all-gather.5.cloned.1.call-done, f32[1024,1024]{0,1:T(8,128)S(1)} %get-tuple-element.297, f32[1024]{0:T(1024)S(1)} %copy-done.87, f32[1024]{0:T(1024)S(1)} %add_rsqrt_fusion), kind=kOutput, calls=%fused_computation.22 | convolution fusion | flops 8593080320 | bytes 29368320 | tf_op jit(solution)/shard_map/dot_general | solution.py:36
  247.7 14.2 %fusion.1 = (bf16[1024,2048]{1,0:T(8,128)(2,1)}, bf16[1024,2048]{1,0:T(8,128)(2,1)}, bf16[1024,2048]{1,0:T(8,128)(2,1)S(1)}) fusion(f32[1024,4096]{1,0:T(8,128)} %fusion.7, bf16[1024,8704]{1,0:T(8,128)(2,1)} %all-gather.5.cloned.1.call-done, bf16[1,1024,1024]{2,1,0:T(8,128)(2,1)S(1)} %copy-done.47), kind=kOutput, calls=%fused_computation.4 | convolution fusion | flops 4326424576 | bytes 35651584 | tf_op jit(solution)/shard_map/dot_general | solution.py:36
  279.9 10.6 %fusion.44 = bf16[1,1024,1024]{1,2,0:T(8,128)(2,1)} fusion(f32[1024,1024]{0,1:T(8,128)} %copy-done.27, bf16[1024,2048]{1,0:T(8,128)(2,1)} %copy-done.103, bf16[1024,8704]{1,0:T(8,128)(2,1)} %all-gather.5.cloned.1.call-done), kind=kOutput, calls=%fused_computation.105 | convolution fusion | flops 4297064448 | bytes 14680064 | tf_op jit(solution)/shard_map/dot_general | solution.py:40
  302.3 14.5 %convolution_convert_fusion = bf16[1024,4096]{1,0:T(8,128)(2,1)} fusion(bf16[1024,4096]{1,0:T(8,128)(2,1)} %pad_maximum_fusion, f32[1024,1024]{0,1:T(8,128)} %copy-done.27, f32[1024]{0:T(1024)S(1)} %copy-done.87, f32[1024]{0:T(1024)S(1)} %add_rsqrt_fusion), kind=kOutput, calls=%fused_computation.13 | convolution fusion | flops 8597274624 | bytes 20979712 | tf_op jit(solution)/shard_map/dot_general | solution.py:44
  316.8 8.3 %constant_dynamic-slice_fusion.3 = (bf16[8,1,64,4096]{3,2,1,0:T(8,128)(2,1)}, bf16[8,64,4096]{2,1,0:T(8,128)(2,1)}) fusion(bf16[8,2,64,4096]{3,2,1,0:T(8,128)(2,1)} %bitcast.330, s32[]{:T(128)S(6)} %select_n.379, s32[]{:T(128)S(6)} %select_n.378), kind=kLoop, calls=%fused_computation.269 | loop fusion | bytes 16777224 | tf_op jit(solution)/shard_map/jit(dynamic_index_in_dim)/dynamic_slice | solution.py:430
  328.7 12.8 %fusion.5 = f32[1024,1024]{1,0:T(8,128)} fusion(bf16[1024,4096]{1,0:T(8,128)(2,1)S(1)} %bitcast.329, bf16[1024,8704]{1,0:T(8,128)(2,1)} %all-gather.5.cloned.1.call-done), kind=kOutput, calls=%fused_computation.20 | convolution fusion | flops 8589934592 | bytes 20971520 | tf_op jit(solution)/shard_map/dot_general | solution.py:40
  376.0 8.1 %fusion.24 = f32[1024,2560]{1,0:T(8,128)S(1)} fusion(bf16[1024,8704]{1,0:T(8,128)(2,1)} %all-gather.5.cloned.1.call-done, f32[1024,1024]{0,1:T(8,128)S(1)} %multiply_add_fusion.1), kind=kOutput, calls=%fused_computation.62 | convolution fusion | flops 5369757696 | bytes 19922944 | tf_op jit(solution)/shard_map/dot_general | solution.py:36
  386.4 13.8 %collective-permute-done.5 = bf16[2,4,32,4096]{3,2,1,0:T(8,128)(2,1)S(1)} collective-permute-done((bf16[2,4,32,4096]{3,2,1,0:T(8,128)(2,1)}, bf16[2,4,32,4096]{3,2,1,0:T(8,128)(2,1)S(1)}, u32[]{:S(2)}, u32[]{:S(2)}) %collective-permute-start.5) | collective-permute-done | bytes 2097184 | tf_op jit(solution)/shard_map/ppermute | solution.py:466
  410.2 24.7 %shard_map.341 = (f32[1024,1024]{1,0:T(8,128)S(1)}, f32[1024,256]{1,0:T(8,128)S(1)}, f32[1024,256]{1,0:T(8,128)S(1)}) custom-call(bf16[1024,1024]{1,0:T(8,128)(2,1)S(1)} %bitcast.305, bf16[1024,256]{1,0:T(8,128)(2,1)S(1)} %bitcast.307, bf16[1024,256]{1,0:T(8,128)(2,1)S(1)} %copy-done.6, f32[1024,1024]{1,0:T(8,128)S(1)} %slice.207.do_ref, ...), custom_call_target="tpu_custom_call" | custom-call | tf_op jit(solution)/shard_map/pallas_call | solution.py:360
  451.9 12.2 %multiply_convert_fusion.2 = (bf16[1024,1536]{1,0:T(8,128)(2,1)}, f32[1024,1536]{1,0:T(8,128)}) fusion(f32[1024,4992]{1,0:T(8,128)} %fusion.120, f32[1024,1536]{1,0:T(8,128)S(1)} %bitcast.303, f32[1024]{0:T(1024)S(1)} %broadcast_multiply_fusion, f32[1024,1536]{1,0:T(8,128)} %copy-done.19, f32[1024,2560]{1,0:T(8,128)S(1)} %copy-done.21, ...), kind=kLoop, calls=%fused_computation.52 | loop fusion | flops 31457280 | bytes 37769216 | tf_op jit(solution)/shard_map/convert_element_type | solution.py:618
  497.9 10.4 %fusion.17 = f32[1024,1024]{1,0:T(8,128)} fusion(bf16[1024,3072]{1,0:T(8,128)(2,1)S(1)} %pad_maximum_fusion.1, bf16[1024,4992]{1,0:T(8,128)(2,1)} %all-gather.3.cloned.1.call-done), kind=kOutput, calls=%fused_computation.40 | convolution fusion | flops 6442450944 | bytes 16777216 | tf_op jit(solution)/shard_map/dot_general | solution.py:40
  508.3 31.9 %shard_map.342 = (f32[1024,1536]{1,0:T(8,128)}, f32[1024,128]{1,0:T(8,128)S(1)}, f32[1024,128]{1,0:T(8,128)S(1)}, f32[1024,128]{1,0:T(8,128)S(1)}, f32[1024,128]{1,0:T(8,128)S(1)}) custom-call(bf16[1024,1792]{1,0:T(8,128)(2,1)S(1)} %copy-done.1, bf16[1024,1792]{1,0:T(8,128)(2,1)S(1)} %copy-done.1, bf16[1024,1792]{1,0:T(8,128)(2,1)S(1)} %copy-done.1, ...), custom_call_target="tpu_custom_call" | custom-call | tf_op jit(solution)/shard_map/pallas_call | solution.py:227
  554.0 8.8 %fusion.122 = (f32[1792]{0:T(1024)S(1)}, f32[1792]{0:T(1024)S(1)}, f32[1024,1792]{1,0:T(8,128)S(1)}) fusion(f32[1024,4992]{1,0:T(8,128)} %fusion.120, f32[1024,1792]{1,0:T(8,128)} %get-tuple-element.217, f32[1024,128]{1,0:T(8,128)S(1)} %get-tuple-element.97, f32[1024,128]{1,0:T(8,128)S(1)} %get-tuple-element.96, f32[1024,1536]{1,0:T(8,128)} %get-tuple-element.229), kind=kLoop, calls=%fused_computation.306 | loop fusion | flops 23851520 | bytes 29374464 | tf_op jit(solution)/shard_map/reduce_sum | solution.py:632
  562.9 9.2 %multiply_reduce_fusion.2 = (f32[1792]{0:T(1024)S(1)}, f32[1792]{0:T(1024)S(1)}, f32[1792]{0:T(1024)S(1)}, f32[1024,1792]{1,0:T(8,128)}, f32[1024,1792]{1,0:T(8,128)}, /*index=5*/f32[1024,1792]{1,0:T(8,128)}) fusion(f32[1024,1792]{1,0:T(8,128)S(1)} %bitcast.312, f32[1024,1792]{1,0:T(8,128)S(1)} %get-tuple-element.208, pred[1024]{0:T(1024)(128)(4,1)S(1)} %copy-done.95, ...), kind=kLoop, calls=%fused_computation.33 | loop fusion | flops 16509696 | bytes 36724736 | tf_op jit(solution)/shard_map/reduce_sum | solution.py:638
  577.9 11.2 %fusion.12 = bf16[1024,1792]{1,0:T(8,128)(2,1)} fusion(f32[1024,1792]{1,0:T(8,128)} %get-tuple-element.211, f32[1024,1792]{1,0:T(8,128)} %get-tuple-element.210, f32[1024,1792]{1,0:T(8,128)} %get-tuple-element.209, f32[1024,1792]{1,0:T(8,128)S(1)} %get-tuple-element.208, f32[1792]{0:T(1024)S(1)} %copy-done.74, f32[1792]{0:T(1024)S(1)} %copy-done.76, ...), kind=kLoop, calls=%fused_computation.27 | loop fusion | flops 14680064 | bytes 33058816 | tf_op jit(solution)/shard_map/add | solution.py:640
  608.0 8.2 %fusion.37 = f32[1024,1024]{0,1:T(8,128)} fusion(bf16[1024,4992]{1,0:T(8,128)(2,1)} %all-gather.3.cloned.1.call-done, bf16[1024,24]{1,0:T(8,128)(2,1)S(1)} %copy-done.66, bf16[1024,1792]{1,0:T(8,128)(2,1)S(1)} %copy-done.42), kind=kOutput, calls=%fused_computation.87 | convolution fusion | flops 4038328320 | bytes 11845632 | tf_op jit(solution)/shard_map/dot_general | solution.py:40
  659.7 8.9 %collective-permute-done.29 = f32[104,128]{1,0:T(8,128)S(1)} collective-permute-done((f32[104,128]{1,0:T(8,128)S(1)}, f32[104,128]{1,0:T(8,128)S(1)}, u32[]{:S(2)}, u32[]{:S(2)}) %collective-permute-start.29) | collective-permute-done | bytes 53280 | tf_op jit(solution)/shard_map/ppermute | solution.py:422
  (444 shorter events, 286.3 us)
Async XLA Ops:
  7.2 92.4 %all-gather.3.cloned.1.call-start = ((), (), s32[]{:S(2)}) async-start(), calls=%async_computation | async-start | bytes 10543104 | tf_op jit(solution)/shard_map/all_gather | solution.py:515
  10.8 210.6 %all-gather.5.cloned.1.call-start = ((), (), s32[]{:S(2)}) async-start(), calls=%async_computation.1 | async-start | bytes 18382848 | tf_op jit(solution)/shard_map/all_gather | solution.py:515
  269.7 32.5 %collective-permute-start = (bf16[8,64,2048]{2,1,0:T(8,128)(2,1)}, bf16[8,64,2048]{2,1,0:T(8,128)(2,1)}, u32[]{:S(2)}, u32[]{:S(2)}) collective-permute-start(bf16[8,64,2048]{2,1,0:T(8,128)(2,1)} %get-tuple-element.250), channel_id=1, source_target_pairs={{0,2},{1,3},{2,0},{3,1},{4,6},{5,7},{6,4},{7,5},{8,10},{9,11},{10,... | collective-permute-start | bytes 6291464 | tf_op jit(solution)/shard_map/ppermute | solution.py:422
  325.1 34.3 %collective-permute-start.3 = (bf16[8,64,4096]{2,1,0:T(8,128)(2,1)}, bf16[8,64,4096]{2,1,0:T(8,128)(2,1)}, u32[]{:S(2)}, u32[]{:S(2)}) collective-permute-start(bf16[8,64,4096]{2,1,0:T(8,128)(2,1)} %get-tuple-element.227), channel_id=1, source_target_pairs={{0,2},{1,3},{2,0},{3,1},{4,6},{5,7},{6,4},{7,5},{8,10},{9,11},{10,... | collective-permute-start | bytes 12582920 | tf_op jit(solution)/shard_map/ppermute | solution.py:422
  327.4 16.1 %collective-permute-start.1 = (bf16[2,4,32,2048]{3,2,1,0:T(8,128)(2,1)S(1)}, bf16[2,4,32,2048]{3,2,1,0:T(8,128)(2,1)}, u32[]{:S(2)}, u32[]{:S(2)}) collective-permute-start(bf16[2,4,32,2048]{3,2,1,0:T(8,128)(2,1)S(1)} %pad_maximum_fusion.12), channel_id=1, source_target_pairs={{0,1},{1,0},{2,6},{3,7},{4,5},{5,4},{6,2},{7,3},{8,9},{9,8},{10,14... | collective-permute-start | bytes 3145736 | tf_op jit(solution)/shard_map/ppermute | solution.py:466
  359.5 26.8 %collective-permute-start.4 = (bf16[2,32,2048]{2,1,0:T(8,128)(2,1)S(1)}, bf16[2,32,2048]{2,1,0:T(8,128)(2,1)S(1)}, u32[]{:S(2)}, u32[]{:S(2)}) collective-permute-start(bf16[2,32,2048]{2,1,0:T(8,128)(2,1)S(1)} %get-tuple-element.275), channel_id=1, source_target_pairs={{0,8},{1,9},{2,10},{3,11},{4,12},{5,13},{6,14},{7,15},{8,0},{9,1},... | collective-permute-start | bytes 786440 | tf_op jit(solution)/shard_map/ppermute | solution.py:422
  367.9 32.3 %collective-permute-start.6 = (bf16[8,64,2560]{2,1,0:T(8,128)(2,1)S(1)}, bf16[8,64,2560]{2,1,0:T(8,128)(2,1)S(1)}, u32[]{:S(2)}, u32[]{:S(2)}) collective-permute-start(bf16[8,64,2560]{2,1,0:T(8,128)(2,1)S(1)} %get-tuple-element.241), channel_id=1, source_target_pairs={{0,2},{1,3},{2,0},{3,1},{4,6},{5,7},{6,4},{7,5},{8,10},{9,11},{10,... | collective-permute-start | bytes 7864328 | tf_op jit(solution)/shard_map/ppermute | solution.py:422
  374.8 25.4 %collective-permute-start.5 = (bf16[2,4,32,4096]{3,2,1,0:T(8,128)(2,1)}, bf16[2,4,32,4096]{3,2,1,0:T(8,128)(2,1)S(1)}, u32[]{:S(2)}, u32[]{:S(2)}) collective-permute-start(bf16[2,4,32,4096]{3,2,1,0:T(8,128)(2,1)} %pad_maximum_fusion.6), channel_id=1, source_target_pairs={{0,1},{1,0},{2,6},{3,7},{4,5},{5,4},{6,2},{7,3},{8,9},{9,8},{10,14... | collective-permute-start | bytes 6291464 | tf_op jit(solution)/shard_map/ppermute | solution.py:466
  404.1 41.4 %collective-permute-start.9 = (bf16[2,4,32,2560]{3,2,1,0:T(8,128)(2,1)}, bf16[2,4,32,2560]{3,2,1,0:T(8,128)(2,1)}, u32[]{:S(2)}, u32[]{:S(2)}) collective-permute-start(bf16[2,4,32,2560]{3,2,1,0:T(8,128)(2,1)} %pad_maximum_fusion.11), channel_id=1, source_target_pairs={{0,1},{1,0},{2,6},{3,7},{4,5},{5,4},{6,2},{7,3},{8,9},{9,8},{10,14... | collective-permute-start | bytes 3932168 | tf_op jit(solution)/shard_map/ppermute | solution.py:466
  408.4 37.1 %collective-permute-start.8 = (bf16[4,32,4096]{2,1,0:T(8,128)(2,1)}, bf16[4,32,4096]{2,1,0:T(8,128)(2,1)}, u32[]{:S(2)}, u32[]{:S(2)}) collective-permute-start(bf16[4,32,4096]{2,1,0:T(8,128)(2,1)} %get-tuple-element.245), channel_id=1, source_target_pairs={{0,4},{1,5},{2,3},{3,2},{4,0},{5,1},{6,7},{7,6},{8,12},{9,13},{10,... | collective-permute-start | bytes 3145736 | tf_op jit(solution)/shard_map/ppermute | solution.py:469
  408.7 36.7 %collective-permute-start.7 = (bf16[1,32,2048]{2,1,0:T(8,128)(2,1)S(1)}, bf16[1,32,2048]{2,1,0:T(8,128)(2,1)S(1)}, u32[]{:S(2)}, u32[]{:S(2)}) collective-permute-start(bf16[1,32,2048]{2,1,0:T(8,128)(2,1)S(1)} %fusion.101), channel_id=1, source_target_pairs={{0,16},{1,17},{2,18},{3,19},{4,20},{5,21},{6,22},{7,23},{8,24},{9,... | collective-permute-start | bytes 393224 | tf_op jit(solution)/shard_map/ppermute | solution.py:422
  468.4 10.1 %collective-permute-start.10 = (bf16[2,32,4096]{2,1,0:T(8,128)(2,1)S(1)}, bf16[2,32,4096]{2,1,0:T(8,128)(2,1)S(1)}, u32[]{:S(2)}, u32[]{:S(2)}) collective-permute-start(bf16[2,32,4096]{2,1,0:T(8,128)(2,1)S(1)} %get-tuple-element.261), channel_id=1, source_target_pairs={{0,8},{1,9},{2,10},{3,11},{4,12},{5,13},{6,14},{7,15},{8,0},{9,1},... | collective-permute-start | bytes 1572872 | tf_op jit(solution)/shard_map/ppermute | solution.py:422
  491.1 51.3 %collective-permute-start.14 = (bf16[8,64,3072]{2,1,0:T(8,128)(2,1)}, bf16[8,64,3072]{2,1,0:T(8,128)(2,1)}, u32[]{:S(2)}, u32[]{:S(2)}) collective-permute-start(bf16[8,64,3072]{2,1,0:T(8,128)(2,1)} %get-tuple-element.234), channel_id=1, source_target_pairs={{0,2},{1,3},{2,0},{3,1},{4,6},{5,7},{6,4},{7,5},{8,10},{9,11},{10,... | collective-permute-start | bytes 9437192 | tf_op jit(solution)/shard_map/ppermute | solution.py:422
  496.4 46.0 %collective-permute-start.12 = (bf16[1,32,4096]{2,1,0:T(8,128)(2,1)}, bf16[1,32,4096]{2,1,0:T(8,128)(2,1)S(1)}, u32[]{:S(2)}, u32[]{:S(2)}) collective-permute-start(bf16[1,32,4096]{2,1,0:T(8,128)(2,1)} %fusion.85), channel_id=1, source_target_pairs={{0,16},{1,17},{2,18},{3,19},{4,20},{5,21},{6,22},{7,23},{8,24},{9,... | collective-permute-start | bytes 786440 | tf_op jit(solution)/shard_map/ppermute | solution.py:422
  497.8 44.6 %collective-permute-start.13 = (bf16[2,32,2560]{2,1,0:T(8,128)(2,1)S(1)}, bf16[2,32,2560]{2,1,0:T(8,128)(2,1)S(1)}, u32[]{:S(2)}, u32[]{:S(2)}) collective-permute-start(bf16[2,32,2560]{2,1,0:T(8,128)(2,1)S(1)} %get-tuple-element.273), channel_id=1, source_target_pairs={{0,8},{1,9},{2,10},{3,11},{4,12},{5,13},{6,14},{7,15},{8,0},{9,1},... | collective-permute-start | bytes 983048 | tf_op jit(solution)/shard_map/ppermute | solution.py:422
  573.8 15.5 %collective-permute-start.15 = (bf16[1,32,2560]{2,1,0:T(8,128)(2,1)}, bf16[1,32,2560]{2,1,0:T(8,128)(2,1)}, u32[]{:S(2)}, u32[]{:S(2)}) collective-permute-start(bf16[1,32,2560]{2,1,0:T(8,128)(2,1)} %fusion.98), channel_id=1, source_target_pairs={{0,16},{1,17},{2,18},{3,19},{4,20},{5,21},{6,22},{7,23},{8,24},{9,... | collective-permute-start | bytes 491528 | tf_op jit(solution)/shard_map/ppermute | solution.py:422
  576.6 19.9 %collective-permute-start.16 = (bf16[2,4,32,3072]{3,2,1,0:T(8,128)(2,1)}, bf16[2,4,32,3072]{3,2,1,0:T(8,128)(2,1)}, u32[]{:S(2)}, u32[]{:S(2)}) collective-permute-start(bf16[2,4,32,3072]{3,2,1,0:T(8,128)(2,1)} %pad_maximum_fusion.10), channel_id=1, source_target_pairs={{0,1},{1,0},{2,6},{3,7},{4,5},{5,4},{6,2},{7,3},{8,9},{9,8},{10,14... | collective-permute-start | bytes 4718600 | tf_op jit(solution)/shard_map/ppermute | solution.py:466
  603.5 15.4 %collective-permute-start.18 = (bf16[8,64,1920]{2,1,0:T(8,128)(2,1)S(1)}, bf16[8,64,1920]{2,1,0:T(8,128)(2,1)S(1)}, u32[]{:S(2)}, u32[]{:S(2)}) collective-permute-start(bf16[8,64,1920]{2,1,0:T(8,128)(2,1)S(1)} %get-tuple-element.255), channel_id=1, source_target_pairs={{0,2},{1,3},{2,0},{3,1},{4,6},{5,7},{6,4},{7,5},{8,10},{9,11},{10,... | collective-permute-start | bytes 5898248 | tf_op jit(solution)/shard_map/ppermute | solution.py:422
  607.6 11.2 %collective-permute-start.17 = (bf16[4,32,3072]{2,1,0:T(8,128)(2,1)S(1)}, bf16[4,32,3072]{2,1,0:T(8,128)(2,1)S(1)}, u32[]{:S(2)}, u32[]{:S(2)}) collective-permute-start(bf16[4,32,3072]{2,1,0:T(8,128)(2,1)S(1)} %get-tuple-element.257), channel_id=1, source_target_pairs={{0,4},{1,5},{2,3},{3,2},{4,0},{5,1},{6,7},{7,6},{8,12},{9,13},{10,... | collective-permute-start | bytes 2359304 | tf_op jit(solution)/shard_map/ppermute | solution.py:469
  620.5 13.6 %collective-permute-start.20 = (bf16[2,4,32,1920]{3,2,1,0:T(8,128)(2,1)}, bf16[2,4,32,1920]{3,2,1,0:T(8,128)(2,1)}, u32[]{:S(2)}, u32[]{:S(2)}) collective-permute-start(bf16[2,4,32,1920]{3,2,1,0:T(8,128)(2,1)} %pad_maximum_fusion.13), channel_id=1, source_target_pairs={{0,1},{1,0},{2,6},{3,7},{4,5},{5,4},{6,2},{7,3},{8,9},{9,8},{10,14... | collective-permute-start | bytes 2949128 | tf_op jit(solution)/shard_map/ppermute | solution.py:466
  622.4 11.6 %collective-permute-start.19 = (bf16[2,32,3072]{2,1,0:T(8,128)(2,1)}, bf16[2,32,3072]{2,1,0:T(8,128)(2,1)S(1)}, u32[]{:S(2)}, u32[]{:S(2)}) collective-permute-start(bf16[2,32,3072]{2,1,0:T(8,128)(2,1)} %get-tuple-element.271), channel_id=1, source_target_pairs={{0,8},{1,9},{2,10},{3,11},{4,12},{5,13},{6,14},{7,15},{8,0},{9,1},... | collective-permute-start | bytes 1179656 | tf_op jit(solution)/shard_map/ppermute | solution.py:422
  654.7 17.6 %collective-permute-start.21 = (bf16[1,32,3072]{2,1,0:T(8,128)(2,1)}, bf16[1,32,3072]{2,1,0:T(8,128)(2,1)S(1)}, u32[]{:S(2)}, u32[]{:S(2)}) collective-permute-start(bf16[1,32,3072]{2,1,0:T(8,128)(2,1)} %fusion.95), channel_id=1, source_target_pairs={{0,16},{1,17},{2,18},{3,19},{4,20},{5,21},{6,22},{7,23},{8,24},{9,... | collective-permute-start | bytes 589832 | tf_op jit(solution)/shard_map/ppermute | solution.py:422
  656.3 12.2 %collective-permute-start.29 = (f32[104,128]{1,0:T(8,128)S(1)}, f32[104,128]{1,0:T(8,128)S(1)}, u32[]{:S(2)}, u32[]{:S(2)}) collective-permute-start(f32[104,128]{1,0:T(8,128)S(1)} %add.722), channel_id=1, source_target_pairs={{0,16},{1,17},{2,18},{3,19},{4,20},{5,21},{6,22},{7,23},{8,24},{9,... | collective-permute-start | bytes 159752 | tf_op jit(solution)/shard_map/ppermute | solution.py:422
  659.3 13.0 %collective-permute-start.22 = (bf16[4,32,1920]{2,1,0:T(8,128)(2,1)S(1)}, bf16[4,32,1920]{2,1,0:T(8,128)(2,1)S(1)}, u32[]{:S(2)}, u32[]{:S(2)}) collective-permute-start(bf16[4,32,1920]{2,1,0:T(8,128)(2,1)S(1)} %get-tuple-element.269), channel_id=1, source_target_pairs={{0,4},{1,5},{2,3},{3,2},{4,0},{5,1},{6,7},{7,6},{8,12},{9,13},{10,... | collective-permute-start | bytes 1474568 | tf_op jit(solution)/shard_map/ppermute | solution.py:469
  (121 other events, 2728.8 us)
Sparse Core Ops, SparseCore 0:
  11.5 88.0 all-gather.2
  103.1 118.3 all-gather.4

commit v4 on v3

--- a/solution.py
+++ b/solution.py
@@ -129,8 +129,8 @@
 
 
 def scan_bwd_kernel(
-    x_ref, b_ref, c_ref, ld_ref, st_ref, states_ref, dy_ref,
-    dx_ref, db_ref, dc_ref, dst_ref, dld_ref, dstate, grow, gcol,
+    x_ref, b_ref, c_ref, ld_ref, st_ref, states_ref, dy_ref, skip_ref,
+    dx_ref, dst_ref, dld_ref, dskip_ref, dstate, grow, gcol,
 ):
     spread = head_spread()
     gather = head_gather()
@@ -140,6 +140,7 @@
         dstate[...] = jnp.zeros_like(dstate)
         grow[...] = jnp.zeros_like(grow)
         gcol[...] = jnp.zeros_like(gcol)
+        dskip_ref[...] = jnp.zeros_like(dskip_ref)
 
     st, cum, cum_t, st_t, doc, doc_row, carried, gap, keep = block_terms(ld_ref, st_ref, spread)
     rows = iota2((SPAN, SPAN), 0)
@@ -174,7 +175,9 @@
             gcol[:, h : h + 1] = jnp.sum(products, axis=1, keepdims=True)
             grow[h : h + 1, :] = jnp.sum(products * step, axis=0, keepdims=True)
         inside = mm(jnp.concatenate(mats, axis=1), split_pair(dy_low[:, lo:hi]))
+        inside = inside + skip_ref[:, lo:hi] * dy[:, lo:hi]
         dx_ref[:, lo:hi] = inside + from_tail[:, lo:hi] * tail_wide[:, lo:hi]
+    dskip_ref[0:1, :] += jnp.sum(dy * x_blk.astype(f32), axis=0, keepdims=True)
     flowing = dy * carried_wide
     flowing_low = flowing.astype(bf16)
     d_cum = split_mm(flowing * mm(c_blk, old_low), gather)
@@ -189,8 +192,8 @@
     dld_ref[...] = exact_mm(jnp.where(cols >= rows, 1.0, 0.0), d_cum)
     d_aff_low = d_aff.astype(bf16)
     pushed = (x_blk.astype(f32) * tail_wide).astype(bf16)
-    dc_ref[...] = mm_tn(d_aff_low, b_blk) + mm_nt(flowing_low, old_low)
-    db_ref[...] = mm(d_aff_low, c_blk) + mm_nt(pushed, d_new_low)
+    dx_ref[:, D_SSM + STATE :] = mm_tn(d_aff_low, b_blk) + mm_nt(flowing_low, old_low)
+    dx_ref[:, D_SSM : D_SSM + STATE] = mm(d_aff_low, c_blk) + mm_nt(pushed, d_new_low)
     dstate[...] = d_new * keep_wide + mm_tn(c_blk, flowing_low)
 
 
@@ -220,7 +223,7 @@
     )(act_low, act_low, act_low, ld, st)
 
 
-def scan_bwd(act_low, ld, st, states, dy):
+def scan_bwd(act_low, ld, st, states, dy, skip):
     length = act_low.shape[0]
     blocks = length // SPAN
     end = blocks - 1
@@ -235,20 +238,19 @@
             pl.BlockSpec((SPAN, 128), lambda i: (end - i, 0)),
             pl.BlockSpec((1, STATE, D_SSM), lambda i: (end - i, 0, 0)),
             pl.BlockSpec((SPAN, D_SSM), lambda i: (end - i, 0)),
+            pl.BlockSpec((1, D_SSM), lambda i: (0, 0)),
         ],
         out_specs=[
-            pl.BlockSpec((SPAN, D_SSM), lambda i: (end - i, 0)),
-            pl.BlockSpec((SPAN, STATE), lambda i: (end - i, 0)),
-            pl.BlockSpec((SPAN, STATE), lambda i: (end - i, 0)),
+            pl.BlockSpec((SPAN, CONV_CH), lambda i: (end - i, 0)),
             pl.BlockSpec((SPAN, 128), lambda i: (end - i, 0)),
             pl.BlockSpec((SPAN, 128), lambda i: (end - i, 0)),
+            pl.BlockSpec((8, D_SSM), lambda i: (0, 0)),
         ],
         out_shape=[
-            jax.ShapeDtypeStruct((length, D_SSM), f32),
-            jax.ShapeDtypeStruct((length, STATE), f32),
-            jax.ShapeDtypeStruct((length, STATE), f32),
+            jax.ShapeDtypeStruct((length, CONV_CH), f32),
             jax.ShapeDtypeStruct((length, 128), f32),
             jax.ShapeDtypeStruct((length, 128), f32),
+            jax.ShapeDtypeStruct((8, D_SSM), f32),
         ],
         scratch_shapes=[
             pltpu.VMEM((STATE, D_SSM), f32),
@@ -256,7 +258,7 @@
             pltpu.VMEM((SPAN, SPAN), f32),
         ],
         compiler_params=pltpu.CompilerParams(vmem_limit_bytes=40 * 2**20),
-    )(act_low, act_low, act_low, ld, st, states, dy)
+    )(act_low, act_low, act_low, ld, st, states, dy, skip)
 
 
 def key_span(block):
@@ -380,14 +382,138 @@
     )(query, key, value, d_out, lse, doc_col, doc_row)
 
 
+LANES = 128
+CONV_BLOCKS = CONV_CH // LANES
+
+
+def conv_shifts(values, mask_ref, taps):
+    shifts = [values]
+    for offset in range(1, taps):
+        allowed = jnp.broadcast_to(mask_ref[:, offset : offset + 1], values.shape)
+        shifts.append(jnp.where(allowed > 0.0, pltpu.roll(values, offset, 0), 0.0))
+    return shifts
+
+
+def conv_sum(shifts, weight_ref, bias_ref):
+    total = bias_ref[...]
+    for offset, shifted in enumerate(shifts):
+        total = total + weight_ref[offset : offset + 1, :] * shifted
+    return total
+
+
+def conv_fwd_kernel(x_ref, mask_ref, weight_ref, bias_ref, act_ref):
+    total = conv_sum(conv_shifts(x_ref[...], mask_ref, weight_ref.shape[0]), weight_ref, bias_ref)
+    act_ref[...] = (total * jax.nn.sigmoid(total)).astype(bf16)
+
+
+def conv_bwd_kernel(
+    x_ref, d_act_ref, d_raw_ref, mask_ref, weight_ref, bias_ref, out_ref, small_ref
+):
+    step = pl.program_id(0)
+    length = x_ref.shape[0]
+
+    @pl.when(step == CONV_BLOCKS)
+    def _():
+        out_ref[...] = d_raw_ref[...]
+
+    @pl.when(step < CONV_BLOCKS)
+    def _():
+        shifts = conv_shifts(x_ref[...], mask_ref, weight_ref.shape[0])
+        total = conv_sum(shifts, weight_ref, bias_ref)
+        gate = jax.nn.sigmoid(total)
+        d_total = d_act_ref[...] * (gate * (1.0 + total * (1.0 - gate)))
+        small_ref[...] = jnp.zeros_like(small_ref)
+        small_ref[0:1, :] = jnp.sum(d_total, axis=0, keepdims=True)
+        d_in = weight_ref[0:1, :] * d_total
+        for offset, shifted in enumerate(shifts):
+            small_ref[offset + 1 : offset + 2, :] = jnp.sum(d_total * shifted, axis=0, keepdims=True)
+            if offset:
+                allowed = jnp.broadcast_to(mask_ref[:, offset : offset + 1], d_total.shape)
+                masked = jnp.where(allowed > 0.0, d_total, 0.0)
+                later = pltpu.roll(masked, length - offset, 0)
+                d_in = d_in + weight_ref[offset : offset + 1, :] * later
+        out_ref[...] = d_in.astype(bf16)
+
+
+def conv_fwd(proj, first, masks, weight, bias):
+    length, taps = masks.shape
+    return pl.pallas_call(
+        conv_fwd_kernel,
+        grid=(CONV_BLOCKS,),
+        in_specs=[
+            pl.BlockSpec((length, LANES), lambda i: (0, first + i)),
+            pl.BlockSpec((length, taps), lambda i: (0, 0)),
+            pl.BlockSpec((taps, LANES), lambda i: (0, i)),
+            pl.BlockSpec((1, LANES), lambda i: (0, i)),
+        ],
+        out_specs=pl.BlockSpec((length, LANES), lambda i: (0, i)),
+        out_shape=jax.ShapeDtypeStruct((length, CONV_CH), bf16),
+        compiler_params=pltpu.CompilerParams(vmem_limit_bytes=40 * 2**20),
+    )(proj, masks, weight, bias)
+
+
+def conv_bwd(proj, first, d_act, d_raw, masks, weight, bias):
+    length, taps = masks.shape
+    end = CONV_BLOCKS - 1
+    return pl.pallas_call(
+        conv_bwd_kernel,
+        grid=(CONV_BLOCKS + 1,),
+        in_specs=[
+            pl.BlockSpec((length, LANES), lambda i: (0, first + jnp.minimum(i, end))),
+            pl.BlockSpec((length, LANES), lambda i: (0, jnp.minimum(i, end))),
+            pl.BlockSpec((length, LANES), lambda i: (0, 0)),
+            pl.BlockSpec((length, taps), lambda i: (0, 0)),
+            pl.BlockSpec((taps, LANES), lambda i: (0, jnp.minimum(i, end))),
+            pl.BlockSpec((1, LANES), lambda i: (0, jnp.minimum(i, end))),
+        ],
+        out_specs=[
+            pl.BlockSpec((length, LANES), lambda i: (0, i)),
+            pl.BlockSpec((8, LANES), lambda i: (0, jnp.minimum(i, end))),
+        ],
+        out_shape=[
+            jax.ShapeDtypeStruct((length, CONV_CH + LANES), bf16),
+            jax.ShapeDtypeStruct((8, CONV_CH), f32),
+        ],
+        compiler_params=pltpu.CompilerParams(vmem_limit_bytes=40 * 2**20),
+    )(proj, d_act, d_raw, masks, weight, bias)
+
+
+def units_bwd_kernel(cot_ref, down_ref, both_ref, out_ref):
+    units = down_ref.shape[1]
+    d_hidden = mm(cot_ref[...], down_ref[...])
+    gate = both_ref[:, :units]
+    sigmoid = jax.nn.sigmoid(gate)
+    slope = sigmoid * (1.0 + gate * (1.0 - sigmoid))
+    out_ref[:, :units] = (d_hidden * both_ref[:, units:] * slope).astype(bf16)
+    out_ref[:, units:] = (d_hidden * (gate * sigmoid)).astype(bf16)
+
+
+def units_bwd(cot, weights, both):
+    length, width = cot.shape
+    units = both.shape[1] // 2
+    rows = 128
+    return pl.pallas_call(
+        units_bwd_kernel,
+        grid=(length // rows,),
+        in_specs=[
+            pl.BlockSpec((rows, width), lambda i: (i, 0)),
+            pl.BlockSpec((width, units), lambda i: (0, 0)),
+            pl.BlockSpec((rows, 2 * units), lambda i: (i, 0)),
+        ],
+        out_specs=pl.BlockSpec((rows, 2 * units), lambda i: (i, 0)),
+        out_shape=jax.ShapeDtypeStruct((length, 2 * units), bf16),
+        compiler_params=pltpu.CompilerParams(vmem_limit_bytes=40 * 2**20),
+    )(cot, weights, both)
+
+
 def inv_norm(values):
     return lax.rsqrt(jnp.mean(values * values, axis=-1, keepdims=True) + eps)
 
 
-def norm_back(normed_grad, gain, values, inv):
+def norm_back(normed_grad, gain, values, inv, tie=lambda mean: mean):
     unit = values * inv
     scaled = normed_grad * gain
-    back = inv * (scaled - unit * jnp.mean(scaled * unit, axis=-1, keepdims=True))
+    back = inv * (scaled - unit * tie(jnp.mean(scaled * unit, axis=-1, keepdims=True)))
     return back, jnp.sum(normed_grad * unit, axis=0)
 
 
@@ -527,12 +653,12 @@
     w_first = gather(
         (w_in[:, :D_SSM], w_query, w_key, w_value, w_in[:, D_SSM:conv_end], w_in[:, conv_end:], dt_pad)
     )
-    w_later = gather((w_attn_out.T, w_out.T, w_gate, w_up, w_down.T))
-    second_end = w_attn_out.shape[0] + w_out.shape[0]
-    third_end = second_end + 2 * w_gate.shape[1]
-    w_second = w_later[:, :second_end]
-    w_third = w_later[:, second_end:third_end]
-    w_fourth = w_later[:, third_end:]
+    w_later = gather((w_down.T, w_gate, w_up, w_attn_out.T, w_out.T))
+    fourth_end = w_down.shape[0]
+    third_end = fourth_end + 2 * w_gate.shape[1]
+    w_fourth = w_later[:, :fourth_end]
+    w_third = w_later[:, fourth_end:third_end]
+    w_second = w_later[:, third_end:]
 
     stream = tokens[0].astype(f32)
     doc_ids = segments[0]
@@ -545,7 +671,6 @@
     q_at, k_at, v_at = D_SSM, D_SSM + HEADS * HEAD_DIM, D_SSM + (HEADS + KV_HEADS) * HEAD_DIM
     conv_at = D_SSM + QKV
     dt_at = conv_at + CONV_CH
-    conv_in = proj[:, conv_at:dt_at]
     cosine, sine = angles(length)
     query = turn(proj[:, q_at:k_at], cosine, sine).astype(bf16)
     key = turn(proj[:, k_at:v_at], cosine, sine).astype(bf16)
@@ -555,13 +680,9 @@
     attended, lse = attend_fwd(query, key, value, doc_col, doc_row)
 
     taps = conv_weight.shape[0]
-    convolved = conv_bias[None, :] + conv_weight[0][None, :] * conv_in
-    for offset in range(1, taps):
-        shifted = jnp.pad(conv_in, ((offset, 0), (0, 0)))[:length]
-        convolved = convolved + jnp.where(
-            same_doc(doc_ids, offset), conv_weight[offset][None, :] * shifted, 0.0
-        )
-    act_low = jax.nn.silu(convolved).astype(bf16)
+    masks = jnp.concatenate([same_doc(doc_ids, offset) for offset in range(taps)], axis=1).astype(f32)
+    conv_bias_row = conv_bias[None, :]
+    act_low = conv_fwd(proj, conv_at // LANES, masks, conv_weight, conv_bias_row)
     x_heads = act_low[:, :D_SSM]
     raw = proj[:, dt_at : dt_at + M_HEADS] + dt_bias
     step_size = jax.nn.softplus(raw)
@@ -592,20 +713,16 @@
     mixed = (resid + mm_nt(hidden, w_fourth)).astype(bf16)
 
     sums = Sums()
-    d_hidden = mm(cot, w_fourth)
     sums.start("fourth", mm_tn(cot, hidden))
-    d_both = jnp.concatenate(
-        [(d_hidden * up * silu_slope(gate)).astype(bf16), (d_hidden * jax.nn.silu(gate)).astype(bf16)],
-        axis=1,
-    )
+    d_both = units_bwd(cot, w_later, both)
     d_both = sums.step(d_both)
     sums.start("third", mm_tn(mid_in, d_both))
-    d_mid = sums.step(mm_nt(d_both, w_third), "fourth")
-    back, g_norm_mid = norm_back(d_mid, norm_mid, resid, inv_mid)
-    d_resid = sums.step(cot.astype(f32) + back)
+    d_mid = mm_nt(d_both, w_third)
+    back, g_norm_mid = norm_back(d_mid, norm_mid, resid, inv_mid, sums.step)
+    d_resid = cot.astype(f32) + back
     d_resid_low = d_resid.astype(bf16)
     sums.start("second", mm_tn(d_resid_low, branches))
-    d_branches = sums.step(mm(d_resid_low, w_second))
+    d_branches = sums.step(mm(d_resid_low, w_second), "fourth", "second")
     attn_width = HEADS * HEAD_DIM
     d_query, d_key, d_value = attend_bwd(
         query, key, value, d_branches[:, :attn_width], lse, doc_col, doc_row
@@ -624,35 +741,26 @@
     )
     d_ssm, d_first = sums.step((d_ssm, d_first))
     sums.start("first", mm_tn(normed, d_first))
-    g_skip = jnp.sum(jnp.sum(d_ssm * x_heads.astype(f32), axis=0).reshape(M_HEADS, M_HDIM), axis=1)
-    d_x, d_b, d_c, d_st, d_ld = scan_bwd(act_low, ld, st, states, d_ssm)
-    d_x = sums.step(d_x)
-    d_act = jnp.concatenate([d_x + skip_wide * d_ssm, d_b, d_c], axis=1)
-    d_conv = d_act * silu_slope(convolved)
-    g_conv_bias = jnp.sum(d_conv, axis=0)
-    d_conv_in = conv_weight[0][None, :] * d_conv
-    g_taps = [jnp.sum(d_conv * conv_in, axis=0)]
-    for offset in range(1, taps):
-        masked = jnp.where(same_doc(doc_ids, offset), d_conv, 0.0)
-        shifted = jnp.pad(conv_in, ((offset, 0), (0, 0)))[:length]
-        g_taps.append(jnp.sum(masked * shifted, axis=0))
-        later = jnp.pad(masked, ((0, offset), (0, 0)))[offset:]
-        d_conv_in = d_conv_in + conv_weight[offset][None, :] * later
-    d_conv_in = sums.step(d_conv_in)
-    g_conv_weight = jnp.stack(g_taps)
+    d_act, d_st, d_ld, g_skip_wide = scan_bwd(act_low, ld, st, states, d_ssm, skip_wide)
+    g_skip = jnp.sum(g_skip_wide[0].reshape(M_HEADS, M_HDIM), axis=1)
+    d_st = sums.step(d_st)
     d_ld = d_ld[:, :M_HEADS]
     d_step = d_st[:, :M_HEADS] - d_ld * jnp.exp(a_log)
     g_a_log = jnp.sum(d_ld * log_decay, axis=0)
     d_raw = d_step * jax.nn.sigmoid(raw)
     g_dt_bias = jnp.sum(d_raw, axis=0)
-    d_last = jnp.concatenate(
-        [d_conv_in.astype(bf16), jnp.pad(d_raw, ((0, 0), (0, 128 - M_HEADS))).astype(bf16)], axis=1
+    d_raw_low = jnp.pad(d_raw.astype(bf16), ((0, 0), (0, LANES - M_HEADS)))
+    d_last, g_conv = conv_bwd(
+        proj, conv_at // LANES, d_act, d_raw_low, masks, conv_weight, conv_bias_row
     )
+    g_conv_bias, g_conv_weight = g_conv[0], g_conv[1 : taps + 1]
+    d_last = sums.step(d_last)
     sums.start("last", mm_tn(normed, d_last))
-    d_normed = sums.step(mm_nt(d_first, w_first[:, :conv_at]))
-    d_normed = sums.step(d_normed + mm_nt(d_last, w_first[:, conv_at:]))
-    back, g_norm_in = norm_back(d_normed, norm_in, stream, inv_in)
-    grad_tokens = sums.step(d_resid + back)
+    d_normed = mm_nt(d_first, w_first[:, :conv_at])
+    d_last = sums.step(d_last)
+    d_normed = d_normed + mm_nt(d_last, w_first[:, conv_at:])
+    back, g_norm_in = norm_back(d_normed, norm_in, stream, inv_in, sums.step)
+    grad_tokens = d_resid + back
     while sums.flying:
         sums.step(())
     sum_first, sum_last = sums.sums["first"], sums.sums["last"]

time: 705 us -> 654 us (0.928)
  other arithmetic: 175 us -> 110 us
  Pallas kernels: 90.2 us -> 138 us
  matrix products: 148 us -> 132 us
  local copies, waits for them, and re-layouts: 98.6 us -> 89.7 us
  starting transfers between devices: 33 us -> 25.9 us
    pallas_call x0 -> x3, Pallas kernels: none -> 47.1 us  [the longest x1 22.1 us: conv_bwd(): pl.pallas_call(conv_bwd_kernel, grid=(CONV_BLOCKS + 1,), in_specs=[pl.Blo...]
    reduce_sum x4 -> x1, other arithmetic: 23.6 us -> 0.12 us  [shards(): g_skip = jnp.sum(g_skip_wide[0].reshape(M_HEADS, M_HDIM), axis=1)]
    add x4 -> x1, other arithmetic: 23.2 us -> 1.27 us  [shards(): d_resid = cot.astype(f32) + back]
    ppermute x5, waiting for transfers between devices: 21 us -> 0.01 us  [scatter_steps(): other = (yield lax.ppermute(sent, AXES, crossing))]
    dot_general x4 -> x3, matrix products: 55.3 us -> 37.9 us  [mm(): return jnp.dot(left, right, preferred_element_type=f32)]
    convert_element_type x1 -> x2, other arithmetic: 19.2 us -> 3.85 us  [the longest x1 3.02 us: shards(): hidden = (jax.nn.silu(gate) * up).astype(bf16)]
    ppermute x20, waiting for transfers between devices: 17.6 us -> 32.5 us  [flip(): return lax.ppermute(values, AXES, [(i, i ^ bit) for i in range(places)])]
    optimization_barrier x2 -> x0, local copies, waits for them, and re-layouts: 11 us -> none  [step(): lax.optimization_barrier((anchor, tuple((self.flying[name][1] for name in...]
  transfers between devices with their start and end apart: 32 -> 32, of which waited for: 14 -> 13; matrix products, arithmetic and copies ran while one was open for 37% -> 27% of each run, Pallas kernels for 13% -> 21%
where the time goes in v4:
time: 654 us; the launch traced here: 643 us
  Pallas kernels  138 us (21%)
  matrix products  132 us (20%)
  waiting for transfers between devices  126 us (19%)
  other arithmetic  110 us (17%)
  local copies, waits for them, and re-layouts  89.7 us (14%)
  starting transfers between devices  25.9 us (4%)
  between operations  21.1 us (3%)
    all_gather x2, waiting for transfers between devices, gather(): lax.all_gather(jnp.concatenate(parts, axis=1), AXES, axis=0, tiled=True)  85.1 us
    dot_general x5, matrix products, mm_nt(): return lax.dot_general(left, right, NT, preferred_element_type=f32)  52.6 us
    unnamed x225, local copies, waits for them, and re-layouts  42.2 us
    dot_general x5, matrix products, mm_tn(): return lax.dot_general(left, right, TN, preferred_element_type=f32)  41.4 us
    dot_general x3, matrix products, mm(): return jnp.dot(left, right, preferred_element_type=f32)  37.9 us
    pallas_call x1, Pallas kernels, scan_bwd(): pl.pallas_call(scan_bwd_kernel, grid=(blocks,), in_specs=[pl.BlockSpec((S...  32.5 us
    ppermute x20, waiting for transfers between devices, flip(): return lax.ppermute(values, AXES, [(i, i ^ bit) for i in range(places)])  32.5 us
    another operation x15, other arithmetic, along(): jnp.stack([pick(jnp.where(core == 0, second, first), jnp.where(core == 0,...  31.7 us
  transfers between devices with their start and end apart: 32, of which 13 were waited for; matrix products, arithmetic and copies ran while one was open for 27% of the time, Pallas kernels for 21%

profile of v4, /device:TPU:1, one launch (start us, length us, event | category | flops | bytes accessed | tf_op | source)
XLA Modules:
  0.0 642.6 jit_solution(1684675391412472780)
XLA Ops:
  30.7 68.9 %all-gather.3.cloned.1.call-done = bf16[1024,4992]{1,0:T(8,128)(2,1)} async-done(((bf16[32,4992]{1,0:T(8,128)(2,1)}), bf16[1024,4992]{1,0:T(8,128)(2,1)}) %all-gather.3.cloned.1.call-update) | async-done | bytes 10223632 | tf_op jit(solution)/shard_map/all_gather | solution.py:641
  99.6 17.6 %fusion.100.x_ref = f32[1024,4992]{1,0:T(8,128)} fusion(bf16[1024,4992]{1,0:T(8,128)(2,1)} %all-gather.3.cloned.1.call-done, bf16[1,1024,1024]{2,1,0:T(8,128)(2,1)S(1)} %copy-done.40, f32[1024]{0:T(1024)S(1)} %copy-done.92, f32[1024]{0:T(1024)S(1)} %add_rsqrt_fusion.2), kind=kOutput, calls=%fused_computation.259 | convolution fusion | flops 10473177088 | bytes 32776192 | tf_op jit(solution)/shard_map/dot_general | solution.py:36
  137.1 12.4 %shard_map.340.x_ref.b_ref.c_ref = bf16[1024,1792]{1,0:T(8,128)(2,1)S(1)} custom-call(f32[1024,4992]{1,0:T(8,128)} %fusion.100.x_ref, f32[1024,4]{1,0:T(8,128)S(1)} %copy-done.15, f32[4,1792]{1,0:T(4,128)S(1)} %copy-done.22, f32[1,1792]{1,0:T(1,128)S(1)} %broadcast_in_dim.29.bias_ref), custom_call_target="tpu_custom_call" | custom-call | tf_op jit(solution)/shard_map/pallas_call | solution.py:440
  151.3 20.3 %shard_map.339 = (bf16[1024,1024]{1,0:T(8,128)(2,1)S(1)}, f32[8,1,1024]{2,1,0:T(1,128)S(1)}) custom-call(bf16[1024,1024]{1,0:T(8,128)(2,1)S(1)} %bitcast.297, bf16[1024,256]{1,0:T(8,128)(2,1)S(1)} %bitcast.300, bf16[1024,256]{1,0:T(8,128)(2,1)S(1)} %copy-done.11, f32[1024,1]{1,0:T(8,128)S(1)} %copy.132.doc_col_ref, f32[1,1024]{1,0:T(1,128)S(1)} %get-tuple-element.192.doc_row_ref), custom_call_target="tpu_custom_call" | custom-call | tf_op jit(solution)/shard_map/pallas_call | solution.py:333
  179.5 13.2 %shard_map.341 = (f32[1024,1536]{1,0:T(8,128)S(1)}, bf16[8,128,1536]{2,1,0:T(8,128)(2,1)S(1)}) custom-call(bf16[1024,1792]{1,0:T(8,128)(2,1)S(1)} %copy-done.1, bf16[1024,1792]{1,0:T(8,128)(2,1)S(1)} %copy-done.1, bf16[1024,1792]{1,0:T(8,128)(2,1)S(1)} %copy-done.1, f32[1024,128]{1,0:T(8,128)S(1)} %pad.27.ld_ref, f32[1024,128]{1,0:T(8,128)S(1)} %copy-done.9), custom_call_target="tpu_custom_call" | custom-call | tf_op jit(solution)/shard_map/pallas_call | solution.py:203
  192.8 7.4 %multiply_reduce_fusion.2 = (f32[1024]{0:T(1024)S(1)}, f32[1024,1536]{1,0:T(8,128)S(1)}) fusion(f32[1024,4992]{1,0:T(8,128)} %fusion.100.x_ref, f32[1024,1536]{1,0:T(8,128)S(1)} %get-tuple-element.67, bf16[1024,1792]{1,0:T(8,128)(2,1)S(1)} %copy-done.1, f32[1536]{0:T(1024)S(1)} %mul.474), kind=kLoop, calls=%fused_computation.22 | loop fusion | flops 15727616 | bytes 22030336 | tf_op jit(solution)/shard_map/reduce_sum | solution.py:510
  205.3 16.1 %all-gather.5.cloned.1.call-done.down_ref = bf16[1024,8704]{1,0:T(8,128)(2,1)} async-done(((bf16[32,8704]{1,0:T(8,128)(2,1)}), bf16[1024,8704]{1,0:T(8,128)(2,1)}) %all-gather.5.cloned.1.call-update) | async-done | bytes 17825808 | tf_op jit(solution)/shard_map/all_gather | solution.py:641
  221.5 10.9 %multiply_reduce_fusion.5 = (f32[1024]{0:T(1024)S(1)}, f32[1024,1024]{1,0:T(8,128)}) fusion(bf16[1024,8704]{1,0:T(8,128)(2,1)} %all-gather.5.cloned.1.call-done.down_ref, bf16[1024,1536]{1,0:T(8,128)(2,1)} %multiply_convert_fusion.1, bf16[1024,1024]{1,0:T(8,128)(2,1)} %copy-done.26, bf16[1,1024,1024]{2,1,0:T(8,128)(2,1)} %param.20), kind=kOutput, calls=%fused_computation.52 | convolution fusion | flops 5383388160 | bytes 16781312 | tf_op jit(solution)/shard_map/dot_general | solution.py:40
  232.3 12.6 %fusion.3.both_ref = f32[1024,4096]{1,0:T(8,128)S(1)} fusion(bf16[1024,8704]{1,0:T(8,128)(2,1)} %all-gather.5.cloned.1.call-done.down_ref, f32[1024,1024]{1,0:T(8,128)} %get-tuple-element.199, f32[1024]{0:T(1024)S(1)} %copy-done.91, f32[1024]{0:T(1024)S(1)} %add_rsqrt_fusion), kind=kOutput, calls=%fused_computation.5 | convolution fusion | flops 8593080320 | bytes 29368320 | tf_op jit(solution)/shard_map/dot_general | solution.py:36
  251.2 6.4 convolution_convert_fusion.4
  262.0 12.7 %shard_map.342 = bf16[1024,4096]{1,0:T(8,128)(2,1)S(1)} custom-call(bf16[1024,1024]{1,0:T(8,128)(2,1)S(1)} %bitcast.299, bf16[1024,8704]{1,0:T(8,128)(2,1)} %all-gather.5.cloned.1.call-done.down_ref, f32[1024,4096]{1,0:T(8,128)} %copy-done.29), custom_call_target="tpu_custom_call" | custom-call | tf_op jit(solution)/shard_map/pallas_call | solution.py:495
  274.7 13.1 %convolution_convert_fusion = bf16[1024,4096]{1,0:T(8,128)(2,1)S(1)} fusion(bf16[1024,4096]{1,0:T(8,128)(2,1)S(1)} %shard_map.342, f32[1024,1024]{1,0:T(8,128)} %get-tuple-element.199, f32[1024]{0:T(1024)S(1)} %copy-done.91, f32[1024]{0:T(1024)S(1)} %add_rsqrt_fusion), kind=kOutput, calls=%fused_computation.2 | convolution fusion | flops 8597274624 | bytes 20979712 | tf_op jit(solution)/shard_map/dot_general | solution.py:44
  302.2 14.5 %multiply_reduce_fusion.3 = (f32[1024]{0:T(1024)S(1)}, f32[1024]{0:T(1024)S(1)}, f32[1024,1024]{1,0:T(8,128)S(1)}) fusion(f32[1024,1024]{1,0:T(8,128)S(1)} %copy-done.50, f32[1024]{0:T(1024)S(1)} %add_rsqrt_fusion, f32[1024]{0:T(1024)S(1)} %copy-done.91, bf16[1024,4096]{1,0:T(8,128)(2,1)} %copy-done.5, ...), kind=kOutput, calls=%fused_computation.44 | convolution fusion | flops 8596224000 | bytes 25182208 | tf_op jit(solution)/shard_map/dot_general | solution.py:40
  339.1 7.7 %fusion.12 = f32[1024,2560]{1,0:T(8,128)S(1)} fusion(bf16[1024,8704]{1,0:T(8,128)(2,1)} %all-gather.5.cloned.1.call-done.down_ref, f32[1024,1024]{1,0:T(8,128)S(1)} %multiply_add_fusion.1), kind=kOutput, calls=%fused_computation.29 | convolution fusion | flops 5369757696 | bytes 19922944 | tf_op jit(solution)/shard_map/dot_general | solution.py:36
  356.1 24.7 %shard_map.343 = (f32[1024,1024]{1,0:T(8,128)S(1)}, f32[1024,256]{1,0:T(8,128)S(1)}, f32[1024,256]{1,0:T(8,128)S(1)}) custom-call(bf16[1024,1024]{1,0:T(8,128)(2,1)S(1)} %bitcast.298, bf16[1024,256]{1,0:T(8,128)(2,1)S(1)} %bitcast.301, bf16[1024,256]{1,0:T(8,128)(2,1)S(1)} %copy-done.12, f32[1024,1024]{1,0:T(8,128)S(1)} %slice.165.do_ref, ...), custom_call_target="tpu_custom_call" | custom-call | tf_op jit(solution)/shard_map/pallas_call | solution.py:362
  402.4 8.6 %multiply_convert_fusion = (bf16[1024,1536]{1,0:T(8,128)(2,1)S(1)}, f32[1024,1536]{1,0:T(8,128)}) fusion(f32[1024,4992]{1,0:T(8,128)} %fusion.100.x_ref, f32[1024,1536]{1,0:T(8,128)S(1)} %bitcast.296, f32[1024]{0:T(1024)S(1)} %broadcast_multiply_fusion, f32[1024,1536]{1,0:T(8,128)S(1)} %bitcast.306, f32[1024,2560]{1,0:T(8,128)S(1)} %copy-done.31, ...), kind=kLoop, calls=%fused_computation.18 | loop fusion | flops 31457280 | bytes 37769216 | tf_op jit(solution)/shard_map/convert_element_type | solution.py:735
  423.9 6.4 collective-permute-done.8
  438.3 8.4 %convolution_convert_fusion.1 = bf16[1024,3072]{1,0:T(8,128)(2,1)S(1)} fusion(bf16[1024,3072]{1,0:T(8,128)(2,1)S(1)} %pad_maximum_fusion, bf16[1,1024,1024]{2,1,0:T(8,128)(2,1)S(1)} %copy-done.41, f32[1024]{0:T(1024)S(1)} %copy-done.93, f32[1024]{0:T(1024)S(1)} %copy-done.90), kind=kOutput, calls=%fused_computation.26 | convolution fusion | flops 6449790976 | bytes 14688256 | tf_op jit(solution)/shard_map/dot_general | solution.py:44
  451.6 10.7 %fusion.30 = bf16[1,1024,1024]{2,1,0:T(8,128)(2,1)} fusion(f32[1024,1024]{1,0:T(8,128)} %get-tuple-element.199, bf16[1024,2048]{1,0:T(8,128)(2,1)} %copy-done.48, bf16[1024,8704]{1,0:T(8,128)(2,1)} %all-gather.5.cloned.1.call-done.down_ref), kind=kOutput, calls=%fused_computation.67 | convolution fusion | flops 4297064448 | bytes 14680064 | tf_op jit(solution)/shard_map/dot_general | solution.py:40
  464.6 32.5 %shard_map.344 = (f32[1024,1792]{1,0:T(8,128)}, f32[1024,128]{1,0:T(8,128)S(1)}, f32[1024,128]{1,0:T(8,128)S(1)}, f32[8,1536]{1,0:T(8,128)S(1)}) custom-call(bf16[1024,1792]{1,0:T(8,128)(2,1)S(1)} %copy-done.3, bf16[1024,1792]{1,0:T(8,128)(2,1)S(1)} %copy-done.3, bf16[1024,1792]{1,0:T(8,128)(2,1)S(1)} %copy-done.3, f32[1024,128]{1,0:T(8,128)S(1)} %pad.27.ld_ref, ...), custom_call_target="tpu_custom_call" | custom-call | tf_op jit(solution)/shard_map/pallas_call | solution.py:230
  515.2 22.1 %shard_map.345 = (bf16[1024,1920]{1,0:T(8,128)(2,1)S(1)}, f32[8,1792]{1,0:T(8,128)S(1)}) custom-call(f32[1024,4992]{1,0:T(8,128)} %fusion.100.x_ref, f32[1024,1792]{1,0:T(8,128)S(1)} %copy-done.8, bf16[1024,128]{1,0:T(8,128)(2,1)S(1)} %pad.28.d_raw_ref, f32[1024,4]{1,0:T(8,128)S(1)} %copy-done.16, f32[4,1792]{1,0:T(4,128)S(1)} %copy-done.23, ...), custom_call_target="tpu_custom_call" | custom-call | tf_op jit(solution)/shard_map/pallas_call | solution.py:458
  544.8 7.4 %convolution_convert_fusion.3 = bf16[1024,1920]{1,0:T(8,128)(2,1)S(1)} fusion(bf16[1024,1920]{1,0:T(8,128)(2,1)S(1)} %copy-done.25, bf16[1,1024,1024]{2,1,0:T(8,128)(2,1)} %param.20, f32[1024]{0:T(1024)S(1)} %copy-done.93, f32[1024]{0:T(1024)S(1)} %copy-done.90), kind=kOutput, calls=%fused_computation.58 | convolution fusion | flops 4032692224 | bytes 9969664 | tf_op jit(solution)/shard_map/dot_general | solution.py:44
  564.9 10.5 %fusion.22 = (f32[1024]{0:T(1024)S(1)}, f32[1024]{0:T(1024)S(1)}, f32[1024,1024]{1,0:T(8,128)}) fusion(bf16[1,1024,1024]{2,1,0:T(8,128)(2,1)S(1)} %copy-done.42, f32[1024]{0:T(1024)S(1)} %copy-done.90, f32[1024]{0:T(1024)S(1)} %copy-done.93, f32[1024,1024]{1,0:T(8,128)} %fusion.27, bf16[1024,3072]{1,0:T(8,128)(2,1)S(1)} %bitcast.324, ...), kind=kOutput, calls=%fused_computation.39 | convolution fusion | flops 6450837504 | bytes 23085056 | tf_op jit(solution)/shard_map/dot_general | solution.py:40
  583.9 12.0 %collective-permute-done.27 = f32[104,128]{1,0:T(8,128)S(1)} collective-permute-done((f32[104,128]{1,0:T(8,128)S(1)}, f32[104,128]{1,0:T(8,128)S(1)}, u32[]{:S(2)}, u32[]{:S(2)}) %collective-permute-start.27) | collective-permute-done | bytes 53280 | tf_op jit(solution)/shard_map/ppermute | solution.py:548
  (425 shorter events, 244.3 us)
Async XLA Ops:
  7.2 92.4 %all-gather.3.cloned.1.call-start = ((), (), s32[]{:S(2)}) async-start(), calls=%async_computation | async-start | bytes 10543104 | tf_op jit(solution)/shard_map/all_gather | solution.py:641
  10.9 210.6 %all-gather.5.cloned.1.call-start = ((), (), s32[]{:S(2)}) async-start(), calls=%async_computation.1 | async-start | bytes 18382848 | tf_op jit(solution)/shard_map/all_gather | solution.py:641
  261.7 12.9 %collective-permute-start = (bf16[8,64,2048]{2,1,0:T(8,128)(2,1)S(1)}, bf16[8,64,2048]{2,1,0:T(8,128)(2,1)}, u32[]{:S(2)}, u32[]{:S(2)}) collective-permute-start(bf16[8,64,2048]{2,1,0:T(8,128)(2,1)S(1)} %get-tuple-element.152), channel_id=1, source_target_pairs={{0,2},{1,3},{2,0},{3,1},{4,6},{5,7},{6,4},{7,5},{8,10},{9,11},{10,... | collective-permute-start | bytes 6291464 | tf_op jit(solution)/shard_map/ppermute | solution.py:548
  292.2 24.6 %collective-permute-start.2 = (bf16[8,64,4096]{2,1,0:T(8,128)(2,1)}, bf16[8,64,4096]{2,1,0:T(8,128)(2,1)}, u32[]{:S(2)}, u32[]{:S(2)}) collective-permute-start(bf16[8,64,4096]{2,1,0:T(8,128)(2,1)} %get-tuple-element.131), channel_id=1, source_target_pairs={{0,2},{1,3},{2,0},{3,1},{4,6},{5,7},{6,4},{7,5},{8,10},{9,11},{10,... | collective-permute-start | bytes 12582920 | tf_op jit(solution)/shard_map/ppermute | solution.py:548
  301.0 15.8 %collective-permute-start.1 = (bf16[2,4,32,2048]{3,2,1,0:T(8,128)(2,1)S(1)}, bf16[2,4,32,2048]{3,2,1,0:T(8,128)(2,1)S(1)}, u32[]{:S(2)}, u32[]{:S(2)}) collective-permute-start(bf16[2,4,32,2048]{3,2,1,0:T(8,128)(2,1)S(1)} %pad_maximum_fusion.11), channel_id=1, source_target_pairs={{0,1},{1,0},{2,6},{3,7},{4,5},{5,4},{6,2},{7,3},{8,9},{9,8},{10,14... | collective-permute-start | bytes 3145736 | tf_op jit(solution)/shard_map/ppermute | solution.py:592
  328.2 18.6 %collective-permute-start.4 = (bf16[8,64,2560]{2,1,0:T(8,128)(2,1)}, bf16[8,64,2560]{2,1,0:T(8,128)(2,1)S(1)}, u32[]{:S(2)}, u32[]{:S(2)}) collective-permute-start(bf16[8,64,2560]{2,1,0:T(8,128)(2,1)} %get-tuple-element.143), channel_id=1, source_target_pairs={{0,2},{1,3},{2,0},{3,1},{4,6},{5,7},{6,4},{7,5},{8,10},{9,11},{10,... | collective-permute-start | bytes 7864328 | tf_op jit(solution)/shard_map/ppermute | solution.py:548
  332.0 14.9 %collective-permute-start.3 = (bf16[4,32,2048]{2,1,0:T(8,128)(2,1)S(1)}, bf16[4,32,2048]{2,1,0:T(8,128)(2,1)S(1)}, u32[]{:S(2)}, u32[]{:S(2)}) collective-permute-start(bf16[4,32,2048]{2,1,0:T(8,128)(2,1)S(1)} %get-tuple-element.167), channel_id=1, source_target_pairs={{0,4},{1,5},{2,3},{3,2},{4,0},{5,1},{6,7},{7,6},{8,12},{9,13},{10,... | collective-permute-start | bytes 1572872 | tf_op jit(solution)/shard_map/ppermute | solution.py:595
  337.9 55.2 %collective-permute-start.6 = (bf16[2,4,32,4096]{3,2,1,0:T(8,128)(2,1)}, bf16[2,4,32,4096]{3,2,1,0:T(8,128)(2,1)}, u32[]{:S(2)}, u32[]{:S(2)}) collective-permute-start(bf16[2,4,32,4096]{3,2,1,0:T(8,128)(2,1)} %pad_maximum_fusion.5), channel_id=1, source_target_pairs={{0,1},{1,0},{2,6},{3,7},{4,5},{5,4},{6,2},{7,3},{8,9},{9,8},{10,14... | collective-permute-start | bytes 6291464 | tf_op jit(solution)/shard_map/ppermute | solution.py:592
  350.4 42.8 %collective-permute-start.7 = (bf16[2,4,32,2560]{3,2,1,0:T(8,128)(2,1)}, bf16[2,4,32,2560]{3,2,1,0:T(8,128)(2,1)}, u32[]{:S(2)}, u32[]{:S(2)}) collective-permute-start(bf16[2,4,32,2560]{3,2,1,0:T(8,128)(2,1)} %pad_maximum_fusion.10), channel_id=1, source_target_pairs={{0,1},{1,0},{2,6},{3,7},{4,5},{5,4},{6,2},{7,3},{8,9},{9,8},{10,14... | collective-permute-start | bytes 3932168 | tf_op jit(solution)/shard_map/ppermute | solution.py:592
  354.9 38.3 %collective-permute-start.5 = (bf16[2,32,2048]{2,1,0:T(8,128)(2,1)}, bf16[2,32,2048]{2,1,0:T(8,128)(2,1)S(1)}, u32[]{:S(2)}, u32[]{:S(2)}) collective-permute-start(bf16[2,32,2048]{2,1,0:T(8,128)(2,1)} %get-tuple-element.177), channel_id=1, source_target_pairs={{0,8},{1,9},{2,10},{3,11},{4,12},{5,13},{6,14},{7,15},{8,0},{9,1},... | collective-permute-start | bytes 786440 | tf_op jit(solution)/shard_map/ppermute | solution.py:548
  415.4 21.0 %collective-permute-start.9 = (bf16[4,32,4096]{2,1,0:T(8,128)(2,1)S(1)}, bf16[4,32,4096]{2,1,0:T(8,128)(2,1)S(1)}, u32[]{:S(2)}, u32[]{:S(2)}) collective-permute-start(bf16[4,32,4096]{2,1,0:T(8,128)(2,1)S(1)} %get-tuple-element.147), channel_id=1, source_target_pairs={{0,4},{1,5},{2,3},{3,2},{4,0},{5,1},{6,7},{7,6},{8,12},{9,13},{10,... | collective-permute-start | bytes 3145736 | tf_op jit(solution)/shard_map/ppermute | solution.py:595
  419.0 17.5 %collective-permute-start.10 = (bf16[4,32,2560]{2,1,0:T(8,128)(2,1)S(1)}, bf16[4,32,2560]{2,1,0:T(8,128)(2,1)S(1)}, u32[]{:S(2)}, u32[]{:S(2)}) collective-permute-start(bf16[4,32,2560]{2,1,0:T(8,128)(2,1)S(1)} %get-tuple-element.161), channel_id=1, source_target_pairs={{0,4},{1,5},{2,3},{3,2},{4,0},{5,1},{6,7},{7,6},{8,12},{9,13},{10,... | collective-permute-start | bytes 1966088 | tf_op jit(solution)/shard_map/ppermute | solution.py:595
  421.7 8.6 %collective-permute-start.8 = (bf16[1,32,2048]{2,1,0:T(8,128)(2,1)S(1)}, bf16[1,32,2048]{2,1,0:T(8,128)(2,1)S(1)}, u32[]{:S(2)}, u32[]{:S(2)}) collective-permute-start(bf16[1,32,2048]{2,1,0:T(8,128)(2,1)S(1)} %fusion.86), channel_id=1, source_target_pairs={{0,16},{1,17},{2,18},{3,19},{4,20},{5,21},{6,22},{7,23},{8,24},{9,... | collective-permute-start | bytes 393224 | tf_op jit(solution)/shard_map/ppermute | solution.py:548
  449.9 48.0 %collective-permute-start.13 = (bf16[8,64,3072]{2,1,0:T(8,128)(2,1)}, bf16[8,64,3072]{2,1,0:T(8,128)(2,1)}, u32[]{:S(2)}, u32[]{:S(2)}) collective-permute-start(bf16[8,64,3072]{2,1,0:T(8,128)(2,1)} %get-tuple-element.136), channel_id=1, source_target_pairs={{0,2},{1,3},{2,0},{3,1},{4,6},{5,7},{6,4},{7,5},{8,10},{9,11},{10,... | collective-permute-start | bytes 9437192 | tf_op jit(solution)/shard_map/ppermute | solution.py:548
  462.5 35.4 %collective-permute-start.11 = (bf16[2,32,4096]{2,1,0:T(8,128)(2,1)S(1)}, bf16[2,32,4096]{2,1,0:T(8,128)(2,1)S(1)}, u32[]{:S(2)}, u32[]{:S(2)}) collective-permute-start(bf16[2,32,4096]{2,1,0:T(8,128)(2,1)S(1)} %get-tuple-element.163), channel_id=1, source_target_pairs={{0,8},{1,9},{2,10},{3,11},{4,12},{5,13},{6,14},{7,15},{8,0},{9,1},... | collective-permute-start | bytes 1572872 | tf_op jit(solution)/shard_map/ppermute | solution.py:548
  463.8 34.0 %collective-permute-start.12 = (bf16[2,32,2560]{2,1,0:T(8,128)(2,1)S(1)}, bf16[2,32,2560]{2,1,0:T(8,128)(2,1)S(1)}, u32[]{:S(2)}, u32[]{:S(2)}) collective-permute-start(bf16[2,32,2560]{2,1,0:T(8,128)(2,1)S(1)} %get-tuple-element.175), channel_id=1, source_target_pairs={{0,8},{1,9},{2,10},{3,11},{4,12},{5,13},{6,14},{7,15},{8,0},{9,1},... | collective-permute-start | bytes 983048 | tf_op jit(solution)/shard_map/ppermute | solution.py:548
  502.9 36.4 %collective-permute-start.16 = (bf16[2,4,32,3072]{3,2,1,0:T(8,128)(2,1)}, bf16[2,4,32,3072]{3,2,1,0:T(8,128)(2,1)}, u32[]{:S(2)}, u32[]{:S(2)}) collective-permute-start(bf16[2,4,32,3072]{3,2,1,0:T(8,128)(2,1)} %pad_maximum_fusion.9), channel_id=1, source_target_pairs={{0,1},{1,0},{2,6},{3,7},{4,5},{5,4},{6,2},{7,3},{8,9},{9,8},{10,14... | collective-permute-start | bytes 4718600 | tf_op jit(solution)/shard_map/ppermute | solution.py:592
  505.0 34.2 %collective-permute-start.15 = (bf16[1,32,2560]{2,1,0:T(8,128)(2,1)}, bf16[1,32,2560]{2,1,0:T(8,128)(2,1)}, u32[]{:S(2)}, u32[]{:S(2)}) collective-permute-start(bf16[1,32,2560]{2,1,0:T(8,128)(2,1)} %fusion.83), channel_id=1, source_target_pairs={{0,16},{1,17},{2,18},{3,19},{4,20},{5,21},{6,22},{7,23},{8,24},{9,... | collective-permute-start | bytes 491528 | tf_op jit(solution)/shard_map/ppermute | solution.py:548
  507.0 32.3 %collective-permute-start.14 = (bf16[1,32,4096]{2,1,0:T(8,128)(2,1)}, bf16[1,32,4096]{2,1,0:T(8,128)(2,1)S(1)}, u32[]{:S(2)}, u32[]{:S(2)}) collective-permute-start(bf16[1,32,4096]{2,1,0:T(8,128)(2,1)} %fusion.70), channel_id=1, source_target_pairs={{0,16},{1,17},{2,18},{3,19},{4,20},{5,21},{6,22},{7,23},{8,24},{9,... | collective-permute-start | bytes 786440 | tf_op jit(solution)/shard_map/ppermute | solution.py:548
  543.6 13.8 %collective-permute-start.17 = (bf16[4,32,3072]{2,1,0:T(8,128)(2,1)S(1)}, bf16[4,32,3072]{2,1,0:T(8,128)(2,1)S(1)}, u32[]{:S(2)}, u32[]{:S(2)}) collective-permute-start(bf16[4,32,3072]{2,1,0:T(8,128)(2,1)S(1)} %get-tuple-element.159), channel_id=1, source_target_pairs={{0,4},{1,5},{2,3},{3,2},{4,0},{5,1},{6,7},{7,6},{8,12},{9,13},{10,... | collective-permute-start | bytes 2359304 | tf_op jit(solution)/shard_map/ppermute | solution.py:595
  581.3 29.2 %collective-permute-start.20 = (bf16[2,4,32,1920]{3,2,1,0:T(8,128)(2,1)}, bf16[2,4,32,1920]{3,2,1,0:T(8,128)(2,1)}, u32[]{:S(2)}, u32[]{:S(2)}) collective-permute-start(bf16[2,4,32,1920]{3,2,1,0:T(8,128)(2,1)} %pad_maximum_fusion.12), channel_id=1, source_target_pairs={{0,1},{1,0},{2,6},{3,7},{4,5},{5,4},{6,2},{7,3},{8,9},{9,8},{10,14... | collective-permute-start | bytes 2949128 | tf_op jit(solution)/shard_map/ppermute | solution.py:592
  581.7 14.2 %collective-permute-start.27 = (f32[104,128]{1,0:T(8,128)S(1)}, f32[104,128]{1,0:T(8,128)S(1)}, u32[]{:S(2)}, u32[]{:S(2)}) collective-permute-start(f32[104,128]{1,0:T(8,128)S(1)} %fusion.117), channel_id=1, source_target_pairs={{0,4},{1,5},{2,6},{3,7},{4,0},{5,1},{6,2},{7,3},{8,12},{9,13},{10,... | collective-permute-start | bytes 159752 | tf_op jit(solution)/shard_map/ppermute | solution.py:548
  601.1 9.3 %collective-permute-start.19 = (bf16[2,32,3072]{2,1,0:T(8,128)(2,1)}, bf16[2,32,3072]{2,1,0:T(8,128)(2,1)S(1)}, u32[]{:S(2)}, u32[]{:S(2)}) collective-permute-start(bf16[2,32,3072]{2,1,0:T(8,128)(2,1)} %get-tuple-element.173), channel_id=1, source_target_pairs={{0,8},{1,9},{2,10},{3,11},{4,12},{5,13},{6,14},{7,15},{8,0},{9,1},... | collective-permute-start | bytes 1179656 | tf_op jit(solution)/shard_map/ppermute | solution.py:548
  613.8 8.0 %collective-permute-start.22 = (bf16[4,32,1920]{2,1,0:T(8,128)(2,1)S(1)}, bf16[4,32,1920]{2,1,0:T(8,128)(2,1)S(1)}, u32[]{:S(2)}, u32[]{:S(2)}) collective-permute-start(bf16[4,32,1920]{2,1,0:T(8,128)(2,1)S(1)} %get-tuple-element.171), channel_id=1, source_target_pairs={{0,4},{1,5},{2,3},{3,2},{4,0},{5,1},{6,7},{7,6},{8,12},{9,13},{10,... | collective-permute-start | bytes 1474568 | tf_op jit(solution)/shard_map/ppermute | solution.py:595
  (114 other events, 1500.2 us)
Sparse Core Ops, SparseCore 0:
  11.5 88.0 all-gather.2
  103.0 118.3 all-gather.4

commit v5 on v4

--- a/solution.py
+++ b/solution.py
@@ -739,7 +739,6 @@
         ],
         axis=1,
     )
-    d_ssm, d_first = sums.step((d_ssm, d_first))
     sums.start("first", mm_tn(normed, d_first))
     d_act, d_st, d_ld, g_skip_wide = scan_bwd(act_low, ld, st, states, d_ssm, skip_wide)
     g_skip = jnp.sum(g_skip_wide[0].reshape(M_HEADS, M_HDIM), axis=1)

time: 654 us -> 658 us (level)
  matrix products: 132 us -> 140 us
    mul x0 -> x1, other arithmetic: none -> 9.69 us  [shards(): d_ssm = d_mixed_in * jax.nn.silu(z_gate)]
    convert_element_type x1 -> x0, other arithmetic: 8.59 us -> none  [shards(): (d_mixed_in * ssm_out * silu_slope(z_gate)).astype(bf16)]
    ppermute x5, waiting for transfers between devices: 8.53 us -> 1.36 us  [scatter_steps(): other = (yield lax.ppermute(sent, AXES, back))]
    unnamed x225 -> x207, local copies, waits for them, and re-layouts: 42.2 us -> 37.3 us
  transfers between devices with their start and end apart: 32 -> 32, of which waited for: 13 -> 11; matrix products, arithmetic and copies ran while one was open for 27% -> 29% of each run, Pallas kernels for 21% -> 21%
where the time goes in v5:
time: 658 us; the launch traced here: 646 us
  matrix products  140 us (21%)
  Pallas kernels  137 us (21%)
  waiting for transfers between devices  125 us (19%)
  other arithmetic  112 us (17%)
  local copies, waits for them, and re-layouts  85 us (13%)
  starting transfers between devices  25.9 us (4%)
  between operations  21 us (3%)
    all_gather x2, waiting for transfers between devices, gather(): lax.all_gather(jnp.concatenate(parts, axis=1), AXES, axis=0, tiled=True)  87.6 us
    dot_general x5, matrix products, mm_nt(): return lax.dot_general(left, right, NT, preferred_element_type=f32)  57.6 us
    dot_general x3, matrix products, mm(): return jnp.dot(left, right, preferred_element_type=f32)  41 us
    dot_general x5, matrix products, mm_tn(): return lax.dot_general(left, right, TN, preferred_element_type=f32)  41 us
    unnamed x207, local copies, waits for them, and re-layouts  37.3 us
    ppermute x20, waiting for transfers between devices, flip(): return lax.ppermute(values, AXES, [(i, i ^ bit) for i in range(places)])  35.7 us
    pallas_call x1, Pallas kernels, scan_bwd(): pl.pallas_call(scan_bwd_kernel, grid=(blocks,), in_specs=[pl.BlockSpec((S...  32.5 us
    another operation x15, other arithmetic, along(): jnp.stack([pick(jnp.where(core == 0, second, first), jnp.where(core == 0,...  28.4 us
  transfers between devices with their start and end apart: 32, of which 11 were waited for; matrix products, arithmetic and copies ran while one was open for 29% of the time, Pallas kernels for 21%

profile of v5, /device:TPU:1, one launch (start us, length us, event | category | flops | bytes accessed | tf_op | source)
XLA Modules:
  0.0 645.9 jit_solution(5405815183323581306)
XLA Ops:
  28.3 71.3 %all-gather.3.cloned.1.call-done = bf16[1024,4992]{1,0:T(8,128)(2,1)} async-done(((bf16[32,4992]{1,0:T(8,128)(2,1)}), bf16[1024,4992]{1,0:T(8,128)(2,1)}) %all-gather.3.cloned.1.call-update) | async-done | bytes 10223632 | tf_op jit(solution)/shard_map/all_gather | solution.py:641
  99.6 17.6 %fusion.102.x_ref = f32[1024,4992]{1,0:T(8,128)} fusion(bf16[1024,4992]{1,0:T(8,128)(2,1)} %all-gather.3.cloned.1.call-done, bf16[1,1024,1024]{2,1,0:T(8,128)(2,1)S(1)} %copy-done.37, f32[1024]{0:T(1024)S(1)} %copy-done.82, f32[1024]{0:T(1024)S(1)} %add_rsqrt_fusion.2), kind=kOutput, calls=%fused_computation.261 | convolution fusion | flops 10473177088 | bytes 32776192 | tf_op jit(solution)/shard_map/dot_general | solution.py:36
  137.1 12.4 %shard_map.340.x_ref.b_ref.c_ref = bf16[1024,1792]{1,0:T(8,128)(2,1)S(1)} custom-call(f32[1024,4992]{1,0:T(8,128)} %fusion.102.x_ref, f32[1024,4]{1,0:T(8,128)S(1)} %copy-done.15, f32[4,1792]{1,0:T(4,128)S(1)} %copy-done.24, f32[1,1792]{1,0:T(1,128)S(1)} %broadcast_in_dim.29.bias_ref), custom_call_target="tpu_custom_call" | custom-call | tf_op jit(solution)/shard_map/pallas_call | solution.py:440
  151.3 20.3 %shard_map.339 = (bf16[1024,1024]{1,0:T(8,128)(2,1)S(1)}, f32[8,1,1024]{2,1,0:T(1,128)S(1)}) custom-call(bf16[1024,1024]{1,0:T(8,128)(2,1)S(1)} %bitcast.295, bf16[1024,256]{1,0:T(8,128)(2,1)S(1)} %bitcast.298, bf16[1024,256]{1,0:T(8,128)(2,1)S(1)} %copy-done.11, f32[1024,1]{1,0:T(8,128)S(1)} %copy.132.doc_col_ref, f32[1,1024]{1,0:T(1,128)S(1)} %get-tuple-element.188.doc_row_ref), custom_call_target="tpu_custom_call" | custom-call | tf_op jit(solution)/shard_map/pallas_call | solution.py:333
  179.6 13.2 %shard_map.341 = (f32[1024,1536]{1,0:T(8,128)S(1)}, bf16[8,128,1536]{2,1,0:T(8,128)(2,1)S(1)}) custom-call(bf16[1024,1792]{1,0:T(8,128)(2,1)S(1)} %copy-done.1, bf16[1024,1792]{1,0:T(8,128)(2,1)S(1)} %copy-done.1, bf16[1024,1792]{1,0:T(8,128)(2,1)S(1)} %copy-done.1, f32[1024,128]{1,0:T(8,128)S(1)} %pad.27.ld_ref, f32[1024,128]{1,0:T(8,128)S(1)} %copy-done.9), custom_call_target="tpu_custom_call" | custom-call | tf_op jit(solution)/shard_map/pallas_call | solution.py:203
  192.8 7.4 %multiply_reduce_fusion.2 = (f32[1024]{0:T(1024)S(1)}, f32[1024,1536]{1,0:T(8,128)S(1)}) fusion(f32[1024,4992]{1,0:T(8,128)} %fusion.102.x_ref, f32[1024,1536]{1,0:T(8,128)S(1)} %get-tuple-element.65, bf16[1024,1792]{1,0:T(8,128)(2,1)S(1)} %copy-done.1, f32[1536]{0:T(1024)S(1)} %mul.474), kind=kLoop, calls=%fused_computation.22 | loop fusion | flops 15727616 | bytes 22030336 | tf_op jit(solution)/shard_map/reduce_sum | solution.py:510
  205.1 16.3 %all-gather.5.cloned.1.call-done.down_ref = bf16[1024,8704]{1,0:T(8,128)(2,1)} async-done(((bf16[32,8704]{1,0:T(8,128)(2,1)}), bf16[1024,8704]{1,0:T(8,128)(2,1)}) %all-gather.5.cloned.1.call-update) | async-done | bytes 17825808 | tf_op jit(solution)/shard_map/all_gather | solution.py:641
  221.4 10.9 %multiply_reduce_fusion.5 = (f32[1024]{0:T(1024)S(1)}, f32[1024,1024]{1,0:T(8,128)}) fusion(bf16[1024,8704]{1,0:T(8,128)(2,1)} %all-gather.5.cloned.1.call-done.down_ref, bf16[1024,1536]{1,0:T(8,128)(2,1)} %multiply_convert_fusion.1, bf16[1024,1024]{1,0:T(8,128)(2,1)} %copy-done.27, bf16[1,1024,1024]{2,1,0:T(8,128)(2,1)} %param.20), kind=kOutput, calls=%fused_computation.52 | convolution fusion | flops 5383388160 | bytes 16781312 | tf_op jit(solution)/shard_map/dot_general | solution.py:40
  232.3 12.6 %fusion.3.both_ref = f32[1024,4096]{1,0:T(8,128)S(1)} fusion(bf16[1024,8704]{1,0:T(8,128)(2,1)} %all-gather.5.cloned.1.call-done.down_ref, f32[1024,1024]{1,0:T(8,128)} %get-tuple-element.195, f32[1024]{0:T(1024)S(1)} %copy-done.81, f32[1024]{0:T(1024)S(1)} %add_rsqrt_fusion), kind=kOutput, calls=%fused_computation.5 | convolution fusion | flops 8593080320 | bytes 29368320 | tf_op jit(solution)/shard_map/dot_general | solution.py:36
  261.7 12.7 %shard_map.342 = bf16[1024,4096]{1,0:T(8,128)(2,1)S(1)} custom-call(bf16[1024,1024]{1,0:T(8,128)(2,1)S(1)} %bitcast.297, bf16[1024,8704]{1,0:T(8,128)(2,1)} %all-gather.5.cloned.1.call-done.down_ref, f32[1024,4096]{1,0:T(8,128)} %copy-done.30), custom_call_target="tpu_custom_call" | custom-call | tf_op jit(solution)/shard_map/pallas_call | solution.py:495
  274.4 13.1 %convolution_convert_fusion = bf16[1024,4096]{1,0:T(8,128)(2,1)S(1)} fusion(bf16[1024,4096]{1,0:T(8,128)(2,1)S(1)} %shard_map.342, f32[1024,1024]{1,0:T(8,128)} %get-tuple-element.195, f32[1024]{0:T(1024)S(1)} %copy-done.81, f32[1024]{0:T(1024)S(1)} %add_rsqrt_fusion), kind=kOutput, calls=%fused_computation.2 | convolution fusion | flops 8597274624 | bytes 20979712 | tf_op jit(solution)/shard_map/dot_general | solution.py:44
  302.0 14.4 %multiply_reduce_fusion.3 = (f32[1024]{0:T(1024)S(1)}, f32[1024]{0:T(1024)S(1)}, f32[1024,1024]{1,0:T(8,128)S(1)}) fusion(f32[1024,1024]{1,0:T(8,128)S(1)} %copy-done.47, f32[1024]{0:T(1024)S(1)} %add_rsqrt_fusion, f32[1024]{0:T(1024)S(1)} %copy-done.81, bf16[1024,4096]{1,0:T(8,128)(2,1)} %copy-done.5, ...), kind=kOutput, calls=%fused_computation.44 | convolution fusion | flops 8596224000 | bytes 25182208 | tf_op jit(solution)/shard_map/dot_general | solution.py:40
  319.0 6.2 convolution_convert_fusion.2
  337.1 10.8 %fusion.12 = f32[1024,2560]{1,0:T(8,128)} fusion(bf16[1024,8704]{1,0:T(8,128)(2,1)} %all-gather.5.cloned.1.call-done.down_ref, f32[1024,1024]{1,0:T(8,128)S(1)} %multiply_add_fusion.1), kind=kOutput, calls=%fused_computation.29 | convolution fusion | flops 5369757696 | bytes 19922944 | tf_op jit(solution)/shard_map/dot_general | solution.py:36
  356.2 24.7 %shard_map.343 = (f32[1024,1024]{1,0:T(8,128)S(1)}, f32[1024,256]{1,0:T(8,128)S(1)}, f32[1024,256]{1,0:T(8,128)S(1)}) custom-call(bf16[1024,1024]{1,0:T(8,128)(2,1)S(1)} %bitcast.296, bf16[1024,256]{1,0:T(8,128)(2,1)S(1)} %bitcast.299, bf16[1024,256]{1,0:T(8,128)(2,1)S(1)} %copy-done.12, f32[1024,1024]{1,0:T(8,128)S(1)} %slice.165.do_ref, ...), custom_call_target="tpu_custom_call" | custom-call | tf_op jit(solution)/shard_map/pallas_call | solution.py:362
  401.9 9.7 %fusion.29 = (f32[1024,1536]{1,0:T(8,128)}, bf16[1024,1536]{1,0:T(8,128)(2,1)}) fusion(f32[1024]{0:T(1024)S(1)} %broadcast_multiply_fusion, f32[1024,1536]{1,0:T(8,128)S(1)} %bitcast.304, f32[1024,2560]{1,0:T(8,128)S(1)} %bitcast.308, f32[1536]{0:T(1024)S(1)} %copy-done.78, f32[1024]{0:T(1024)S(1)} %add_rsqrt_fusion.1, f32[1024,4992]{1,0:T(8,128)} %fusion.102.x_ref, ...), kind=kLoop, calls=%fused_computation.61 | loop fusion | flops 31457280 | bytes 37769216 | tf_op jit(solution)/shard_map/mul | solution.py:732
  411.6 10.1 %convolution_convert_fusion.1 = bf16[1024,3072]{1,0:T(8,128)(2,1)S(1)} fusion(bf16[1024,256]{1,0:T(8,128)(2,1)S(1)} %convert_element_type.881, bf16[1024,256]{1,0:T(8,128)(2,1)} %bitcast.340, bf16[1024,1024]{1,0:T(8,128)(2,1)} %bitcast.333, bf16[1024,1536]{1,0:T(8,128)(2,1)} %get-tuple-element.122, bf16[1,1024,1024]{2,1,0:T(8,128)(2,1)S(1)} %copy-done.38, ...), kind=kOutput, calls=%fused_computation.26 | convolution fusion | flops 6474956800 | bytes 14688256 | tf_op jit(solution)/shard_map/dot_general | solution.py:44
  438.6 8.6 %fusion.30 = bf16[1,1024,1024]{2,1,0:T(8,128)(2,1)} fusion(f32[1024,1024]{1,0:T(8,128)S(1)} %copy-done.48, bf16[1024,2048]{1,0:T(8,128)(2,1)S(1)} %copy-done.46, bf16[1024,8704]{1,0:T(8,128)(2,1)} %all-gather.5.cloned.1.call-done.down_ref), kind=kOutput, calls=%fused_computation.67 | convolution fusion | flops 4297064448 | bytes 14680064 | tf_op jit(solution)/shard_map/dot_general | solution.py:40
  447.2 32.5 %shard_map.344 = (f32[1024,1792]{1,0:T(8,128)}, f32[1024,128]{1,0:T(8,128)S(1)}, f32[1024,128]{1,0:T(8,128)S(1)}, f32[8,1536]{1,0:T(8,128)S(1)}) custom-call(bf16[1024,1792]{1,0:T(8,128)(2,1)S(1)} %copy-done.3, bf16[1024,1792]{1,0:T(8,128)(2,1)S(1)} %copy-done.3, bf16[1024,1792]{1,0:T(8,128)(2,1)S(1)} %copy-done.3, f32[1024,128]{1,0:T(8,128)S(1)} %pad.27.ld_ref, ...), custom_call_target="tpu_custom_call" | custom-call | tf_op jit(solution)/shard_map/pallas_call | solution.py:230
  486.4 12.3 %fusion.5 = f32[1024,1024]{1,0:T(8,128)} fusion(bf16[1024,4992]{1,0:T(8,128)(2,1)} %all-gather.3.cloned.1.call-done, bf16[1024,256]{1,0:T(8,128)(2,1)S(1)} %copy-done.66, bf16[1024,256]{1,0:T(8,128)(2,1)} %bitcast.341, bf16[1024,1024]{1,0:T(8,128)(2,1)} %bitcast.334, bf16[1024,1536]{1,0:T(8,128)(2,1)S(1)} %copy-done.51), kind=kOutput, calls=%fused_computation.7 | convolution fusion | flops 6467616768 | bytes 16777216 | tf_op jit(solution)/shard_map/dot_general | solution.py:40
  508.9 21.6 %shard_map.345 = (bf16[1024,1920]{1,0:T(8,128)(2,1)S(1)}, f32[8,1792]{1,0:T(8,128)S(1)}) custom-call(f32[1024,4992]{1,0:T(8,128)} %fusion.102.x_ref, f32[1024,1792]{1,0:T(8,128)S(1)} %copy-done.8, bf16[1024,128]{1,0:T(8,128)(2,1)S(1)} %pad.28.d_raw_ref, f32[1024,4]{1,0:T(8,128)S(1)} %copy-done.16, f32[4,1792]{1,0:T(4,128)S(1)} %copy-done.25, ...), custom_call_target="tpu_custom_call" | custom-call | tf_op jit(solution)/shard_map/pallas_call | solution.py:458
  552.9 11.2 %collective-permute-done.15 = bf16[1,32,4096]{2,1,0:T(8,128)(2,1)} collective-permute-done((bf16[1,32,4096]{2,1,0:T(8,128)(2,1)}, bf16[1,32,4096]{2,1,0:T(8,128)(2,1)}, u32[]{:S(2)}, u32[]{:S(2)}) %collective-permute-start.15) | collective-permute-done | bytes 262176 | tf_op jit(solution)/shard_map/ppermute | solution.py:548
  567.3 11.4 %fusion.22 = (f32[1024]{0:T(1024)S(1)}, f32[1024]{0:T(1024)S(1)}, f32[1024,1024]{1,0:T(8,128)}) fusion(bf16[1,1024,1024]{2,1,0:T(8,128)(2,1)S(1)} %copy-done.40, f32[1024]{0:T(1024)S(1)} %copy-done.80, f32[1024]{0:T(1024)S(1)} %copy-done.83, f32[1024,1024]{1,0:T(8,128)} %fusion.5, bf16[1024,1920]{1,0:T(8,128)(2,1)} %copy-done.26, ...), kind=kOutput, calls=%fused_computation.39 | convolution fusion | flops 4034918400 | bytes 18366464 | tf_op jit(solution)/shard_map/dot_general | solution.py:40
  590.3 10.8 %collective-permute-done.27 = f32[104,128]{1,0:T(8,128)S(1)} collective-permute-done((f32[104,128]{1,0:T(8,128)S(1)}, f32[104,128]{1,0:T(8,128)S(1)}, u32[]{:S(2)}, u32[]{:S(2)}) %collective-permute-start.27) | collective-permute-done | bytes 53280 | tf_op jit(solution)/shard_map/ppermute | solution.py:548
  (405 shorter events, 232.7 us)
Async XLA Ops:
  7.2 92.4 %all-gather.3.cloned.1.call-start = ((), (), s32[]{:S(2)}) async-start(), calls=%async_computation | async-start | bytes 10543104 | tf_op jit(solution)/shard_map/all_gather | solution.py:641
  10.9 210.5 %all-gather.5.cloned.1.call-start = ((), (), s32[]{:S(2)}) async-start(), calls=%async_computation.1 | async-start | bytes 18382848 | tf_op jit(solution)/shard_map/all_gather | solution.py:641
  261.5 12.9 %collective-permute-start = (bf16[8,64,2048]{2,1,0:T(8,128)(2,1)S(1)}, bf16[8,64,2048]{2,1,0:T(8,128)(2,1)}, u32[]{:S(2)}, u32[]{:S(2)}) collective-permute-start(bf16[8,64,2048]{2,1,0:T(8,128)(2,1)S(1)} %get-tuple-element.148), channel_id=1, source_target_pairs={{0,2},{1,3},{2,0},{3,1},{4,6},{5,7},{6,4},{7,5},{8,10},{9,11},{10,... | collective-permute-start | bytes 6291464 | tf_op jit(solution)/shard_map/ppermute | solution.py:548
  291.9 24.5 %collective-permute-start.2 = (bf16[8,64,4096]{2,1,0:T(8,128)(2,1)}, bf16[8,64,4096]{2,1,0:T(8,128)(2,1)}, u32[]{:S(2)}, u32[]{:S(2)}) collective-permute-start(bf16[8,64,4096]{2,1,0:T(8,128)(2,1)} %get-tuple-element.127), channel_id=1, source_target_pairs={{0,2},{1,3},{2,0},{3,1},{4,6},{5,7},{6,4},{7,5},{8,10},{9,11},{10,... | collective-permute-start | bytes 12582920 | tf_op jit(solution)/shard_map/ppermute | solution.py:548
  300.7 15.7 %collective-permute-start.1 = (bf16[2,4,32,2048]{3,2,1,0:T(8,128)(2,1)S(1)}, bf16[2,4,32,2048]{3,2,1,0:T(8,128)(2,1)S(1)}, u32[]{:S(2)}, u32[]{:S(2)}) collective-permute-start(bf16[2,4,32,2048]{3,2,1,0:T(8,128)(2,1)S(1)} %pad_maximum_fusion.13), channel_id=1, source_target_pairs={{0,1},{1,0},{2,6},{3,7},{4,5},{5,4},{6,2},{7,3},{8,9},{9,8},{10,14... | collective-permute-start | bytes 3145736 | tf_op jit(solution)/shard_map/ppermute | solution.py:592
  325.7 22.2 %collective-permute-start.4 = (bf16[8,64,2560]{2,1,0:T(8,128)(2,1)S(1)}, bf16[8,64,2560]{2,1,0:T(8,128)(2,1)S(1)}, u32[]{:S(2)}, u32[]{:S(2)}) collective-permute-start(bf16[8,64,2560]{2,1,0:T(8,128)(2,1)S(1)} %get-tuple-element.139), channel_id=1, source_target_pairs={{0,2},{1,3},{2,0},{3,1},{4,6},{5,7},{6,4},{7,5},{8,10},{9,11},{10,... | collective-permute-start | bytes 7864328 | tf_op jit(solution)/shard_map/ppermute | solution.py:548
  330.3 17.6 %collective-permute-start.3 = (bf16[4,32,2048]{2,1,0:T(8,128)(2,1)S(1)}, bf16[4,32,2048]{2,1,0:T(8,128)(2,1)S(1)}, u32[]{:S(2)}, u32[]{:S(2)}) collective-permute-start(bf16[4,32,2048]{2,1,0:T(8,128)(2,1)S(1)} %get-tuple-element.161), channel_id=1, source_target_pairs={{0,4},{1,5},{2,3},{3,2},{4,0},{5,1},{6,7},{7,6},{8,12},{9,13},{10,... | collective-permute-start | bytes 1572872 | tf_op jit(solution)/shard_map/ppermute | solution.py:595
  335.8 56.2 %collective-permute-start.6 = (bf16[2,4,32,4096]{3,2,1,0:T(8,128)(2,1)}, bf16[2,4,32,4096]{3,2,1,0:T(8,128)(2,1)}, u32[]{:S(2)}, u32[]{:S(2)}) collective-permute-start(bf16[2,4,32,4096]{3,2,1,0:T(8,128)(2,1)} %pad_maximum_fusion.5), channel_id=1, source_target_pairs={{0,1},{1,0},{2,6},{3,7},{4,5},{5,4},{6,2},{7,3},{8,9},{9,8},{10,14... | collective-permute-start | bytes 6291464 | tf_op jit(solution)/shard_map/ppermute | solution.py:592
  350.9 41.1 %collective-permute-start.7 = (bf16[2,4,32,2560]{3,2,1,0:T(8,128)(2,1)}, bf16[2,4,32,2560]{3,2,1,0:T(8,128)(2,1)}, u32[]{:S(2)}, u32[]{:S(2)}) collective-permute-start(bf16[2,4,32,2560]{3,2,1,0:T(8,128)(2,1)} %pad_maximum_fusion.10), channel_id=1, source_target_pairs={{0,1},{1,0},{2,6},{3,7},{4,5},{5,4},{6,2},{7,3},{8,9},{9,8},{10,14... | collective-permute-start | bytes 3932168 | tf_op jit(solution)/shard_map/ppermute | solution.py:592
  353.1 38.9 %collective-permute-start.5 = (bf16[2,32,2048]{2,1,0:T(8,128)(2,1)}, bf16[2,32,2048]{2,1,0:T(8,128)(2,1)}, u32[]{:S(2)}, u32[]{:S(2)}) collective-permute-start(bf16[2,32,2048]{2,1,0:T(8,128)(2,1)} %get-tuple-element.173), channel_id=1, source_target_pairs={{0,8},{1,9},{2,10},{3,11},{4,12},{5,13},{6,14},{7,15},{8,0},{9,1},... | collective-permute-start | bytes 786440 | tf_op jit(solution)/shard_map/ppermute | solution.py:548
  425.1 54.6 %collective-permute-start.11 = (bf16[8,64,3072]{2,1,0:T(8,128)(2,1)}, bf16[8,64,3072]{2,1,0:T(8,128)(2,1)}, u32[]{:S(2)}, u32[]{:S(2)}) collective-permute-start(bf16[8,64,3072]{2,1,0:T(8,128)(2,1)} %get-tuple-element.132), channel_id=1, source_target_pairs={{0,2},{1,3},{2,0},{3,1},{4,6},{5,7},{6,4},{7,5},{8,10},{9,11},{10,... | collective-permute-start | bytes 9437192 | tf_op jit(solution)/shard_map/ppermute | solution.py:548
  430.4 49.3 %collective-permute-start.8 = (bf16[1,32,2048]{2,1,0:T(8,128)(2,1)S(1)}, bf16[1,32,2048]{2,1,0:T(8,128)(2,1)S(1)}, u32[]{:S(2)}, u32[]{:S(2)}) collective-permute-start(bf16[1,32,2048]{2,1,0:T(8,128)(2,1)S(1)} %fusion.86), channel_id=1, source_target_pairs={{0,16},{1,17},{2,18},{3,19},{4,20},{5,21},{6,22},{7,23},{8,24},{9,... | collective-permute-start | bytes 393224 | tf_op jit(solution)/shard_map/ppermute | solution.py:548
  434.0 45.8 %collective-permute-start.10 = (bf16[4,32,2560]{2,1,0:T(8,128)(2,1)S(1)}, bf16[4,32,2560]{2,1,0:T(8,128)(2,1)S(1)}, u32[]{:S(2)}, u32[]{:S(2)}) collective-permute-start(bf16[4,32,2560]{2,1,0:T(8,128)(2,1)S(1)} %get-tuple-element.157), channel_id=1, source_target_pairs={{0,4},{1,5},{2,3},{3,2},{4,0},{5,1},{6,7},{7,6},{8,12},{9,13},{10,... | collective-permute-start | bytes 1966088 | tf_op jit(solution)/shard_map/ppermute | solution.py:595
  437.9 41.9 %collective-permute-start.9 = (bf16[4,32,4096]{2,1,0:T(8,128)(2,1)S(1)}, bf16[4,32,4096]{2,1,0:T(8,128)(2,1)S(1)}, u32[]{:S(2)}, u32[]{:S(2)}) collective-permute-start(bf16[4,32,4096]{2,1,0:T(8,128)(2,1)S(1)} %get-tuple-element.143), channel_id=1, source_target_pairs={{0,4},{1,5},{2,3},{3,2},{4,0},{5,1},{6,7},{7,6},{8,12},{9,13},{10,... | collective-permute-start | bytes 3145736 | tf_op jit(solution)/shard_map/ppermute | solution.py:595
  485.6 45.0 %collective-permute-start.14 = (bf16[2,4,32,3072]{3,2,1,0:T(8,128)(2,1)}, bf16[2,4,32,3072]{3,2,1,0:T(8,128)(2,1)}, u32[]{:S(2)}, u32[]{:S(2)}) collective-permute-start(bf16[2,4,32,3072]{3,2,1,0:T(8,128)(2,1)} %pad_maximum_fusion.9), channel_id=1, source_target_pairs={{0,1},{1,0},{2,6},{3,7},{4,5},{5,4},{6,2},{7,3},{8,9},{9,8},{10,14... | collective-permute-start | bytes 4718600 | tf_op jit(solution)/shard_map/ppermute | solution.py:592
  500.0 30.5 %collective-permute-start.12 = (bf16[2,32,4096]{2,1,0:T(8,128)(2,1)}, bf16[2,32,4096]{2,1,0:T(8,128)(2,1)}, u32[]{:S(2)}, u32[]{:S(2)}) collective-permute-start(bf16[2,32,4096]{2,1,0:T(8,128)(2,1)} %get-tuple-element.159), channel_id=1, source_target_pairs={{0,8},{1,9},{2,10},{3,11},{4,12},{5,13},{6,14},{7,15},{8,0},{9,1},... | collective-permute-start | bytes 1572872 | tf_op jit(solution)/shard_map/ppermute | solution.py:548
  503.5 27.0 %collective-permute-start.13 = (bf16[2,32,2560]{2,1,0:T(8,128)(2,1)}, bf16[2,32,2560]{2,1,0:T(8,128)(2,1)S(1)}, u32[]{:S(2)}, u32[]{:S(2)}) collective-permute-start(bf16[2,32,2560]{2,1,0:T(8,128)(2,1)} %get-tuple-element.171), channel_id=1, source_target_pairs={{0,8},{1,9},{2,10},{3,11},{4,12},{5,13},{6,14},{7,15},{8,0},{9,1},... | collective-permute-start | bytes 983048 | tf_op jit(solution)/shard_map/ppermute | solution.py:548
  538.4 25.8 %collective-permute-start.18 = (bf16[8,64,1920]{2,1,0:T(8,128)(2,1)}, bf16[8,64,1920]{2,1,0:T(8,128)(2,1)}, u32[]{:S(2)}, u32[]{:S(2)}) collective-permute-start(bf16[8,64,1920]{2,1,0:T(8,128)(2,1)} %get-tuple-element.153), channel_id=1, source_target_pairs={{0,2},{1,3},{2,0},{3,1},{4,6},{5,7},{6,4},{7,5},{8,10},{9,11},{10,... | collective-permute-start | bytes 5898248 | tf_op jit(solution)/shard_map/ppermute | solution.py:548
  542.4 10.5 %collective-permute-start.16 = (bf16[1,32,2560]{2,1,0:T(8,128)(2,1)}, bf16[1,32,2560]{2,1,0:T(8,128)(2,1)}, u32[]{:S(2)}, u32[]{:S(2)}) collective-permute-start(bf16[1,32,2560]{2,1,0:T(8,128)(2,1)} %fusion.83), channel_id=1, source_target_pairs={{0,16},{1,17},{2,18},{3,19},{4,20},{5,21},{6,22},{7,23},{8,24},{9,... | collective-permute-start | bytes 491528 | tf_op jit(solution)/shard_map/ppermute | solution.py:548
  546.8 17.4 %collective-permute-start.17 = (bf16[4,32,3072]{2,1,0:T(8,128)(2,1)}, bf16[4,32,3072]{2,1,0:T(8,128)(2,1)}, u32[]{:S(2)}, u32[]{:S(2)}) collective-permute-start(bf16[4,32,3072]{2,1,0:T(8,128)(2,1)} %get-tuple-element.155), channel_id=1, source_target_pairs={{0,4},{1,5},{2,3},{3,2},{4,0},{5,1},{6,7},{7,6},{8,12},{9,13},{10,... | collective-permute-start | bytes 2359304 | tf_op jit(solution)/shard_map/ppermute | solution.py:595
  548.7 15.4 %collective-permute-start.15 = (bf16[1,32,4096]{2,1,0:T(8,128)(2,1)}, bf16[1,32,4096]{2,1,0:T(8,128)(2,1)}, u32[]{:S(2)}, u32[]{:S(2)}) collective-permute-start(bf16[1,32,4096]{2,1,0:T(8,128)(2,1)} %fusion.70), channel_id=1, source_target_pairs={{0,16},{1,17},{2,18},{3,19},{4,20},{5,21},{6,22},{7,23},{8,24},{9,... | collective-permute-start | bytes 786440 | tf_op jit(solution)/shard_map/ppermute | solution.py:548
  586.5 29.5 %collective-permute-start.20 = (bf16[2,4,32,1920]{3,2,1,0:T(8,128)(2,1)}, bf16[2,4,32,1920]{3,2,1,0:T(8,128)(2,1)}, u32[]{:S(2)}, u32[]{:S(2)}) collective-permute-start(bf16[2,4,32,1920]{3,2,1,0:T(8,128)(2,1)} %pad_maximum_fusion.14), channel_id=1, source_target_pairs={{0,1},{1,0},{2,6},{3,7},{4,5},{5,4},{6,2},{7,3},{8,9},{9,8},{10,14... | collective-permute-start | bytes 2949128 | tf_op jit(solution)/shard_map/ppermute | solution.py:592
  587.5 13.6 %collective-permute-start.27 = (f32[104,128]{1,0:T(8,128)S(1)}, f32[104,128]{1,0:T(8,128)S(1)}, u32[]{:S(2)}, u32[]{:S(2)}) collective-permute-start(f32[104,128]{1,0:T(8,128)S(1)} %fusion.117), channel_id=1, source_target_pairs={{0,4},{1,5},{2,6},{3,7},{4,0},{5,1},{6,2},{7,3},{8,12},{9,13},{10,... | collective-permute-start | bytes 159752 | tf_op jit(solution)/shard_map/ppermute | solution.py:548
  606.3 9.8 %collective-permute-start.19 = (bf16[2,32,3072]{2,1,0:T(8,128)(2,1)}, bf16[2,32,3072]{2,1,0:T(8,128)(2,1)S(1)}, u32[]{:S(2)}, u32[]{:S(2)}) collective-permute-start(bf16[2,32,3072]{2,1,0:T(8,128)(2,1)} %get-tuple-element.169), channel_id=1, source_target_pairs={{0,8},{1,9},{2,10},{3,11},{4,12},{5,13},{6,14},{7,15},{8,0},{9,1},... | collective-permute-start | bytes 1179656 | tf_op jit(solution)/shard_map/ppermute | solution.py:548
  (105 other events, 1357.6 us)
Sparse Core Ops, SparseCore 0:
  11.5 88.0 all-gather.2
  103.0 118.3 all-gather.4
